TPU v7x, 512 devices: a whole 4x4x16 slice. The times are simulated.
512 devices in a mesh: lon: 64 (over y, z_lo, core), lat: 8 (over x, z_hi).
Axes of the slice: x: 4, y: 4, z: 16 (z_hi: 2, z_lo: 8; z = z_hi * 8 + z_lo), core: 2. Of those that a mesh axis runs over, the one named last changes fastest.
Arguments:
- tokens: bfloat16 [48, 768, 384], P('lat', 'lon'), may hold values from -6 to 6
- kinds: int32 [48, 768, 2], P('lat', 'lon'), may hold values from 0 to 15
- kind_embed: bfloat16 [16, 192], replicated, may hold values from -3 to 3
- pair_index: int32 [144, 144], replicated, may hold values from 0 to 3311
- bias_table: float32 [8, 6, 3312], P('lat'), may hold values from -4 to 4
- attn_gain: float32 [192], replicated, may hold values from 0.3 to 4
- mlp_gain: float32 [192], replicated, may hold values from 0.3 to 4
- mix_weight: bfloat16 [192, 576], replicated, may hold values from -0.4375 to 0.4375
- out_weight: bfloat16 [192, 192], replicated, may hold values from -0.4375 to 0.4375
- up_weight: bfloat16 [192, 768], replicated, may hold values from -0.4375 to 0.4375
- down_weight: bfloat16 [768, 192], replicated, may hold values from -0.21875 to 0.21875
- cotangent: bfloat16 [48, 768, 384], P('lat', 'lon'), may hold values from -8 to 8
Outputs:
- token_grad: bfloat16 [48, 768, 384], P('lat', 'lon')
- mix_grad: float32 [192, 576], P('lon')
- out_grad: float32 [192, 192], P('lon')
- up_grad: float32 [192, 768], P('lon')
- down_grad: float32 [768, 192], P('lon')
- gain_grad: float32 [2, 192], P(None, 'lon')
- embed_grad: float32 [16, 192], P(None, 'lon')
- bias_grad: float32 [8, 6, 3312], P('lat')
All inputs are finite; a program needn't handle non-finite values.
Results may differ from a plain program's by a relative error of at most 0.012.
The roundings to bfloat16 on the way count: a program that leaves them out, or rounds other values in their place, can miss the bound.
Values may be sent and summed in bfloat16 or wider, within the bound.
A program may use at most 64 MiB of HBM per device.

v0:
```python
import jax
import jax.numpy as jnp
from jax import lax
from jax.sharding import PartitionSpec as P

WIN_LAT = 6
WIN_LON = 12
KINDS = 16
PAIRS = 3312


NORM_EPS = 1e-05
RMS_EPS = 1e-06
GELU_SQRT = 0.7978845608028654
GELU_CUBE = 0.044715


def shifted(array, axis, by):
    size = lax.axis_size(axis)
    return lax.ppermute(array, axis, [(i, (i + by) % size) for i in range(size)])


def layer_norm(values, gain):
    centre_val = jnp.mean(values, axis=-1, keepdims=True)
    centred = values - centre_val
    inverse = lax.rsqrt(jnp.mean(centred * centred, axis=-1, keepdims=True) + NORM_EPS)
    normed = centred * inverse
    return (normed * gain, normed, inverse)


def norm_backward(upstream, normed, inverse, gain):
    scaled = upstream * gain
    result = inverse * (
        scaled
        - jnp.mean(scaled, axis=-1, keepdims=True)
        - normed * jnp.mean(scaled * normed, axis=-1, keepdims=True)
    )
    return (result, jnp.sum(upstream * normed, axis=(0, 1)))


def gelu_parts(inner):
    tangent = jnp.tanh(GELU_SQRT * (inner + GELU_CUBE * inner * inner * inner))
    activated = 0.5 * inner * (1.0 + tangent)
    derivative = 0.5 * (1.0 + tangent) + 0.5 * inner * (1.0 - tangent * tangent) * GELU_SQRT * (
        1.0 + 3.0 * GELU_CUBE * inner * inner
    )
    return (activated, derivative)


def window_backward(stored, upstream, groups, bias_dense, weights):
    mix_weight, out_weight, up_weight, down_weight, attn_gain, mlp_gain = weights
    window_count, win_size, channels = stored.shape
    head_count = bias_dense.shape[1]
    head_size = channels // head_count
    score_scale = head_size ** (-0.5)
    shaped = (window_count, win_size, head_count, head_size)
    residual_in = stored.astype(jnp.float32)
    normed_one, hat_one, inv_one = layer_norm(residual_in, attn_gain)
    first_in = normed_one.astype(jnp.bfloat16)
    mixed = jnp.einsum(
        "nwc,cd->nwd", first_in, mix_weight, preferred_element_type=jnp.float32
    ).astype(jnp.bfloat16)
    queries = mixed[..., :channels].reshape(shaped)
    key_rows = mixed[..., channels : 2 * channels].reshape(shaped)
    value_rows = mixed[..., 2 * channels :].reshape(shaped)
    scores = (
        jnp.einsum("nqhd,nkhd->nhqk", queries, key_rows, preferred_element_type=jnp.float32)
        * score_scale
        + bias_dense
    )
    allowed = groups[:, None, :, None] == groups[:, None, None, :]
    expon = jnp.where(allowed, jnp.exp(scores), 0.0)
    attend = expon / jnp.sum(expon, axis=-1, keepdims=True)
    attend_low = attend.astype(jnp.bfloat16)
    context = (
        jnp.einsum("nhqk,nkhd->nqhd", attend_low, value_rows, preferred_element_type=jnp.float32)
        .astype(jnp.bfloat16)
        .reshape(window_count, win_size, channels)
    )
    residual_mid = residual_in + jnp.einsum(
        "nwc,cd->nwd", context, out_weight, preferred_element_type=jnp.float32
    )
    normed_two, hat_two, inv_two = layer_norm(residual_mid, mlp_gain)
    second_in = normed_two.astype(jnp.bfloat16)
    hidden_pre = jnp.einsum("nwc,cf->nwf", second_in, up_weight, preferred_element_type=jnp.float32)
    hidden_act, hidden_slope = gelu_parts(hidden_pre)
    hidden_low = hidden_act.astype(jnp.bfloat16)
    down_grad = jnp.einsum("nwf,nwc->fc", hidden_low, upstream, preferred_element_type=jnp.float32)
    hidden_grad = (
        jnp.einsum("nwc,fc->nwf", upstream, down_weight, preferred_element_type=jnp.float32)
        * hidden_slope
    ).astype(jnp.bfloat16)
    up_grad = jnp.einsum("nwc,nwf->cf", second_in, hidden_grad, preferred_element_type=jnp.float32)
    second_grad = jnp.einsum(
        "nwf,cf->nwc", hidden_grad, up_weight, preferred_element_type=jnp.float32
    )
    mid_back, mlp_gain_grad = norm_backward(second_grad, hat_two, inv_two, mlp_gain)
    mid_grad = upstream.astype(jnp.float32) + mid_back
    mid_low = mid_grad.astype(jnp.bfloat16)
    out_grad = jnp.einsum("nwc,nwd->cd", context, mid_low, preferred_element_type=jnp.float32)
    context_grad = (
        jnp.einsum("nwd,cd->nwc", mid_low, out_weight, preferred_element_type=jnp.float32)
        .astype(jnp.bfloat16)
        .reshape(shaped)
    )
    attend_grad = jnp.einsum(
        "nqhd,nkhd->nhqk", context_grad, value_rows, preferred_element_type=jnp.float32
    )
    value_grad = jnp.einsum(
        "nhqk,nqhd->nkhd", attend_low, context_grad, preferred_element_type=jnp.float32
    ).astype(jnp.bfloat16)
    score_grad = attend * (attend_grad - jnp.sum(attend * attend_grad, axis=-1, keepdims=True))
    score_low = score_grad.astype(jnp.bfloat16)
    query_grad = (
        jnp.einsum("nhqk,nkhd->nqhd", score_low, key_rows, preferred_element_type=jnp.float32)
        * score_scale
    ).astype(jnp.bfloat16)
    key_grad = (
        jnp.einsum("nhqk,nqhd->nkhd", score_low, queries, preferred_element_type=jnp.float32)
        * score_scale
    ).astype(jnp.bfloat16)
    flat_shape = (window_count, win_size, channels)
    mixed_grad = jnp.concatenate(
        [
            query_grad.reshape(flat_shape),
            key_grad.reshape(flat_shape),
            value_grad.reshape(flat_shape),
        ],
        axis=-1,
    )
    mix_grad = jnp.einsum("nwc,nwd->cd", first_in, mixed_grad, preferred_element_type=jnp.float32)
    first_grad = jnp.einsum(
        "nwd,cd->nwc", mixed_grad, mix_weight, preferred_element_type=jnp.float32
    )
    in_back, attn_gain_grad = norm_backward(first_grad, hat_one, inv_one, attn_gain)
    moved_grad = mid_grad + in_back
    return (
        moved_grad,
        score_grad,
        (mix_grad, out_grad, up_grad, down_grad, attn_gain_grad, mlp_gain_grad),
    )


def grid_windows(grid, channels):
    lat_rows, lon_cols, flat = grid.shape
    levels = flat // channels
    shaped = grid.reshape(
        lat_rows // WIN_LAT, WIN_LAT, lon_cols // WIN_LON, WIN_LON, levels, channels
    )
    return shaped.transpose(0, 2, 1, 3, 4, 5).reshape(-1, WIN_LAT * WIN_LON * levels, channels)


def windows_grid(windows, lat_rows, lon_cols, channels):
    levels = windows.shape[1] // (WIN_LAT * WIN_LON)
    shaped = windows.reshape(
        lat_rows // WIN_LAT, lon_cols // WIN_LON, WIN_LAT, WIN_LON, levels, channels
    )
    return shaped.transpose(0, 2, 1, 3, 4, 5).reshape(lat_rows, lon_cols, levels * channels)


def shards(
    tokens,
    kinds,
    kind_embed,
    pair_index,
    bias_table,
    attn_gain,
    mlp_gain,
    mix_weight,
    out_weight,
    up_weight,
    down_weight,
    cotangent,
):
    lat_dev, lon_dev, flat = tokens.shape
    channels = mix_weight.shape[0]
    levels = flat // channels
    head_count = bias_table.shape[1]
    band_count = lat_dev // WIN_LAT
    column_wins = lon_dev // WIN_LON
    half_lat = WIN_LAT // 2
    half_lon = WIN_LON // 2
    kind_hot = (kinds[..., None] == jnp.arange(KINDS, dtype=jnp.int32)).astype(jnp.bfloat16)
    embedded = jnp.einsum(
        "abln,nc->ablc", kind_hot, kind_embed, preferred_element_type=jnp.float32
    ).reshape(lat_dev, lon_dev, flat)
    stored = (tokens.astype(jnp.float32) + embedded).astype(jnp.bfloat16)
    east_in, east_up = shifted((stored[:, :half_lon], cotangent[:, :half_lon]), "lon", -1)
    wide_in = jnp.concatenate([stored[:, half_lon:], east_in], axis=1)
    wide_up = jnp.concatenate([cotangent[:, half_lon:], east_up], axis=1)
    south_in, south_up = shifted((wide_in[:half_lat], wide_up[:half_lat]), "lat", -1)
    moved_in = jnp.concatenate([wide_in[half_lat:], south_in], axis=0)
    moved_up = jnp.concatenate([wide_up[half_lat:], south_up], axis=0)
    lat_total = lat_dev * lax.axis_size("lat")
    orig_rows = lax.axis_index("lat") * lat_dev + half_lat + jnp.arange(lat_dev, dtype=jnp.int32)
    row_group = (orig_rows >= lat_total).astype(jnp.int32)
    group_grid = jnp.broadcast_to(row_group[:, None, None], (lat_dev, lon_dev, levels))
    groups = grid_windows(group_grid, 1)[..., 0]
    bias_dense = bias_table[:, :, pair_index]
    win_size = pair_index.shape[0]
    bias_windows = bias_dense[:, None].reshape(
        band_count * column_wins, head_count, win_size, win_size
    )
    weights = (mix_weight, out_weight, up_weight, down_weight, attn_gain, mlp_gain)
    moved_grad, score_grad, grads = window_backward(
        grid_windows(moved_in, channels),
        grid_windows(moved_up, channels),
        groups,
        bias_windows,
        weights,
    )
    shifted_grad = windows_grid(moved_grad, lat_dev, lon_dev, channels)
    north_grad = shifted(shifted_grad[lat_dev - half_lat :], "lat", 1)
    lat_fixed = jnp.concatenate([north_grad, shifted_grad[: lat_dev - half_lat]], axis=0)
    west_grad = shifted(lat_fixed[:, lon_dev - half_lon :], "lon", 1)
    grid_grad = jnp.concatenate([west_grad, lat_fixed[:, : lon_dev - half_lon]], axis=1)
    score_sum = jnp.sum(
        score_grad.reshape(band_count, column_wins, head_count, win_size * win_size), axis=1
    )
    pair_rows = score_sum.reshape(band_count * head_count, win_size * win_size).T
    bias_local = jax.ops.segment_sum(
        pair_rows, pair_index.reshape(-1), num_segments=PAIRS
    ).T.reshape(band_count, head_count, PAIRS)
    bias_part = lax.psum(bias_local, "lon")
    embed_local = jnp.einsum(
        "abln,ablc->nc",
        kind_hot.astype(jnp.float32),
        grid_grad.reshape(lat_dev, lon_dev, levels, channels),
        precision=lax.Precision.HIGHEST,
    )
    gain_pair = jnp.stack([grads[4], grads[5]])
    summed = lax.psum((grads[0], grads[1], grads[2], grads[3], gain_pair, embed_local), "lat")
    shares = (
        lax.psum_scatter(summed[0], "lon", scatter_dimension=0, tiled=True),
        lax.psum_scatter(summed[1], "lon", scatter_dimension=0, tiled=True),
        lax.psum_scatter(summed[2], "lon", scatter_dimension=0, tiled=True),
        lax.psum_scatter(summed[3], "lon", scatter_dimension=0, tiled=True),
        lax.psum_scatter(summed[4], "lon", scatter_dimension=1, tiled=True),
        lax.psum_scatter(summed[5], "lon", scatter_dimension=1, tiled=True),
    )
    lat_count = lax.axis_size("lat")
    lon_count = lax.axis_size("lon")
    local_sq = (
        sum((jnp.sum(item * item) for item in shares)) / lat_count
        + jnp.sum(bias_part * bias_part) / lon_count
    )
    total_sq = lax.psum(local_sq, ("lon", "lat"))
    param_total = sum((item.size for item in shares)) * lon_count + bias_part.size * lat_count
    factor = lax.rsqrt(total_sq / param_total + RMS_EPS)
    return (
        grid_grad.astype(jnp.bfloat16),
        shares[0] * factor,
        shares[1] * factor,
        shares[2] * factor,
        shares[3] * factor,
        shares[4] * factor,
        shares[5] * factor,
        bias_part * factor,
    )


def solution(mesh):
    return jax.shard_map(
        shards,
        mesh=mesh,
        in_specs=(
            P("lat", "lon", None),
            P("lat", "lon", None),
            P(),
            P(),
            P("lat", None, None),
            P(),
            P(),
            P(),
            P(),
            P(),
            P(),
            P("lat", "lon", None),
        ),
        out_specs=(
            P("lat", "lon", None),
            P("lon", None),
            P("lon", None),
            P("lon", None),
            P("lon", None),
            P(None, "lon"),
            P(None, "lon"),
            P("lat", None, None),
        ),
        check_vma=False,
    )
```

profile of v0, /device:TPU:1, one launch (start us, length us, event | category | flops | bytes accessed | tf_op | source)
XLA Modules:
  0.0 1521.7 jit_solution(110191556064372523)
XLA Ops:
  9.5 8.8 collective-permute-start.2
  19.2 9.7 collective-permute-start
  30.7 38.7 %gather_fusion = f32[20736,6]{1,0:T(8,128)} fusion(f32[6,3312]{0,1:T(8,128)S(1)} %bitcast.83, s32[21504]{0:T(1024)S(1)} %pad_clamp_fusion), kind=kCustom, calls=%fused_computation | custom fusion | bytes 1078272 | tf_op jit(solution)/shard_map/gather | solution.py:199
  69.4 11.7 copy.56
  83.7 10.1 collective-permute-start.3
  93.9 6.1 collective-permute-start.1
  103.1 4.3 collective-permute-done.1
  113.2 216.6 %fusion = f32[16,192]{1,0:T(8,128)S(1)} fusion(f32[768,192]{1,0:T(8,128)S(1)} %fusion.17), kind=kCustom, calls=%all-reduce-scatter | all-reduce-scatter fusion | flops 196609 | bytes 604160
  342.8 17.7 %collective-permute-start.15 = (f32[16,192]{1,0:T(8,128)S(1)}, f32[16,192]{1,0:T(8,128)S(1)}, u32[]{:S(2)}, u32[]{:S(2)}) collective-permute-start(f32[16,192]{1,0:T(8,128)S(1)} %fusion), channel_id=1, source_target_pairs={{0,80},{8,88},{16,96},{24,104},{32,112},{40,120},{48,128},{56,136}... | collective-permute-start | bytes 36872
  362.3 6.2 copy.64
  368.5 113.6 %scatter_custom_fusion = f32[3312,6]{1,0:T(8,128)} fusion(s32[20736]{0:T(1024)} %reshape.486, f32[20736,6]{1,0:T(8,128)} %copy.64, f32[]{:T(128)} %constant.19.clone.1), kind=kCustom, calls=%fused_computation.23 | custom fusion | flops 124416 | bytes 80000 | tf_op jit(solution)/shard_map/scatter-add | solution.py:221
  482.2 3.4 collective-permute-start.16
  485.6 2.7 collective-permute-start.17
  488.3 4.8 collective-permute-start.18
  497.2 3.1 collective-permute-start.6
  503.8 3.2 collective-permute-start.9
  507.0 4.6 collective-permute-start.4
  513.6 9.5 collective-permute-done.4
  523.2 3.6 collective-permute-start.5
  530.0 420.4 %all-reduce.7 = (f32[2,192]{1,0:T(2,128)S(1)}, f32[16,192]{0,1:T(8,128)S(1)}) all-reduce(f32[2,192]{1,0:T(2,128)S(1)} %pad_maximum_fusion.4, f32[16,192]{0,1:T(8,128)S(1)} %convolution_bitcast_fusion), channel_id=6, replica_groups=mesh['lon'=64,'lat'=8] {'lon'}, use_global_device_ids=true, to_apply=%region_25.26.clone | all-reduce | flops 3456 | bytes 27648
  950.5 364.3 %all-reduce.12.cloned.1.call-done = (f32[192,576]{1,0:T(8,128)}, f32[192,192]{1,0:T(8,128)}, f32[192,768]{1,0:T(8,128)}, f32[1,6,3312]{1,2,0:T(8,128)}) async-done(((f32[192,576]{1,0:T(8,128)}, f32[192,192]{1,0:T(8,128)}, f32[192,768]{1,0:T(8,128)}, f32[1,6,3312]{1,2,0:T(8,128)}), (f32[192,576]{1,0:T(8,128)}, f32[192,192]{1,0:T(8,128)}, f32[192,768]{1,0:T(8,128)}, ...) | async-done | bytes 1259152
  1317.3 65.4 %all-reduce.9 = (f32[3,576]{1,0:T(4,128)S(1)}, f32[3,192]{1,0:T(4,128)S(1)}, f32[3,768]{1,0:T(4,128)S(1)}, f32[12,192]{1,0:T(8,128)S(1)}, f32[2,3]{1,0:T(2,128)S(1)}, /*index=5*/f32[16,3]{0,1:T(4,128)S(1)}) all-reduce(f32[3,576]{1,0:T(4,128)S(1)} %constant_dynamic-slice_fusion.5, ...), channel_id=1, replica_groups=mesh['lon'=64,'lat'=8] {'lat'}, use_global_device_ids=true, to_apply=%region_10.11 | all-reduce | flops 6966 | bytes 55728 | tf_op jit(solution)/shard_map/psum | solution.py:232
  1394.0 112.6 %psum.63 = f32[]{:T(128)} all-reduce(f32[]{:T(128)S(6)} %add.148), channel_id=1, replica_groups=mesh['lon'=64,'lat'=8] {'lon','lat'}, use_global_device_ids=true, to_apply=%region_33.34 | all-reduce | flops 1 | bytes 8 | tf_op jit(solution)/shard_map/psum | solution.py:247
  1512.2 2.6 copy.65
  (190 shorter events, 56.2 us)
Async XLA Ops:
  7.2 1307.6 %all-reduce.12.cloned.1.call-start = ((), (), s32[]{:S(2)}) async-start(), calls=%async_computation | async-start | bytes 5947392
  9.5 74.2 %collective-permute-start.2 = (bf16[6,6,384]{2,1,0:T(8,128)(2,1)S(1)}, bf16[6,6,384]{2,1,0:T(8,128)(2,1)S(1)}, u32[]{:S(2)}, u32[]{:S(2)}) collective-permute-start(bf16[6,6,384]{2,1,0:T(8,128)(2,1)S(1)} %get-tuple-element.60), channel_id=1, source_target_pairs={{0,504},{8,0},{16,8},{24,16},{32,24},{40,32},{48,40},{56,48},{64,5... | collective-permute-start | bytes 82952 | tf_op jit(solution)/shard_map/ppermute | solution.py:20
  19.2 74.7 %collective-permute-start = (bf16[6,6,384]{2,1,0:T(8,128)(2,1)S(1)}, bf16[6,6,384]{2,1,0:T(8,128)(2,1)S(1)}, u32[]{:S(2)}, u32[]{:S(2)}) collective-permute-start(bf16[6,6,384]{2,1,0:T(8,128)(2,1)S(1)} %get-tuple-element.64), channel_id=1, source_target_pairs={{0,504},{8,0},{16,8},{24,16},{32,24},{40,32},{48,40},{56,48},{64,5... | collective-permute-start | bytes 82952 | tf_op jit(solution)/shard_map/ppermute | solution.py:20
  83.7 16.3 %collective-permute-start.3 = (bf16[3,12,384]{2,1,0:T(8,128)(2,1)S(1)}, bf16[3,12,384]{2,1,0:T(8,128)(2,1)S(1)}, u32[]{:S(2)}, u32[]{:S(2)}) collective-permute-start(bf16[3,12,384]{2,1,0:T(8,128)(2,1)S(1)} %get-tuple-element.58), channel_id=1, source_target_pairs={{0,7},{1,0},{2,1},{3,2},{4,3},{5,4},{6,5},{7,6},{8,15},{9,8},{10,9... | collective-permute-start | bytes 82952 | tf_op jit(solution)/shard_map/ppermute | solution.py:20
  93.9 13.4 collective-permute-start.1
  111.8 224.7 %copy-start.13 = (bf16[6,32,144]{2,1,0:T(8,128)(2,1)}, bf16[6,32,144]{2,1,0:T(8,128)(2,1)S(1)}, u32[]{:S(2)}) copy-start(bf16[6,32,144]{2,1,0:T(8,128)(2,1)S(1)} %fusion.7) | copy-start | bytes 165892
  329.8 12.9 collective-permute-start.10
  331.1 151.1 %collective-permute-start.11 = (f32[16,192]{1,0:T(8,128)S(1)}, f32[16,192]{1,0:T(8,128)S(1)}, u32[]{:S(2)}, u32[]{:S(2)}) collective-permute-start(f32[16,192]{1,0:T(8,128)S(1)} %fusion), channel_id=1, source_target_pairs={{0,48},{8,56},{16,64},{24,72},{32,80},{40,88},{48,96},{56,104},{64... | collective-permute-start | bytes 36872
  332.4 153.2 %collective-permute-start.12 = (f32[16,192]{1,0:T(8,128)S(1)}, f32[16,192]{1,0:T(8,128)S(1)}, u32[]{:S(2)}, u32[]{:S(2)}) collective-permute-start(f32[16,192]{1,0:T(8,128)S(1)} %fusion), channel_id=1, source_target_pairs={{0,56},{8,64},{16,72},{24,80},{32,88},{40,96},{48,104},{56,112},{6... | collective-permute-start | bytes 36872
  333.7 154.6 %collective-permute-start.13 = (f32[16,192]{1,0:T(8,128)S(1)}, f32[16,192]{1,0:T(8,128)S(1)}, u32[]{:S(2)}, u32[]{:S(2)}) collective-permute-start(f32[16,192]{1,0:T(8,128)S(1)} %fusion), channel_id=1, source_target_pairs={{0,64},{8,72},{16,80},{24,88},{32,96},{40,104},{48,112},{56,120},{... | collective-permute-start | bytes 36872
  338.0 3.5 collective-permute-start.21
  341.5 151.7 %collective-permute-start.14 = (f32[16,192]{1,0:T(8,128)S(1)}, f32[16,192]{1,0:T(8,128)S(1)}, u32[]{:S(2)}, u32[]{:S(2)}) collective-permute-start(f32[16,192]{1,0:T(8,128)S(1)} %fusion), channel_id=1, source_target_pairs={{0,72},{8,80},{16,88},{24,96},{32,104},{40,112},{48,120},{56,128},... | collective-permute-start | bytes 36872
  342.8 152.4 %collective-permute-start.15 = (f32[16,192]{1,0:T(8,128)S(1)}, f32[16,192]{1,0:T(8,128)S(1)}, u32[]{:S(2)}, u32[]{:S(2)}) collective-permute-start(f32[16,192]{1,0:T(8,128)S(1)} %fusion), channel_id=1, source_target_pairs={{0,80},{8,88},{16,96},{24,104},{32,112},{40,120},{48,128},{56,136}... | collective-permute-start | bytes 36872
  482.2 15.0 collective-permute-start.16
  485.6 14.7 collective-permute-start.17
  488.3 13.8 collective-permute-start.18
  493.2 10.6 collective-permute-start.19
  495.2 11.8 collective-permute-start.20
  497.2 14.6 collective-permute-start.6
  500.3 11.5 collective-permute-start.7
  502.1 9.6 collective-permute-start.8
  503.8 7.9 collective-permute-start.9
  507.0 16.2 %collective-permute-start.4 = (f32[3,12,384]{2,1,0:T(8,128)S(1)}, f32[3,12,384]{2,1,0:T(8,128)S(1)}, u32[]{:S(2)}, u32[]{:S(2)}) collective-permute-start(f32[3,12,384]{2,1,0:T(8,128)S(1)} %slice.63), channel_id=1, source_target_pairs={{0,1},{1,2},{2,3},{3,4},{4,5},{5,6},{6,7},{7,0},{8,9},{9,10},{10,1... | collective-permute-start | bytes 165896 | tf_op jit(solution)/shard_map/ppermute | solution.py:20
  523.2 6.2 collective-permute-start.5
  (26 other events, 1429.0 us)
Sparse Core Ops, SparseCore 0:
  482.3 832.4 all-reduce.11
where the time goes:
time: 1520 us
  blocking collectives  815 us (54%)
  waiting for transfers between devices  381 us (25%)
  other arithmetic  128 us (8%)
  starting transfers between devices  93 us (6%)
  local copies, waits for them, and re-layouts  71.5 us (5%)
  between operations  21.6 us (1%)
    unnamed x2, blocking collectives  637 us
    unnamed x18, waiting for transfers between devices  364 us
    scatter-add x1, other arithmetic, shards(): jax.ops.segment_sum(pair_rows, pair_index.reshape(-1), num_segments=PAIRS)  114 us
    psum x1, blocking collectives, shards(): total_sq = lax.psum(local_sq, ('lon', 'lat'))  113 us
    psum x1, blocking collectives, shards(): lax.psum((grads[0], grads[1], grads[2], grads[3], gain_pair, embed_local)...  65.4 us
    gather x2, local copies, waits for them, and re-layouts, shards(): bias_dense = bias_table[:, :, pair_index]  50.4 us
    unnamed x17, starting transfers between devices  50.1 us
    ppermute x6, starting transfers between devices, shifted(): lax.ppermute(array, axis, [(i, (i + by) % size) for i in range(size)])  42.9 us
  transfers between devices with their start and end apart: 23, of which 4 were waited for; matrix products, arithmetic and copies ran while one was open for 12% of the time, Pallas kernels for 0%

commit v1 on v0

v1 whole, which is shorter than its diff:
```python
import jax
import jax.numpy as jnp
import numpy as np
from jax import lax
from jax.experimental import pallas as pl
from jax.experimental.pallas import tpu as pltpu
from jax.sharding import PartitionSpec as P

F32 = jnp.float32
BF16 = jnp.bfloat16
MESH = pl.DeviceIdType.MESH

C = 192
HEADS = 6
HEAD = 32
FF = 768
WIN_LAT = 6
WIN_LON = 12
KINDS = 16
PAIRS = 3312
TOK = 144
CELLS = 18
PART = 36
LANES = 128
HI = 26
COLS = 2304
TILES = 18
NORM_EPS = 1e-05
RMS_EPS = 1e-06
GELU_SQRT = 0.7978845608028654
GELU_CUBE = 0.044715
LON, LAT = 64, 8
ZLO = 8
VMEM_LIMIT = 56 * 1024 * 1024


def place():
    lon, lat = lax.axis_index("lon"), lax.axis_index("lat")
    return lat // 2, lon // 16, (lat % 2) * ZLO + (lon // 2) % ZLO, lon % 2


def at(x, y, z, core):
    return {"lon": y * 16 + (z % ZLO) * 2 + core, "lat": x * 2 + z // ZLO}


def dot(a, b):
    return lax.dot_general(a, b, (((1,), (0,)), ((), ())), preferred_element_type=F32)


def dot_nt(a, b):
    return lax.dot_general(a, b, (((1,), (1,)), ((), ())), preferred_element_type=F32)


def dot_tn(a, b):
    return lax.dot_general(a, b, (((0,), (0,)), ((), ())), preferred_element_type=F32)


def two_terms(v):
    high = v.astype(BF16)
    return high, (v - high.astype(F32)).astype(BF16)


def halo_kernel(tok_ref, kind_ref, embed_ref, cot_ref, out_ref, tok_s, kind_s, flat_s, send, recv, send_sem, recv_sem):
    lon, lat = lax.axis_index("lon"), lax.axis_index("lat")
    barrier = pltpu.get_barrier_semaphore()
    for dr, dc in ((1, 0), (0, 1), (1, 1)):
        for sign in (1, -1):
            pl.semaphore_signal(
                barrier,
                inc=1,
                device_id={"lon": (lon + sign * dc + LON) % LON, "lat": (lat + sign * dr + LAT) % LAT},
                device_id_type=MESH,
            )
    embed = embed_ref[...].astype(F32)
    blank = jnp.zeros((KINDS, C), F32)
    wide = jnp.concatenate(
        [jnp.concatenate([embed, blank], axis=1), jnp.concatenate([blank, embed], axis=1)], axis=0
    ).astype(BF16)
    for row in range(WIN_LAT):
        tok = tok_ref[row].astype(F32)
        cot = cot_ref[row].astype(F32)
        kind = kind_ref[row]
        for half in range(2):
            quarter = 2 * (row // 3) + half
            start = 6 * (row % 3)
            cells = slice(6 * half, 6 * half + 6)
            tok_s[quarter, start : start + 6, :] = tok[cells]
            flat_s[quarter, CELLS + start : CELLS + start + 6, :] = cot[cells]
            kind_s[quarter, start : start + 6, :] = kind[cells]
    column = lax.broadcasted_iota(jnp.int32, (24, 32), 1)
    lane = lax.broadcasted_iota(jnp.int32, (24, LANES), 1)
    sub = lax.broadcasted_iota(jnp.int32, (24, LANES), 0)
    for quarter in range(4):
        kinds = kind_s[quarter]
        first, second = kinds[:, 0:1], kinds[:, 1:2]
        hot = jnp.where((column == first) | (column == second + KINDS), 1.0, 0.0).astype(BF16)
        stored = tok_s[quarter] + dot(hot, wide)
        flat_s[quarter, 0:CELLS, :] = stored[0:CELLS]
        valid = sub < CELLS
        row = jnp.where(valid & (lane == sub), first.astype(F32), 0.0) + jnp.where(
            valid & (lane == sub + CELLS), second.astype(F32), 0.0
        )
        flat_s[quarter, 36:48, :] = jnp.zeros((12, 2 * C), F32)
        flat_s[quarter, 36:37, 0:LANES] = jnp.sum(row, axis=0, keepdims=True)
        send[quarter] = flat_s[quarter].astype(BF16)
    pl.semaphore_wait(barrier, 6)
    copies = []
    for slot in (3, 2, 1):
        dr, dc = slot // 2, slot % 2
        copy = pltpu.make_async_remote_copy(
            src_ref=send.at[3 - slot],
            dst_ref=recv.at[slot],
            send_sem=send_sem.at[slot],
            recv_sem=recv_sem.at[slot],
            device_id={"lon": (lon - dc + LON) % LON, "lat": (lat - dr + LAT) % LAT},
            device_id_type=MESH,
        )
        copy.start()
        copies.append(copy)
    out_ref[0] = send[3]
    for slot, copy in zip((3, 2, 1), copies):
        copy.wait_recv()
        out_ref[slot] = recv[slot]
    for copy in copies:
        copy.wait_send()


def halo(tokens, kinds, kind_embed, cotangent):
    return pl.pallas_call(
        halo_kernel,
        out_shape=jax.ShapeDtypeStruct((4, 48, 2 * C), BF16),
        in_specs=[pl.BlockSpec(memory_space=pltpu.VMEM)] * 4,
        out_specs=pl.BlockSpec(memory_space=pltpu.VMEM),
        scratch_shapes=[
            pltpu.VMEM((4, 24, 2 * C), F32),
            pltpu.VMEM((4, 24, 2), jnp.int32),
            pltpu.VMEM((4, 48, 2 * C), F32),
            pltpu.VMEM((4, 48, 2 * C), BF16),
            pltpu.VMEM((4, 48, 2 * C), BF16),
            pltpu.SemaphoreType.DMA((4,)),
            pltpu.SemaphoreType.DMA((4,)),
        ],
        compiler_params=pltpu.CompilerParams(collective_id=0, has_side_effects=True, vmem_limit_bytes=VMEM_LIMIT),
        name="halo_in",
    )(tokens, kinds, kind_embed, cotangent)


def layer_norm(values, gain):
    centred = values - jnp.mean(values, axis=-1, keepdims=True)
    inverse = lax.rsqrt(jnp.mean(centred * centred, axis=-1, keepdims=True) + NORM_EPS)
    normed = centred * inverse
    return normed * gain, normed, inverse


def norm_backward(upstream, normed, inverse, gain):
    scaled = upstream * gain
    return inverse * (
        scaled
        - jnp.mean(scaled, axis=-1, keepdims=True)
        - normed * jnp.mean(scaled * normed, axis=-1, keepdims=True)
    )


def dense_rows(ref, values, base):
    ref[base : base + TOK, :] = values[:, 0:LANES]
    tail = values[:, LANES:TOK]
    tail = jnp.concatenate([tail, jnp.zeros((TOK, LANES - 16), tail.dtype)], axis=1)
    row = tail[0:16]
    for group in range(1, 8):
        row = row + pltpu.roll(tail[16 * group : 16 * group + 16], 16 * group, 1)
    ref[base + TOK : base + TOK + 16, :] = row
    ref[base + TOK + 16 : base + TOK + 32, :] = tail[LANES:TOK]


DENSE = TOK + 32


def window_kernel(
    block_ref, index_ref, table_ref, gain1_ref, gain2_ref, mix_ref, out_ref, up_ref, down_ref, order_ref, spread_ref,
    grads_ref, bias_out_ref, back_ref,
    flat_s, x_s, g_s, hot_s, high_s, low_s, table_s, dense_s, bias_s, acc_s, grad_s, rows_s, ge_s, moved_s,
):
    lane36 = lax.broadcasted_iota(jnp.int32, (PART, LANES), 1)
    sub36 = lax.broadcasted_iota(jnp.int32, (PART, LANES), 0)
    for slot in range(4):
        flat_s[slot] = block_ref[slot].astype(F32)
        toks = flat_s[slot, 0:CELLS, :]
        cots = flat_s[slot, CELLS:PART, :]
        base = PART * slot
        x_s[base : base + CELLS, :] = toks[:, 0:C]
        x_s[base + CELLS : base + PART, :] = toks[:, C : 2 * C]
        g_s[base : base + CELLS, :] = cots[:, 0:C]
        g_s[base + CELLS : base + PART, :] = cots[:, C : 2 * C]
        kind_row = flat_s[slot, PART : PART + 1, 0:LANES]
        kind_col = jnp.sum(jnp.where(lane36 == sub36, kind_row, 0.0), axis=1, keepdims=True)
        hot_s[base : base + PART, :] = jnp.where(lane36.astype(F32) == kind_col, 1.0, 0.0)

    order = order_ref[...]
    index = index_ref[...]
    high = (index // LANES).astype(F32).astype(BF16)
    low = (index % LANES).astype(F32).astype(BF16)
    dense_rows(high_s, dot_nt(dot(order, high).astype(BF16), order), 0)
    dense_rows(low_s, dot_nt(dot(order, low).astype(BF16), order), 0)
    table_s[...] = jnp.zeros((HEADS * 32, LANES), F32)
    for row in range(HI):
        width = min(LANES, PAIRS - row * LANES)
        for head in range(HEADS):
            table_s[32 * head + row : 32 * head + row + 1, 0:width] = table_ref[
                0, head : head + 1, row * LANES : row * LANES + width
            ]

    def gather(step, carry):
        start = pl.multiple_of(step * 16, 16)
        lows = low_s[pl.ds(start, 16), :].astype(jnp.int32)
        highs = high_s[pl.ds(start, 16), :]
        totals = [jnp.zeros((16, LANES), F32) for _ in range(HEADS)]
        for row in range(HI):
            chosen = highs == float(row)
            for head in range(HEADS):
                line = jnp.broadcast_to(table_s[32 * head + row : 32 * head + row + 1, :], (16, LANES))
                found = jnp.take_along_axis(line, lows, axis=1, mode="promise_in_bounds")
                totals[head] = jnp.where(chosen, found, totals[head])
        for head in range(HEADS):
            dense_s[pl.ds(pl.multiple_of(head * DENSE + start, 16), 16), :] = totals[head]
        return carry

    lax.fori_loop(0, DENSE // 16, gather, 0)
    for head in range(HEADS):
        base = head * DENSE
        bias_s[head * TOK : head * TOK + TOK, 0:LANES] = dense_s[base : base + TOK, :]
        row = dense_s[base + TOK : base + TOK + 16, :]
        for group in range(8):
            turned = row if group == 0 else pltpu.roll(row, LANES - 16 * group, 1)
            bias_s[head * TOK + 16 * group : head * TOK + 16 * group + 16, LANES:TOK] = turned[:, 0:16]
        bias_s[head * TOK + LANES : head * TOK + TOK, LANES:TOK] = dense_s[base + TOK + 16 : base + TOK + 32, 0:16]

    gain1, gain2 = gain1_ref[...], gain2_ref[...]
    mix_weight, out_weight = mix_ref[...], out_ref[...]
    up_weight, down_weight = up_ref[...], down_ref[...]
    residual = x_s[...]
    upstream = g_s[...]
    upstream_low = upstream.astype(BF16)
    first, hat1, inv1 = layer_norm(residual, gain1)
    first_in = first.astype(BF16)
    mixed = dot(first_in, mix_weight)
    queries = mixed[:, 0:C].astype(BF16).astype(F32)
    keys = mixed[:, C : 2 * C].astype(BF16)
    values = mixed[:, 2 * C : 3 * C].astype(BF16)
    channel = lax.broadcasted_iota(jnp.int32, (TOK, C), 1)
    of_head = [(channel >= HEAD * n) & (channel < HEAD * n + HEAD) for n in range(HEADS)]
    q_stack = jnp.concatenate([jnp.where(m, queries, 0.0) for m in of_head], axis=0).astype(BF16)
    scores = dot_nt(q_stack, keys) * (HEAD**-0.5) + bias_s[...]
    last = lax.axis_index("lat") == LAT - 1
    group_q = ((lax.broadcasted_iota(jnp.int32, (HEADS * TOK, TOK), 0) // 72) % 2).astype(F32)
    group_k = (lax.broadcasted_iota(jnp.int32, (HEADS * TOK, TOK), 1) >= 72).astype(F32)
    allowed = jnp.abs(group_q - group_k) * jnp.where(last, 1.0, 0.0) < 0.5
    expon = jnp.where(allowed, jnp.exp(scores), 0.0)
    attend = expon / jnp.sum(expon, axis=-1, keepdims=True)
    attend_low = attend.astype(BF16)
    context = jnp.zeros((TOK, C), F32)
    for n in range(HEADS):
        context += jnp.where(of_head[n], dot(attend_low[n * TOK : (n + 1) * TOK], values), 0.0)
    context = context.astype(BF16)
    mid = residual + dot(context, out_weight)
    second, hat2, inv2 = layer_norm(mid, gain2)
    second_in = second.astype(BF16)
    inner = dot(second_in, up_weight)
    tangent = jnp.tanh(GELU_SQRT * (inner + GELU_CUBE * inner * inner * inner))
    hidden_low = (0.5 * inner * (1.0 + tangent)).astype(BF16)
    slope = 0.5 * (1.0 + tangent) + 0.5 * inner * (1.0 - tangent * tangent) * GELU_SQRT * (
        1.0 + 3.0 * GELU_CUBE * inner * inner
    )
    hidden_grad = (dot_nt(upstream_low, down_weight) * slope).astype(BF16)
    second_grad = dot_nt(hidden_grad, up_weight)
    mid_grad = upstream + norm_backward(second_grad, hat2, inv2, gain2)
    mid_low = mid_grad.astype(BF16)
    context_grad = dot_nt(mid_low, out_weight).astype(BF16).astype(F32)
    c_stack = jnp.concatenate([jnp.where(m, context_grad, 0.0) for m in of_head], axis=0).astype(BF16)
    attend_grad = dot_nt(c_stack, values)
    value_grad = dot_tn(attend_low, c_stack).astype(BF16)
    score_grad = attend * (attend_grad - jnp.sum(attend * attend_grad, axis=-1, keepdims=True))
    score_low = score_grad.astype(BF16)
    query_grad = jnp.zeros((TOK, C), F32)
    for n in range(HEADS):
        query_grad += jnp.where(of_head[n], dot(score_low[n * TOK : (n + 1) * TOK], keys), 0.0)
        dense_rows(dense_s, score_grad[n * TOK : (n + 1) * TOK], n * DENSE)
    query_grad = (query_grad * (HEAD**-0.5)).astype(BF16)
    key_grad = (dot_tn(score_low, q_stack) * (HEAD**-0.5)).astype(BF16)
    first_grad = (
        dot_nt(query_grad, mix_weight[:, 0:C])
        + dot_nt(key_grad, mix_weight[:, C : 2 * C])
        + dot_nt(value_grad, mix_weight[:, 2 * C : 3 * C])
    )
    moved = mid_grad + norm_backward(first_grad, hat1, inv1, gain1)

    moved_s[...] = moved
    for slot in range(4):
        base = PART * slot
        flat_s[slot, 0:CELLS, 0:C] = moved_s[base : base + CELLS, :]
        flat_s[slot, 0:CELLS, C : 2 * C] = moved_s[base + CELLS : base + PART, :]
        back_ref[slot] = flat_s[slot, 0:32, :].astype(BF16)

    grad_s[:, 0:C] = dot_tn(first_in, query_grad)
    grad_s[:, C : 2 * C] = dot_tn(first_in, key_grad)
    grad_s[:, 2 * C : 3 * C] = dot_tn(first_in, value_grad)
    grad_s[:, 3 * C : 4 * C] = dot_tn(context, mid_low)
    grad_s[:, 4 * C : 8 * C] = dot_tn(second_in, hidden_grad)
    spread = dot(hidden_low, spread_ref[...]).astype(BF16)
    for part in range(4):
        grad_s[:, (8 + part) * C : (9 + part) * C] = dot_tn(spread[:, part * C : (part + 1) * C], upstream_low)
    lane = lax.broadcasted_iota(jnp.int32, (TOK, LANES), 1)
    small = jnp.zeros((C, LANES), F32)
    for left, right in (
        (moved, hot_s[...]),
        (first_grad * hat1, jnp.where(lane == KINDS, 1.0, 0.0)),
        (second_grad * hat2, jnp.where(lane == KINDS + 1, 1.0, 0.0)),
    ):
        for term in two_terms(left):
            small += dot_tn(term, right.astype(BF16))
    ge_s[...] = small
    for tile in range(TILES):
        rows_s[tile // 9, pl.ds(tile % 9, C, stride=9), :] = grad_s[:, tile * LANES : (tile + 1) * LANES]
    extra = jnp.zeros((32, LANES), F32)
    for k in range(6):
        line = ge_s[pl.ds(k, 32, stride=6), :]
        extra += pltpu.roll(line, 18 * k, 1) if k else line
    sub64 = lax.broadcasted_iota(jnp.int32, (64, LANES), 0)
    for half in range(2):
        for block in range(32):
            got = rows_s[half, 54 * block : 54 * block + 64, :]
            tail = jnp.where(sub64 == 54, extra[block : block + 1], 0.0) if half == 0 else jnp.zeros_like(got)
            got = jnp.where(sub64 < 54, got, tail).astype(BF16)
            for part in range(4):
                grads_ref[half, block // 8, part, block % 8] = got[16 * part : 16 * part + 16]

    acc_s[...] = jnp.zeros((208, LANES), F32)
    row32 = lax.broadcasted_iota(jnp.int32, (32, 2 * LANES), 0).astype(F32)
    row128 = lax.broadcasted_iota(jnp.int32, (LANES, 2 * LANES), 0).astype(F32)

    def pair(ref, row):
        return jnp.concatenate([ref[pl.ds(row, 1), :], ref[pl.ds(row + DENSE // 2, 1), :]], axis=1)

    def scatter(step, carry):
        chosen = row32 == pair(high_s, step)
        hot = jnp.where(row128 == pair(low_s, step), 1.0, 0.0).astype(BF16)
        spread_out = [jnp.where(chosen, pair(dense_s, n * DENSE + step), 0.0) for n in range(HEADS)]
        acc_s[0 : 32 * HEADS, :] += dot_nt(jnp.concatenate(spread_out, axis=0).astype(BF16), hot)
        return carry

    lax.fori_loop(0, DENSE // 2, scatter, 0)
    sub16 = lax.broadcasted_iota(jnp.int32, (16, LANES), 0)
    for block in range(16):
        bias_out_ref[block // 8, block % 8] = jnp.where(sub16 < 12, acc_s[12 * block : 12 * block + 16, :], 0.0)


def window(block, pair_index, bias_table, gain1, gain2, mix_weight, out_weight, up_weight, down_weight):
    token = np.arange(TOK)
    slot, level, cell = token // PART, (token % PART) // CELLS, token % CELLS
    row, col = 3 * (slot // 2) + cell // 6, 6 * (slot % 2) + cell % 6
    order = np.zeros((TOK, TOK), np.float32)
    order[token, (row * WIN_LON + col) * 2 + level] = 1.0
    column = np.arange(FF)
    spread = np.zeros((FF, FF), np.float32)
    spread[4 * (column % C) + column // C, column] = 1.0
    vmem = pl.BlockSpec(memory_space=pltpu.VMEM)
    return pl.pallas_call(
        window_kernel,
        out_shape=(
            jax.ShapeDtypeStruct((2, 4, 4, ZLO, 16, LANES), BF16),
            jax.ShapeDtypeStruct((2, ZLO, 16, LANES), F32),
            jax.ShapeDtypeStruct((4, 32, 2 * C), BF16),
        ),
        in_specs=[vmem] * 11,
        out_specs=(vmem, vmem, vmem),
        scratch_shapes=[
            pltpu.VMEM((4, 48, 2 * C), F32),
            pltpu.VMEM((TOK, C), F32),
            pltpu.VMEM((TOK, C), F32),
            pltpu.VMEM((TOK, LANES), F32),
            pltpu.VMEM((DENSE, LANES), F32),
            pltpu.VMEM((DENSE, LANES), F32),
            pltpu.VMEM((HEADS * 32, LANES), F32),
            pltpu.VMEM((HEADS * DENSE, LANES), F32),
            pltpu.VMEM((HEADS * TOK, TOK), F32),
            pltpu.VMEM((208, LANES), F32),
            pltpu.VMEM((C, COLS), F32),
            pltpu.VMEM((2, 9 * C + 16, LANES), F32),
            pltpu.VMEM((C, LANES), F32),
            pltpu.VMEM((TOK, C), F32),
        ],
        compiler_params=pltpu.CompilerParams(vmem_limit_bytes=VMEM_LIMIT),
        name="window",
    )(
        block, pair_index, bias_table, gain1, gain2, mix_weight, out_weight, up_weight, down_weight,
        jnp.asarray(order, BF16), jnp.asarray(spread, BF16),
    )


def reduce_kernel(
    grads_ref, bias_ref, back_ref,
    dense_out, bias_out, back_out, total_out,
    core_r, plane_s, plane_r, line_s, line_r, share, bcore_r, bline_s, bline_r, brow_r, ball, back_r, squares_z, squares_y,
    core_ss, core_rs, plane_ss, plane_rs, line_ss, line_rs, share_ss, share_rs, bcore_ss, bcore_rs, bline_ss, bline_rs,
    brow_ss, brow_rs, ball_ss, ball_rs, bpair_ss, bpair_rs, back_ss, back_rs, sz_ss, sz_rs, sy_ss, sy_rs,
):
    lon, lat = lax.axis_index("lon"), lax.axis_index("lat")
    x, y, z, core = place()
    z_lo, z_hi = z % ZLO, z // ZLO
    other = 1 - core

    def remote(src, dst, send_sem, recv_sem, target):
        return pltpu.make_async_remote_copy(
            src_ref=src, dst_ref=dst, send_sem=send_sem, recv_sem=recv_sem, device_id=target, device_id_type=MESH
        )

    barrier = pltpu.get_barrier_semaphore()
    peers = [at(x, y, z, other)]
    peers += [at((x + d // 4) % 4, (y + d % 4) % 4, z, core) for d in range(1, 16)]
    peers += [at(x, y, (z + d) % 16, core) for d in range(1, 16)]
    peers += [at((x + d) % 4, y, z, other) for d in range(1, 4)]
    for dr, dc in ((1, 0), (0, 1), (1, 1)):
        for sign in (1, -1):
            peers.append({"lon": (lon + sign * dc + LON) % LON, "lat": (lat + sign * dr + LAT) % LAT})
    for peer in peers:
        pl.semaphore_signal(barrier, inc=1, device_id=peer, device_id_type=MESH)
    pl.semaphore_wait(barrier, len(peers))

    sends = []

    bcore = remote(bias_ref.at[other], bcore_r, bcore_ss, bcore_rs, at(x, y, z, other))
    bcore.start()
    sends.append(bcore)
    core_copies = []
    for j in range(4):
        to = (y + 1 + j) % 4
        copy = remote(grads_ref.at[other, to], core_r.at[to], core_ss.at[j], core_rs.at[j], at(x, y, z, other))
        copy.start()
        core_copies.append(copy)
    sends += core_copies
    back_copies = []
    for slot in (3, 2, 1):
        dr, dc = slot // 2, slot % 2
        copy = remote(
            back_ref.at[slot],
            back_r.at[3 - slot],
            back_ss.at[slot],
            back_rs.at[slot],
            {"lon": (lon + dc) % LON, "lat": (lat + dr) % LAT},
        )
        copy.start()
        back_copies.append((slot, copy))
    sends += [copy for _, copy in back_copies]

    bcore.wait_recv()
    for part in range(ZLO):
        bline_s[part] = bias_ref[core, part] + bcore_r[part]
    bline_r[z_lo] = bline_s[z_lo]
    bline_copies = []
    for d in range(1, ZLO):
        to = (z_lo + d) % ZLO
        copy = remote(
            bline_s.at[to], bline_r.at[z_lo], bline_ss.at[d], bline_rs.at[d], at(x, y, z_hi * ZLO + to, core)
        )
        copy.start()
        bline_copies.append(copy)
    sends += bline_copies

    plane_copies = {}
    for j in range(4):
        to_y = (y + 1 + j) % 4
        core_copies[j].wait_recv()
        for part in range(4):
            plane_s[to_y, part] = (grads_ref[core, to_y, part].astype(F32) + core_r[to_y, part].astype(F32)).astype(BF16)
        for i in range(4):
            dx, dy = (i + 1) % 4, (j + 1) % 4
            d = dx * 4 + dy
            to_x = (x + dx) % 4
            if d == 0:
                plane_r[x * 4 + y] = plane_s[y, x]
                continue
            copy = remote(
                plane_s.at[to_y, to_x],
                plane_r.at[x * 4 + y],
                plane_ss.at[d],
                plane_rs.at[d],
                at(to_x, to_y, z, core),
            )
            copy.start()
            plane_copies[d] = copy
    sends += list(plane_copies.values())

    for copy in bline_copies:
        copy.wait_recv()
    part_sum = bline_r[0]
    for part in range(1, ZLO):
        part_sum = part_sum + bline_r[part]
    brow_r[y] = part_sum
    brow_copies = []
    for d in range(1, 4):
        to = (y + d) % 4
        copy = remote(brow_r.at[y], brow_r.at[y], brow_ss.at[d], brow_rs.at[d], at(x, to, z, core))
        copy.start()
        brow_copies.append(copy)
    sends += brow_copies

    for copy in plane_copies.values():
        copy.wait_recv()
    for part in range(ZLO):
        block = plane_r[0, part].astype(F32)
        for source in range(1, 16):
            block = block + plane_r[source, part].astype(F32)
        line_s[part] = block.astype(BF16)
    line_r[z] = line_s[z_lo]
    line_copies = []
    for d in range(1, 16):
        to = (z + d) % 16
        copy = remote(line_s.at[to % ZLO], line_r.at[z], line_ss.at[d], line_rs.at[d], at(x, y, to, core))
        copy.start()
        line_copies.append(copy)
    sends += line_copies

    for copy in brow_copies:
        copy.wait_recv()
    bias_part = (brow_r[0] + brow_r[1]) + (brow_r[2] + brow_r[3])
    ball[core, z_lo] = bias_part
    ball_copies = []
    for d in range(1, ZLO):
        to = (z_lo + d) % ZLO
        copy = remote(
            ball.at[core, z_lo], ball.at[core, z_lo], ball_ss.at[d], ball_rs.at[d], at(x, y, z_hi * ZLO + to, core)
        )
        copy.start()
        ball_copies.append(copy)
    sends += ball_copies

    for copy in line_copies:
        copy.wait_recv()
    piece = line_r[0].astype(F32)
    for source in range(1, 16):
        piece = piece + line_r[source].astype(F32)
    square = 0.5 * jnp.sum(piece * piece) + 0.25 * jnp.sum(bias_part * bias_part)
    mine = core * 4 + x
    share[mine, 0:16, :] = piece
    share[mine, 16:24, :] = jnp.full((8, LANES), square, F32)
    share_copies = []
    for dx, dcore in ((1, 0), (2, 0), (3, 0), (0, 1), (1, 1), (2, 1), (3, 1)):
        d = dcore * 4 + dx
        copy = remote(
            share.at[mine],
            share.at[mine],
            share_ss.at[d],
            share_rs.at[d],
            at((x + dx) % 4, y, z, core + dcore * (1 - 2 * core)),
        )
        copy.start()
        share_copies.append(copy)
    sends += share_copies

    for copy in ball_copies:
        copy.wait_recv()
    bpair = remote(ball.at[core], ball.at[core], bpair_ss, bpair_rs, at(x, y, z, other))
    bpair.start()
    sends.append(bpair)

    for copy in share_copies:
        copy.wait_recv()
    square = share[0, 16:17, :]
    for source in range(1, 8):
        square = square + share[source, 16:17, :]
    squares_z[z] = square
    sz_copies = []
    for d in range(1, 16):
        to = (z + d) % 16
        copy = remote(squares_z.at[z], squares_z.at[z], sz_ss.at[d], sz_rs.at[d], at(x, y, to, core))
        copy.start()
        sz_copies.append(copy)
    sends += sz_copies
    for source in range(8):
        dense_out[source] = share[source, 0:16, :]
    back_out[3] = back_ref[0]
    for slot, copy in back_copies:
        copy.wait_recv()
        back_out[3 - slot] = back_r[3 - slot]
    for copy in sz_copies:
        copy.wait_recv()
    square = squares_z[0]
    for source in range(1, 16):
        square = square + squares_z[source]
    squares_y[y] = square
    sy_copies = []
    for d in range(1, 4):
        copy = remote(squares_y.at[y], squares_y.at[y], sy_ss.at[d], sy_rs.at[d], at(x, (y + d) % 4, z, core))
        copy.start()
        sy_copies.append(copy)
    sends += sy_copies
    bpair.wait_recv()
    bias_out[...] = ball[...]
    for copy in sy_copies:
        copy.wait_recv()
    total_out[...] = (squares_y[0] + squares_y[1]) + (squares_y[2] + squares_y[3])
    for copy in sends:
        copy.wait_send()


def reduce(grads, bias, back):
    vmem = pl.BlockSpec(memory_space=pltpu.VMEM)
    dma = pltpu.SemaphoreType.DMA
    return pl.pallas_call(
        reduce_kernel,
        out_shape=(
            jax.ShapeDtypeStruct((8, 16, LANES), F32),
            jax.ShapeDtypeStruct((2, ZLO, 16, LANES), F32),
            jax.ShapeDtypeStruct((4, 32, 2 * C), BF16),
            jax.ShapeDtypeStruct((1, LANES), F32),
        ),
        in_specs=[vmem] * 3,
        out_specs=(vmem,) * 4,
        scratch_shapes=[
            pltpu.VMEM((4, 4, ZLO, 16, LANES), BF16),
            pltpu.VMEM((4, 4, ZLO, 16, LANES), BF16),
            pltpu.VMEM((16, ZLO, 16, LANES), BF16),
            pltpu.VMEM((ZLO, 16, LANES), BF16),
            pltpu.VMEM((16, 16, LANES), BF16),
            pltpu.VMEM((8, 24, LANES), F32),
            pltpu.VMEM((ZLO, 16, LANES), F32),
            pltpu.VMEM((ZLO, 16, LANES), F32),
            pltpu.VMEM((ZLO, 16, LANES), F32),
            pltpu.VMEM((4, 16, LANES), F32),
            pltpu.VMEM((2, ZLO, 16, LANES), F32),
            pltpu.VMEM((4, 32, 2 * C), BF16),
            pltpu.VMEM((16, 1, LANES), F32),
            pltpu.VMEM((4, 1, LANES), F32),
            dma((4,)), dma((4,)),
            dma((16,)), dma((16,)),
            dma((16,)), dma((16,)),
            dma((8,)), dma((8,)),
            dma, dma,
            dma((8,)), dma((8,)),
            dma((4,)), dma((4,)),
            dma((8,)), dma((8,)),
            dma, dma,
            dma((4,)), dma((4,)),
            dma((16,)), dma((16,)),
            dma((4,)), dma((4,)),
        ],
        compiler_params=pltpu.CompilerParams(collective_id=1, has_side_effects=True, vmem_limit_bytes=VMEM_LIMIT),
        name="sum_over_devices",
    )(grads, bias, back)


def output_kernel(
    dense_ref, bias_ref, back_ref, total_ref,
    token_ref, mix_ref, out_ref, up_ref, down_ref, gain_ref, embed_ref, table_ref,
    dense_s, flat_s, bias_s, back_s, token_s,
):
    count = C * COLS + (KINDS + 2) * C + LAT * HEADS * PAIRS
    factor = lax.rsqrt(total_ref[...] / count + RMS_EPS)
    odd = lax.axis_index("lon") % 2 == 1
    for part in range(8):
        dense_s[part // 4, 16 * (part % 4) : 16 * (part % 4) + 16, :] = dense_ref[part] * factor
    for tile in range(TILES):
        half, t = tile // 9, tile % 9
        even_rows = dense_s[half, pl.ds(t, 3, stride=9), :]
        odd_rows = dense_s[half, pl.ds(27 + t, 3, stride=9), :]
        flat_s[0:3, tile * LANES : (tile + 1) * LANES] = jnp.where(odd, odd_rows, even_rows)
    flat = flat_s[0:3, :]
    mix_ref[...] = flat[:, 0 : 3 * C]
    out_ref[...] = flat[:, 3 * C : 4 * C]
    up_ref[...] = flat[:, 4 * C : 8 * C]
    for row in range(3):
        for part in range(4):
            down_ref[4 * row + part : 4 * row + part + 1, :] = flat[row : row + 1, (8 + part) * C : (9 + part) * C]
    extra = dense_s[0, 54:55, :]
    lane = lax.broadcasted_iota(jnp.int32, (24, LANES), 1)
    sub = lax.broadcasted_iota(jnp.int32, (24, LANES), 0)
    small = jnp.zeros((24, LANES), F32)
    for row in range(3):
        start = jnp.where(odd, 18 * (3 + row), 18 * row)
        column = jnp.sum(jnp.where(lane == sub + start, extra, 0.0), axis=1, keepdims=True)
        small = small + jnp.where(lane == row, column, 0.0)
    embed_ref[...] = small[0:KINDS, 0:3]
    gain_ref[...] = small[KINDS : KINDS + 2, 0:3]
    for block in range(16):
        bias_s[12 * block : 12 * block + 12, :] = bias_ref[block // 8, block % 8, 0:12, :] * factor
    for row in range(HI):
        width = min(LANES, PAIRS - row * LANES)
        table_ref[0, :, row * LANES : row * LANES + width] = bias_s[pl.ds(row, HEADS, stride=32), :][:, 0:width]
    for quarter in range(4):
        back_s[quarter] = back_ref[quarter].astype(F32)
        for i in range(3):
            row, half = 3 * (quarter // 2) + i, quarter % 2
            token_s[row, 6 * half : 6 * half + 6, :] = back_s[quarter, 6 * i : 6 * i + 6, :]
    for row in range(WIN_LAT):
        token_ref[row] = token_s[row, 0:WIN_LON, :].astype(BF16)


def outputs(dense, bias, back, total):
    vmem = pl.BlockSpec(memory_space=pltpu.VMEM)
    return pl.pallas_call(
        output_kernel,
        out_shape=(
            jax.ShapeDtypeStruct((WIN_LAT, WIN_LON, 2 * C), BF16),
            jax.ShapeDtypeStruct((3, 3 * C), F32),
            jax.ShapeDtypeStruct((3, C), F32),
            jax.ShapeDtypeStruct((3, FF), F32),
            jax.ShapeDtypeStruct((12, C), F32),
            jax.ShapeDtypeStruct((2, 3), F32),
            jax.ShapeDtypeStruct((KINDS, 3), F32),
            jax.ShapeDtypeStruct((1, HEADS, PAIRS), F32),
        ),
        in_specs=[vmem] * 4,
        out_specs=(vmem,) * 8,
        scratch_shapes=[
            pltpu.VMEM((2, 64, LANES), F32),
            pltpu.VMEM((8, COLS), F32),
            pltpu.VMEM((HEADS * 32, LANES), F32),
            pltpu.VMEM((4, 32, 2 * C), F32),
            pltpu.VMEM((WIN_LAT, 16, 2 * C), F32),
        ],
        compiler_params=pltpu.CompilerParams(vmem_limit_bytes=VMEM_LIMIT),
        name="scaled_outputs",
    )(dense, bias, back, total)


def shards(
    tokens, kinds, kind_embed, pair_index, bias_table, attn_gain, mlp_gain,
    mix_weight, out_weight, up_weight, down_weight, cotangent,
):
    block = halo(tokens, kinds, kind_embed, cotangent)
    grads, bias, back = window(
        block, pair_index, bias_table, attn_gain.reshape(1, C), mlp_gain.reshape(1, C),
        mix_weight, out_weight, up_weight, down_weight,
    )
    return outputs(*reduce(grads, bias, back))


def solution(mesh):
    return jax.shard_map(
        shards,
        mesh=mesh,
        in_specs=(
            P("lat", "lon", None),
            P("lat", "lon", None),
            P(),
            P(),
            P("lat", None, None),
            P(),
            P(),
            P(),
            P(),
            P(),
            P(),
            P("lat", "lon", None),
        ),
        out_specs=(
            P("lat", "lon", None),
            P("lon", None),
            P("lon", None),
            P("lon", None),
            P("lon", None),
            P(None, "lon"),
            P(None, "lon"),
            P("lat", None, None),
        ),
        check_vma=False,
    )
```

time: 1520 us -> 117 us (0.08)
  blocking collectives: 815 us -> 0 us
  waiting for transfers between devices: 381 us -> 0 us
  other arithmetic: 128 us -> 0 us
  Pallas kernels: 0 us -> 108 us
  starting transfers between devices: 93 us -> 0 us
  local copies, waits for them, and re-layouts: 71.5 us -> 7.83 us
  between operations: 21.6 us -> 0.65 us
    unnamed x2 -> x0, blocking collectives: 637 us -> none
    unnamed x18 -> x0, waiting for transfers between devices: 364 us -> none
    psum x2 -> x0, blocking collectives: 178 us -> none  [the longest x1 113 us: shards(): total_sq = lax.psum(local_sq, ('lon', 'lat'))]
    scatter-add x1 -> x0, other arithmetic: 114 us -> none  [shards(): jax.ops.segment_sum(pair_rows, pair_index.reshape(-1), num_segments=PAIRS)]
    pallas_call x0 -> x4, Pallas kernels: none -> 108 us  [the longest x1 52.3 us: reduce(): pl.pallas_call(reduce_kernel, out_shape=(jax.ShapeDtypeStruct((8, 16, LAN...]
    gather x2 -> x0, local copies, waits for them, and re-layouts: 50.4 us -> none  [shards(): bias_dense = bias_table[:, :, pair_index]]
    unnamed x17 -> x0, starting transfers between devices: 50.1 us -> none
    ppermute x6 -> x0, starting transfers between devices: 42.9 us -> none  [shifted(): lax.ppermute(array, axis, [(i, (i + by) % size) for i in range(size)])]
  transfers between devices with their start and end apart: 23 -> 0, of which waited for: 4 -> 0; matrix products, arithmetic and copies ran while one was open for 12% -> 0% of each run, Pallas kernels for 0% -> 0%
where the time goes in v1:
time: 117 us
  Pallas kernels  108 us (92%)
  local copies, waits for them, and re-layouts  7.83 us (7%)
    pallas_call x1, Pallas kernels, reduce(): pl.pallas_call(reduce_kernel, out_shape=(jax.ShapeDtypeStruct((8, 16, LAN...  52.3 us
    pallas_call x1, Pallas kernels, window(): pl.pallas_call(window_kernel, out_shape=(jax.ShapeDtypeStruct((2, 4, 4, Z...  28.4 us
    pallas_call x1, Pallas kernels, halo(): pl.pallas_call(halo_kernel, out_shape=jax.ShapeDtypeStruct((4, 48, 2 * C)...  25.8 us
    unnamed x3, local copies, waits for them, and re-layouts  4.87 us
    pallas_call x2, local copies, waits for them, and re-layouts, outputs(): pl.pallas_call(output_kernel, out_shape=(jax.ShapeDtypeStruct((WIN_LAT, W...  2.96 us

profile of v1, /device:TPU:1, one launch (start us, length us, event | category | flops | bytes accessed | tf_op | source)
XLA Modules:
  0.0 116.8 jit_solution(10488785115132205271)
XLA Ops:
  0.6 1.4 %copy.22.kind_ref = s32[6,12,2]{2,1,0:T(8,128)} copy(s32[6,12,2]{1,2,0:T(2,128)} %param.15) | data formatting | bytes 1152 | tf_op args[1]
  2.1 25.8 %halo_in.1.block_ref = bf16[4,48,384]{2,1,0:T(8,128)(2,1)} custom-call(bf16[6,12,384]{2,1,0:T(8,128)(2,1)} %tok_ref.1, s32[6,12,2]{2,1,0:T(8,128)} %copy.22.kind_ref, bf16[16,192]{1,0:T(8,128)(2,1)} %embed_ref.1, bf16[6,12,384]{2,1,0:T(8,128)(2,1)} %cot_ref.1), custom_call_target="tpu_custom_call" | custom-call | tf_op jit(solution)/shard_map/halo_in/pallas_call | solution.py:129
  27.9 1.5 %copy.23.table_ref = f32[1,6,3312]{2,1,0:T(8,128)} copy(f32[1,6,3312]{2,0,1:T(1,128)} %param.18) | data formatting | bytes 158976 | tf_op args[4]
  29.4 1.9 %copy.24.down_ref = bf16[768,192]{1,0:T(8,128)(2,1)} copy(bf16[768,192]{0,1:T(8,128)(2,1)} %param.24) | data formatting | bytes 589824 | tf_op args[10]
  31.3 28.4 %window.1 = (bf16[2,4,4,8,16,128]{5,4,3,2,1,0:T(8,128)(2,1)}, f32[2,8,16,128]{3,2,1,0:T(8,128)}, bf16[4,32,384]{2,1,0:T(8,128)(2,1)}) custom-call(bf16[4,48,384]{2,1,0:T(8,128)(2,1)} %halo_in.1.block_ref, s32[144,144]{1,0:T(8,128)} %index_ref.1, f32[1,6,3312]{2,1,0:T(8,128)} %copy.23.table_ref, f32[1,192]{1,0:T(1,128)} %bitcast.2, f32[1,192]{1,0:T(1,128)} %bitcast.3, ...), custom_call_target="tpu_custom_call" | custom-call | tf_op jit(solution)/shard_map/window/pallas_call | solution.py:366
  59.7 52.3 %sum_over_devices.1 = (f32[8,16,128]{2,1,0:T(8,128)}, f32[2,8,16,128]{3,2,1,0:T(8,128)}, bf16[4,32,384]{2,1,0:T(8,128)(2,1)}, f32[1,128]{1,0:T(1,128)}) custom-call(bf16[2,4,4,8,16,128]{5,4,3,2,1,0:T(8,128)(2,1)} %get-tuple-element.15.grads_ref, f32[2,8,16,128]{3,2,1,0:T(8,128)} %get-tuple-element.16.bias_ref, bf16[4,32,384]{2,1,0:T(8,128)(2,1)} %get-tuple-element.17.back_ref), custom_call_target="tpu_custom_call" | custom-call | tf_op jit(solution)/shard_map/sum_over_devices/pallas_call | solution.py:608
  112.0 1.8 %scaled_outputs.1 = (bf16[6,12,384]{2,1,0:T(8,128)(2,1)}, f32[3,576]{1,0:T(4,128)}, f32[3,192]{1,0:T(4,128)}, f32[3,768]{1,0:T(4,128)}, f32[12,192]{1,0:T(8,128)...) custom-call(f32[8,16,128]{2,1,0:T(8,128)} %get-tuple-element.18.dense_ref, ...), custom_call_target="tpu_custom_call" | custom-call | tf_op jit(solution)/shard_map/scaled_outputs/pallas_call | solution.py:699
  113.8 1.3 %copy.25 = f32[16,3]{0,1:T(4,128)} copy(f32[16,3]{1,0:T(8,128)} %get-tuple-element.28) | data formatting | bytes 384 | tf_op jit(solution)/shard_map/scaled_outputs/pallas_call | solution.py:699
  115.2 1.6 %copy.26 = f32[1,6,3312]{2,0,1:T(1,128)} copy(f32[1,6,3312]{2,1,0:T(8,128)} %get-tuple-element.29) | data formatting | bytes 158976 | tf_op jit(solution)/shard_map/scaled_outputs/pallas_call | solution.py:699

commit v2 on v1

--- a/solution.py
+++ b/solution.py
@@ -60,7 +60,27 @@
     return high, (v - high.astype(F32)).astype(BF16)
 
 
-def halo_kernel(tok_ref, kind_ref, embed_ref, cot_ref, out_ref, tok_s, kind_s, flat_s, send, recv, send_sem, recv_sem):
+def dense_rows(ref, values, base):
+    ref[base : base + TOK, :] = values[:, 0:LANES]
+    tail = values[:, LANES:TOK]
+    tail = jnp.concatenate([tail, jnp.zeros((TOK, LANES - 16), tail.dtype)], axis=1)
+    row = tail[0:16]
+    for group in range(1, 8):
+        row = row + pltpu.roll(tail[16 * group : 16 * group + 16], 16 * group, 1)
+    ref[base + TOK : base + TOK + 16, :] = row
+    ref[base + TOK + 16 : base + TOK + 32, :] = tail[LANES:TOK]
+
+
+DENSE = TOK + 32
+FLAT = 3 * PART
+SENT = FLAT + 4
+
+
+def halo_kernel(
+    tok_ref, kind_ref, embed_ref, cot_ref, index_ref, table_ref, order_ref,
+    out_ref, bias_ref, high_ref, low_ref,
+    tok_s, kind_s, flat_s, pack_s, send, recv, table_s, dense_s, send_sem, recv_sem,
+):
     lon, lat = lax.axis_index("lon"), lax.axis_index("lat")
     barrier = pltpu.get_barrier_semaphore()
     for dr, dc in ((1, 0), (0, 1), (1, 1)):
@@ -76,33 +96,32 @@
     wide = jnp.concatenate(
         [jnp.concatenate([embed, blank], axis=1), jnp.concatenate([blank, embed], axis=1)], axis=0
     ).astype(BF16)
+    kind_s[...] = jnp.zeros((4, 8, LANES), F32)
     for row in range(WIN_LAT):
         tok = tok_ref[row].astype(F32)
         cot = cot_ref[row].astype(F32)
-        kind = kind_ref[row]
+        kind = kind_ref[row].astype(F32)
         for half in range(2):
             quarter = 2 * (row // 3) + half
             start = 6 * (row % 3)
             cells = slice(6 * half, 6 * half + 6)
             tok_s[quarter, start : start + 6, :] = tok[cells]
             flat_s[quarter, CELLS + start : CELLS + start + 6, :] = cot[cells]
-            kind_s[quarter, start : start + 6, :] = kind[cells]
-    column = lax.broadcasted_iota(jnp.int32, (24, 32), 1)
-    lane = lax.broadcasted_iota(jnp.int32, (24, LANES), 1)
-    sub = lax.broadcasted_iota(jnp.int32, (24, LANES), 0)
+            kind_s[quarter, 0:2, start : start + 6] = kind[:, cells]
+    sub = lax.broadcasted_iota(jnp.int32, (2 * KINDS, LANES), 0).astype(F32)
     for quarter in range(4):
         kinds = kind_s[quarter]
-        first, second = kinds[:, 0:1], kinds[:, 1:2]
-        hot = jnp.where((column == first) | (column == second + KINDS), 1.0, 0.0).astype(BF16)
-        stored = tok_s[quarter] + dot(hot, wide)
+        hot = (sub == kinds[0:1]) | (sub - KINDS == kinds[1:2])
+        hot = jnp.where(hot, 1.0, 0.0).astype(BF16)[:, 0:24]
+        stored = tok_s[quarter] + dot_tn(hot, wide)
         flat_s[quarter, 0:CELLS, :] = stored[0:CELLS]
-        valid = sub < CELLS
-        row = jnp.where(valid & (lane == sub), first.astype(F32), 0.0) + jnp.where(
-            valid & (lane == sub + CELLS), second.astype(F32), 0.0
-        )
-        flat_s[quarter, 36:48, :] = jnp.zeros((12, 2 * C), F32)
-        flat_s[quarter, 36:37, 0:LANES] = jnp.sum(row, axis=0, keepdims=True)
-        send[quarter] = flat_s[quarter].astype(BF16)
+        for tile in range(3):
+            pack_s[quarter, PART * tile : PART * tile + PART, :] = flat_s[
+                quarter, 0:PART, tile * LANES : (tile + 1) * LANES
+            ]
+        pack_s[quarter, FLAT:SENT, :] = jnp.zeros((4, LANES), F32)
+        pack_s[quarter, FLAT : FLAT + 1, :] = kinds[0:1] + pltpu.roll(kinds, CELLS, 1)[1:2]
+        send[quarter] = pack_s[quarter].astype(BF16)
     pl.semaphore_wait(barrier, 6)
     copies = []
     for slot in (3, 2, 1):
@@ -117,102 +136,25 @@
         )
         copy.start()
         copies.append(copy)
-    out_ref[0] = send[3]
-    for slot, copy in zip((3, 2, 1), copies):
-        copy.wait_recv()
-        out_ref[slot] = recv[slot]
-    for copy in copies:
-        copy.wait_send()
-
-
-def halo(tokens, kinds, kind_embed, cotangent):
-    return pl.pallas_call(
-        halo_kernel,
-        out_shape=jax.ShapeDtypeStruct((4, 48, 2 * C), BF16),
-        in_specs=[pl.BlockSpec(memory_space=pltpu.VMEM)] * 4,
-        out_specs=pl.BlockSpec(memory_space=pltpu.VMEM),
-        scratch_shapes=[
-            pltpu.VMEM((4, 24, 2 * C), F32),
-            pltpu.VMEM((4, 24, 2), jnp.int32),
-            pltpu.VMEM((4, 48, 2 * C), F32),
-            pltpu.VMEM((4, 48, 2 * C), BF16),
-            pltpu.VMEM((4, 48, 2 * C), BF16),
-            pltpu.SemaphoreType.DMA((4,)),
-            pltpu.SemaphoreType.DMA((4,)),
-        ],
-        compiler_params=pltpu.CompilerParams(collective_id=0, has_side_effects=True, vmem_limit_bytes=VMEM_LIMIT),
-        name="halo_in",
-    )(tokens, kinds, kind_embed, cotangent)
-
-
-def layer_norm(values, gain):
-    centred = values - jnp.mean(values, axis=-1, keepdims=True)
-    inverse = lax.rsqrt(jnp.mean(centred * centred, axis=-1, keepdims=True) + NORM_EPS)
-    normed = centred * inverse
-    return normed * gain, normed, inverse
-
-
-def norm_backward(upstream, normed, inverse, gain):
-    scaled = upstream * gain
-    return inverse * (
-        scaled
-        - jnp.mean(scaled, axis=-1, keepdims=True)
-        - normed * jnp.mean(scaled * normed, axis=-1, keepdims=True)
-    )
-
-
-def dense_rows(ref, values, base):
-    ref[base : base + TOK, :] = values[:, 0:LANES]
-    tail = values[:, LANES:TOK]
-    tail = jnp.concatenate([tail, jnp.zeros((TOK, LANES - 16), tail.dtype)], axis=1)
-    row = tail[0:16]
-    for group in range(1, 8):
-        row = row + pltpu.roll(tail[16 * group : 16 * group + 16], 16 * group, 1)
-    ref[base + TOK : base + TOK + 16, :] = row
-    ref[base + TOK + 16 : base + TOK + 32, :] = tail[LANES:TOK]
-
-
-DENSE = TOK + 32
-
-
-def window_kernel(
-    block_ref, index_ref, table_ref, gain1_ref, gain2_ref, mix_ref, out_ref, up_ref, down_ref, order_ref, spread_ref,
-    grads_ref, bias_out_ref, back_ref,
-    flat_s, x_s, g_s, hot_s, high_s, low_s, table_s, dense_s, bias_s, acc_s, grad_s, rows_s, ge_s, moved_s,
-):
-    lane36 = lax.broadcasted_iota(jnp.int32, (PART, LANES), 1)
-    sub36 = lax.broadcasted_iota(jnp.int32, (PART, LANES), 0)
-    for slot in range(4):
-        flat_s[slot] = block_ref[slot].astype(F32)
-        toks = flat_s[slot, 0:CELLS, :]
-        cots = flat_s[slot, CELLS:PART, :]
-        base = PART * slot
-        x_s[base : base + CELLS, :] = toks[:, 0:C]
-        x_s[base + CELLS : base + PART, :] = toks[:, C : 2 * C]
-        g_s[base : base + CELLS, :] = cots[:, 0:C]
-        g_s[base + CELLS : base + PART, :] = cots[:, C : 2 * C]
-        kind_row = flat_s[slot, PART : PART + 1, 0:LANES]
-        kind_col = jnp.sum(jnp.where(lane36 == sub36, kind_row, 0.0), axis=1, keepdims=True)
-        hot_s[base : base + PART, :] = jnp.where(lane36.astype(F32) == kind_col, 1.0, 0.0)
 
     order = order_ref[...]
     index = index_ref[...]
     high = (index // LANES).astype(F32).astype(BF16)
     low = (index % LANES).astype(F32).astype(BF16)
-    dense_rows(high_s, dot_nt(dot(order, high).astype(BF16), order), 0)
-    dense_rows(low_s, dot_nt(dot(order, low).astype(BF16), order), 0)
+    dense_rows(high_ref, dot_nt(dot(order, high).astype(BF16), order), 0)
+    dense_rows(low_ref, dot_nt(dot(order, low).astype(BF16), order), 0)
     table_s[...] = jnp.zeros((HEADS * 32, LANES), F32)
     for row in range(HI):
         width = min(LANES, PAIRS - row * LANES)
         for head in range(HEADS):
             table_s[32 * head + row : 32 * head + row + 1, 0:width] = table_ref[
-                0, head : head + 1, row * LANES : row * LANES + width
+                head, :, row * LANES : row * LANES + width
             ]
 
     def gather(step, carry):
         start = pl.multiple_of(step * 16, 16)
-        lows = low_s[pl.ds(start, 16), :].astype(jnp.int32)
-        highs = high_s[pl.ds(start, 16), :]
+        lows = low_ref[pl.ds(start, 16), :].astype(jnp.int32)
+        highs = high_ref[pl.ds(start, 16), :]
         totals = [jnp.zeros((16, LANES), F32) for _ in range(HEADS)]
         for row in range(HI):
             chosen = highs == float(row)
@@ -227,12 +169,93 @@
     lax.fori_loop(0, DENSE // 16, gather, 0)
     for head in range(HEADS):
         base = head * DENSE
-        bias_s[head * TOK : head * TOK + TOK, 0:LANES] = dense_s[base : base + TOK, :]
+        bias_ref[head * TOK : head * TOK + TOK, 0:LANES] = dense_s[base : base + TOK, :]
         row = dense_s[base + TOK : base + TOK + 16, :]
         for group in range(8):
             turned = row if group == 0 else pltpu.roll(row, LANES - 16 * group, 1)
-            bias_s[head * TOK + 16 * group : head * TOK + 16 * group + 16, LANES:TOK] = turned[:, 0:16]
-        bias_s[head * TOK + LANES : head * TOK + TOK, LANES:TOK] = dense_s[base + TOK + 16 : base + TOK + 32, 0:16]
+            bias_ref[head * TOK + 16 * group : head * TOK + 16 * group + 16, LANES:TOK] = turned[:, 0:16]
+        bias_ref[head * TOK + LANES : head * TOK + TOK, LANES:TOK] = dense_s[base + TOK + 16 : base + TOK + 32, 0:16]
+
+    out_ref[0] = send[3]
+    for slot, copy in zip((3, 2, 1), copies):
+        copy.wait_recv()
+        out_ref[slot] = recv[slot]
+    for copy in copies:
+        copy.wait_send()
+
+
+def halo(tokens, kinds, kind_embed, cotangent, pair_index, bias_table):
+    token = np.arange(TOK)
+    slot, level, cell = token // PART, (token % PART) // CELLS, token % CELLS
+    row, col = 3 * (slot // 2) + cell // 6, 6 * (slot % 2) + cell % 6
+    order = np.zeros((TOK, TOK), np.float32)
+    order[token, (row * WIN_LON + col) * 2 + level] = 1.0
+    vmem = pl.BlockSpec(memory_space=pltpu.VMEM)
+    return pl.pallas_call(
+        halo_kernel,
+        out_shape=(
+            jax.ShapeDtypeStruct((4, SENT, LANES), BF16),
+            jax.ShapeDtypeStruct((HEADS * TOK, TOK), F32),
+            jax.ShapeDtypeStruct((DENSE, LANES), F32),
+            jax.ShapeDtypeStruct((DENSE, LANES), F32),
+        ),
+        in_specs=[vmem] * 7,
+        out_specs=(vmem,) * 4,
+        scratch_shapes=[
+            pltpu.VMEM((4, 24, 2 * C), F32),
+            pltpu.VMEM((4, 8, LANES), F32),
+            pltpu.VMEM((4, 40, 2 * C), F32),
+            pltpu.VMEM((4, SENT, LANES), F32),
+            pltpu.VMEM((4, SENT, LANES), BF16),
+            pltpu.VMEM((4, SENT, LANES), BF16),
+            pltpu.VMEM((HEADS * 32, LANES), F32),
+            pltpu.VMEM((HEADS * DENSE, LANES), F32),
+            pltpu.SemaphoreType.DMA((4,)),
+            pltpu.SemaphoreType.DMA((4,)),
+        ],
+        compiler_params=pltpu.CompilerParams(collective_id=0, has_side_effects=True, vmem_limit_bytes=VMEM_LIMIT),
+        name="halo_in",
+    )(tokens, kinds, kind_embed, cotangent, pair_index, bias_table, jnp.asarray(order, BF16))
+
+
+def layer_norm(values, gain):
+    centred = values - jnp.mean(values, axis=-1, keepdims=True)
+    inverse = lax.rsqrt(jnp.mean(centred * centred, axis=-1, keepdims=True) + NORM_EPS)
+    normed = centred * inverse
+    return normed * gain, normed, inverse
+
+
+def norm_backward(upstream, normed, inverse, gain):
+    scaled = upstream * gain
+    return inverse * (
+        scaled
+        - jnp.mean(scaled, axis=-1, keepdims=True)
+        - normed * jnp.mean(scaled * normed, axis=-1, keepdims=True)
+    )
+
+
+def window_kernel(
+    block_ref, bias_ref, gain1_ref, gain2_ref, mix_ref, out_ref, up_ref, down_ref,
+    first_in_ref, query_grad_ref, key_grad_ref, value_grad_ref, context_ref, mid_low_ref, second_in_ref, hidden_grad_ref,
+    hidden_low_ref, upstream_ref, score_ref, extra_ref, back_ref,
+    flat_s, x_s, g_s, hot_s, ge_s, moved_s, pack_s,
+):
+    lane36 = lax.broadcasted_iota(jnp.int32, (PART, LANES), 1)
+    sub36 = lax.broadcasted_iota(jnp.int32, (PART, LANES), 0)
+    for slot in range(4):
+        pack_s[slot] = block_ref[slot].astype(F32)
+        for tile in range(3):
+            flat_s[slot, 0:PART, tile * LANES : (tile + 1) * LANES] = pack_s[slot, PART * tile : PART * tile + PART, :]
+        toks = flat_s[slot, 0:CELLS, :]
+        cots = flat_s[slot, CELLS:PART, :]
+        base = PART * slot
+        x_s[base : base + CELLS, :] = toks[:, 0:C]
+        x_s[base + CELLS : base + PART, :] = toks[:, C : 2 * C]
+        g_s[base : base + CELLS, :] = cots[:, 0:C]
+        g_s[base + CELLS : base + PART, :] = cots[:, C : 2 * C]
+        kind_row = pack_s[slot, FLAT : FLAT + 1, :]
+        kind_col = jnp.sum(jnp.where(lane36 == sub36, kind_row, 0.0), axis=1, keepdims=True)
+        hot_s[base : base + PART, :] = jnp.where(lane36.astype(F32) == kind_col, 1.0, 0.0)
 
     gain1, gain2 = gain1_ref[...], gain2_ref[...]
     mix_weight, out_weight = mix_ref[...], out_ref[...]
@@ -249,7 +272,7 @@
     channel = lax.broadcasted_iota(jnp.int32, (TOK, C), 1)
     of_head = [(channel >= HEAD * n) & (channel < HEAD * n + HEAD) for n in range(HEADS)]
     q_stack = jnp.concatenate([jnp.where(m, queries, 0.0) for m in of_head], axis=0).astype(BF16)
-    scores = dot_nt(q_stack, keys) * (HEAD**-0.5) + bias_s[...]
+    scores = dot_nt(q_stack, keys) * (HEAD**-0.5) + bias_ref[...]
     last = lax.axis_index("lat") == LAT - 1
     group_q = ((lax.broadcasted_iota(jnp.int32, (HEADS * TOK, TOK), 0) // 72) % 2).astype(F32)
     group_k = (lax.broadcasted_iota(jnp.int32, (HEADS * TOK, TOK), 1) >= 72).astype(F32)
@@ -270,7 +293,7 @@
     slope = 0.5 * (1.0 + tangent) + 0.5 * inner * (1.0 - tangent * tangent) * GELU_SQRT * (
         1.0 + 3.0 * GELU_CUBE * inner * inner
     )
-    hidden_grad = (dot_nt(upstream_low, down_weight) * slope).astype(BF16)
+    hidden_grad = (dot(upstream_low, down_weight) * slope).astype(BF16)
     second_grad = dot_nt(hidden_grad, up_weight)
     mid_grad = upstream + norm_backward(second_grad, hat2, inv2, gain2)
     mid_low = mid_grad.astype(BF16)
@@ -283,7 +306,7 @@
     query_grad = jnp.zeros((TOK, C), F32)
     for n in range(HEADS):
         query_grad += jnp.where(of_head[n], dot(score_low[n * TOK : (n + 1) * TOK], keys), 0.0)
-        dense_rows(dense_s, score_grad[n * TOK : (n + 1) * TOK], n * DENSE)
+        dense_rows(score_ref, score_grad[n * TOK : (n + 1) * TOK], n * DENSE)
     query_grad = (query_grad * (HEAD**-0.5)).astype(BF16)
     key_grad = (dot_tn(score_low, q_stack) * (HEAD**-0.5)).astype(BF16)
     first_grad = (
@@ -298,16 +321,22 @@
         base = PART * slot
         flat_s[slot, 0:CELLS, 0:C] = moved_s[base : base + CELLS, :]
         flat_s[slot, 0:CELLS, C : 2 * C] = moved_s[base + CELLS : base + PART, :]
-        back_ref[slot] = flat_s[slot, 0:32, :].astype(BF16)
-
-    grad_s[:, 0:C] = dot_tn(first_in, query_grad)
-    grad_s[:, C : 2 * C] = dot_tn(first_in, key_grad)
-    grad_s[:, 2 * C : 3 * C] = dot_tn(first_in, value_grad)
-    grad_s[:, 3 * C : 4 * C] = dot_tn(context, mid_low)
-    grad_s[:, 4 * C : 8 * C] = dot_tn(second_in, hidden_grad)
-    spread = dot(hidden_low, spread_ref[...]).astype(BF16)
-    for part in range(4):
-        grad_s[:, (8 + part) * C : (9 + part) * C] = dot_tn(spread[:, part * C : (part + 1) * C], upstream_low)
+        for tile in range(3):
+            pack_s[slot, CELLS * tile : CELLS * tile + CELLS, :] = flat_s[
+                slot, 0:CELLS, tile * LANES : (tile + 1) * LANES
+            ]
+        back_ref[slot] = pack_s[slot, 0:64, :].astype(BF16)
+
+    first_in_ref[...] = first_in
+    query_grad_ref[...] = query_grad
+    key_grad_ref[...] = key_grad
+    value_grad_ref[...] = value_grad
+    context_ref[...] = context
+    mid_low_ref[...] = mid_low
+    second_in_ref[...] = second_in
+    hidden_grad_ref[...] = hidden_grad
+    hidden_low_ref[...] = hidden_low
+    upstream_ref[...] = upstream_low
     lane = lax.broadcasted_iota(jnp.int32, (TOK, LANES), 1)
     small = jnp.zeros((C, LANES), F32)
     for left, right in (
@@ -318,87 +347,46 @@
         for term in two_terms(left):
             small += dot_tn(term, right.astype(BF16))
     ge_s[...] = small
-    for tile in range(TILES):
-        rows_s[tile // 9, pl.ds(tile % 9, C, stride=9), :] = grad_s[:, tile * LANES : (tile + 1) * LANES]
     extra = jnp.zeros((32, LANES), F32)
     for k in range(6):
         line = ge_s[pl.ds(k, 32, stride=6), :]
         extra += pltpu.roll(line, 18 * k, 1) if k else line
-    sub64 = lax.broadcasted_iota(jnp.int32, (64, LANES), 0)
-    for half in range(2):
-        for block in range(32):
-            got = rows_s[half, 54 * block : 54 * block + 64, :]
-            tail = jnp.where(sub64 == 54, extra[block : block + 1], 0.0) if half == 0 else jnp.zeros_like(got)
-            got = jnp.where(sub64 < 54, got, tail).astype(BF16)
-            for part in range(4):
-                grads_ref[half, block // 8, part, block % 8] = got[16 * part : 16 * part + 16]
-
-    acc_s[...] = jnp.zeros((208, LANES), F32)
-    row32 = lax.broadcasted_iota(jnp.int32, (32, 2 * LANES), 0).astype(F32)
-    row128 = lax.broadcasted_iota(jnp.int32, (LANES, 2 * LANES), 0).astype(F32)
-
-    def pair(ref, row):
-        return jnp.concatenate([ref[pl.ds(row, 1), :], ref[pl.ds(row + DENSE // 2, 1), :]], axis=1)
-
-    def scatter(step, carry):
-        chosen = row32 == pair(high_s, step)
-        hot = jnp.where(row128 == pair(low_s, step), 1.0, 0.0).astype(BF16)
-        spread_out = [jnp.where(chosen, pair(dense_s, n * DENSE + step), 0.0) for n in range(HEADS)]
-        acc_s[0 : 32 * HEADS, :] += dot_nt(jnp.concatenate(spread_out, axis=0).astype(BF16), hot)
-        return carry
-
-    lax.fori_loop(0, DENSE // 2, scatter, 0)
-    sub16 = lax.broadcasted_iota(jnp.int32, (16, LANES), 0)
-    for block in range(16):
-        bias_out_ref[block // 8, block % 8] = jnp.where(sub16 < 12, acc_s[12 * block : 12 * block + 16, :], 0.0)
-
-
-def window(block, pair_index, bias_table, gain1, gain2, mix_weight, out_weight, up_weight, down_weight):
-    token = np.arange(TOK)
-    slot, level, cell = token // PART, (token % PART) // CELLS, token % CELLS
-    row, col = 3 * (slot // 2) + cell // 6, 6 * (slot % 2) + cell % 6
-    order = np.zeros((TOK, TOK), np.float32)
-    order[token, (row * WIN_LON + col) * 2 + level] = 1.0
-    column = np.arange(FF)
-    spread = np.zeros((FF, FF), np.float32)
-    spread[4 * (column % C) + column // C, column] = 1.0
+    extra_ref[...] = extra
+
+
+def window(block, bias, gain1, gain2, mix_weight, out_weight, up_weight, down_weight):
     vmem = pl.BlockSpec(memory_space=pltpu.VMEM)
+    narrow = jax.ShapeDtypeStruct((TOK, C), BF16)
+    wide = jax.ShapeDtypeStruct((TOK, FF), BF16)
     return pl.pallas_call(
         window_kernel,
         out_shape=(
-            jax.ShapeDtypeStruct((2, 4, 4, ZLO, 16, LANES), BF16),
-            jax.ShapeDtypeStruct((2, ZLO, 16, LANES), F32),
-            jax.ShapeDtypeStruct((4, 32, 2 * C), BF16),
+            narrow, narrow, narrow, narrow, narrow, narrow, narrow, wide, wide, narrow,
+            jax.ShapeDtypeStruct((HEADS * DENSE, LANES), F32),
+            jax.ShapeDtypeStruct((32, LANES), F32),
+            jax.ShapeDtypeStruct((4, 64, LANES), BF16),
         ),
-        in_specs=[vmem] * 11,
-        out_specs=(vmem, vmem, vmem),
+        in_specs=[vmem] * 8,
+        out_specs=(vmem,) * 13,
         scratch_shapes=[
-            pltpu.VMEM((4, 48, 2 * C), F32),
+            pltpu.VMEM((4, 40, 2 * C), F32),
             pltpu.VMEM((TOK, C), F32),
             pltpu.VMEM((TOK, C), F32),
             pltpu.VMEM((TOK, LANES), F32),
-            pltpu.VMEM((DENSE, LANES), F32),
-            pltpu.VMEM((DENSE, LANES), F32),
-            pltpu.VMEM((HEADS * 32, LANES), F32),
-            pltpu.VMEM((HEADS * DENSE, LANES), F32),
-            pltpu.VMEM((HEADS * TOK, TOK), F32),
-            pltpu.VMEM((208, LANES), F32),
-            pltpu.VMEM((C, COLS), F32),
-            pltpu.VMEM((2, 9 * C + 16, LANES), F32),
             pltpu.VMEM((C, LANES), F32),
             pltpu.VMEM((TOK, C), F32),
+            pltpu.VMEM((4, SENT, LANES), F32),
         ],
         compiler_params=pltpu.CompilerParams(vmem_limit_bytes=VMEM_LIMIT),
         name="window",
-    )(
-        block, pair_index, bias_table, gain1, gain2, mix_weight, out_weight, up_weight, down_weight,
-        jnp.asarray(order, BF16), jnp.asarray(spread, BF16),
-    )
+    )(block, bias, gain1, gain2, mix_weight, out_weight, up_weight, down_weight)
 
 
 def reduce_kernel(
-    grads_ref, bias_ref, back_ref,
+    first_in_ref, query_grad_ref, key_grad_ref, value_grad_ref, context_ref, mid_low_ref, second_in_ref, hidden_grad_ref,
+    hidden_low_ref, upstream_ref, score_ref, extra_ref, back_ref, high_ref, low_ref, spread_ref,
     dense_out, bias_out, back_out, total_out,
+    grad_s, rows_s, grads, acc_s, bias_s,
     core_r, plane_s, plane_r, line_s, line_r, share, bcore_r, bline_s, bline_r, brow_r, ball, back_r, squares_z, squares_y,
     core_ss, core_rs, plane_ss, plane_rs, line_ss, line_rs, share_ss, share_rs, bcore_ss, bcore_rs, bline_ss, bline_rs,
     brow_ss, brow_rs, ball_ss, ball_rs, bpair_ss, bpair_rs, back_ss, back_rs, sz_ss, sz_rs, sy_ss, sy_rs,
@@ -423,17 +411,35 @@
             peers.append({"lon": (lon + sign * dc + LON) % LON, "lat": (lat + sign * dr + LAT) % LAT})
     for peer in peers:
         pl.semaphore_signal(barrier, inc=1, device_id=peer, device_id_type=MESH)
+
+    first_in = first_in_ref[...]
+    upstream_low = upstream_ref[...]
+    grad_s[:, 0:C] = dot_tn(first_in, query_grad_ref[...])
+    grad_s[:, C : 2 * C] = dot_tn(first_in, key_grad_ref[...])
+    grad_s[:, 2 * C : 3 * C] = dot_tn(first_in, value_grad_ref[...])
+    grad_s[:, 3 * C : 4 * C] = dot_tn(context_ref[...], mid_low_ref[...])
+    grad_s[:, 4 * C : 8 * C] = dot_tn(second_in_ref[...], hidden_grad_ref[...])
+    spread = dot(hidden_low_ref[...], spread_ref[...]).astype(BF16)
+    for part in range(4):
+        grad_s[:, (8 + part) * C : (9 + part) * C] = dot_tn(spread[:, part * C : (part + 1) * C], upstream_low)
+    for tile in range(TILES):
+        rows_s[tile // 9, pl.ds(tile % 9, C, stride=9), :] = grad_s[:, tile * LANES : (tile + 1) * LANES]
+    sub64 = lax.broadcasted_iota(jnp.int32, (64, LANES), 0)
+    for half in range(2):
+        for block in range(32):
+            got = rows_s[half, 54 * block : 54 * block + 64, :]
+            tail = jnp.where(sub64 == 54, extra_ref[block : block + 1, :], 0.0) if half == 0 else 0.0
+            got = jnp.where(sub64 < 54, got, tail).astype(BF16)
+            for part in range(4):
+                grads[half, block // 8, part, block % 8] = got[16 * part : 16 * part + 16]
+
     pl.semaphore_wait(barrier, len(peers))
-
     sends = []
 
-    bcore = remote(bias_ref.at[other], bcore_r, bcore_ss, bcore_rs, at(x, y, z, other))
-    bcore.start()
-    sends.append(bcore)
     core_copies = []
     for j in range(4):
         to = (y + 1 + j) % 4
-        copy = remote(grads_ref.at[other, to], core_r.at[to], core_ss.at[j], core_rs.at[j], at(x, y, z, other))
+        copy = remote(grads.at[other, to], core_r.at[to], core_ss.at[j], core_rs.at[j], at(x, y, z, other))
         copy.start()
         core_copies.append(copy)
     sends += core_copies
@@ -451,26 +457,12 @@
         back_copies.append((slot, copy))
     sends += [copy for _, copy in back_copies]
 
-    bcore.wait_recv()
-    for part in range(ZLO):
-        bline_s[part] = bias_ref[core, part] + bcore_r[part]
-    bline_r[z_lo] = bline_s[z_lo]
-    bline_copies = []
-    for d in range(1, ZLO):
-        to = (z_lo + d) % ZLO
-        copy = remote(
-            bline_s.at[to], bline_r.at[z_lo], bline_ss.at[d], bline_rs.at[d], at(x, y, z_hi * ZLO + to, core)
-        )
-        copy.start()
-        bline_copies.append(copy)
-    sends += bline_copies
-
     plane_copies = {}
     for j in range(4):
         to_y = (y + 1 + j) % 4
         core_copies[j].wait_recv()
         for part in range(4):
-            plane_s[to_y, part] = (grads_ref[core, to_y, part].astype(F32) + core_r[to_y, part].astype(F32)).astype(BF16)
+            plane_s[to_y, part] = (grads[core, to_y, part].astype(F32) + core_r[to_y, part].astype(F32)).astype(BF16)
         for i in range(4):
             dx, dy = (i + 1) % 4, (j + 1) % 4
             d = dx * 4 + dy
@@ -489,19 +481,41 @@
             plane_copies[d] = copy
     sends += list(plane_copies.values())
 
-    for copy in bline_copies:
-        copy.wait_recv()
-    part_sum = bline_r[0]
-    for part in range(1, ZLO):
-        part_sum = part_sum + bline_r[part]
-    brow_r[y] = part_sum
-    brow_copies = []
-    for d in range(1, 4):
-        to = (y + d) % 4
-        copy = remote(brow_r.at[y], brow_r.at[y], brow_ss.at[d], brow_rs.at[d], at(x, to, z, core))
-        copy.start()
-        brow_copies.append(copy)
-    sends += brow_copies
+    acc_s[...] = jnp.zeros((208, LANES), F32)
+    row32 = lax.broadcasted_iota(jnp.int32, (32, 2 * LANES), 0).astype(F32)
+    row128 = lax.broadcasted_iota(jnp.int32, (LANES, 2 * LANES), 0).astype(F32)
+
+    def pair(ref, row):
+        return jnp.concatenate([ref[pl.ds(row, 1), :], ref[pl.ds(row + DENSE // 2, 1), :]], axis=1)
+
+    def scatter(step, carry):
+        chosen = row32 == pair(high_ref, step)
+        hot = jnp.where(row128 == pair(low_ref, step), 1.0, 0.0).astype(BF16)
+        spread_out = [jnp.where(chosen, pair(score_ref, n * DENSE + step), 0.0) for n in range(HEADS)]
+        acc_s[0 : 32 * HEADS, :] += dot_nt(jnp.concatenate(spread_out, axis=0).astype(BF16), hot)
+        return carry
+
+    lax.fori_loop(0, DENSE // 2, scatter, 0)
+    sub16 = lax.broadcasted_iota(jnp.int32, (16, LANES), 0)
+    for block in range(16):
+        bias_s[block // 8, block % 8] = jnp.where(sub16 < 12, acc_s[12 * block : 12 * block + 16, :], 0.0)
+
+    bcore = remote(bias_s.at[other], bcore_r, bcore_ss, bcore_rs, at(x, y, z, other))
+    bcore.start()
+    sends.append(bcore)
+    bcore.wait_recv()
+    for part in range(ZLO):
+        bline_s[part] = bias_s[core, part] + bcore_r[part]
+    bline_r[z_lo] = bline_s[z_lo]
+    bline_copies = []
+    for d in range(1, ZLO):
+        to = (z_lo + d) % ZLO
+        copy = remote(
+            bline_s.at[to], bline_r.at[z_lo], bline_ss.at[d], bline_rs.at[d], at(x, y, z_hi * ZLO + to, core)
+        )
+        copy.start()
+        bline_copies.append(copy)
+    sends += bline_copies
 
     for copy in plane_copies.values():
         copy.wait_recv()
@@ -518,6 +532,20 @@
         copy.start()
         line_copies.append(copy)
     sends += line_copies
+
+    for copy in bline_copies:
+        copy.wait_recv()
+    part_sum = bline_r[0]
+    for part in range(1, ZLO):
+        part_sum = part_sum + bline_r[part]
+    brow_r[y] = part_sum
+    brow_copies = []
+    for d in range(1, 4):
+        to = (y + d) % 4
+        copy = remote(brow_r.at[y], brow_r.at[y], brow_ss.at[d], brow_rs.at[d], at(x, to, z, core))
+        copy.start()
+        brow_copies.append(copy)
+    sends += brow_copies
 
     for copy in brow_copies:
         copy.wait_recv()
@@ -602,7 +630,10 @@
         copy.wait_send()
 
 
-def reduce(grads, bias, back):
+def reduce(*operands):
+    column = np.arange(FF)
+    spread = np.zeros((FF, FF), np.float32)
+    spread[4 * (column % C) + column // C, column] = 1.0
     vmem = pl.BlockSpec(memory_space=pltpu.VMEM)
     dma = pltpu.SemaphoreType.DMA
     return pl.pallas_call(
@@ -610,12 +641,17 @@
         out_shape=(
             jax.ShapeDtypeStruct((8, 16, LANES), F32),
             jax.ShapeDtypeStruct((2, ZLO, 16, LANES), F32),
-            jax.ShapeDtypeStruct((4, 32, 2 * C), BF16),
+            jax.ShapeDtypeStruct((4, 64, LANES), BF16),
             jax.ShapeDtypeStruct((1, LANES), F32),
         ),
-        in_specs=[vmem] * 3,
+        in_specs=[vmem] * 16,
         out_specs=(vmem,) * 4,
         scratch_shapes=[
+            pltpu.VMEM((C, COLS), F32),
+            pltpu.VMEM((2, 9 * C + 16, LANES), F32),
+            pltpu.VMEM((2, 4, 4, ZLO, 16, LANES), BF16),
+            pltpu.VMEM((208, LANES), F32),
+            pltpu.VMEM((2, ZLO, 16, LANES), F32),
             pltpu.VMEM((4, 4, ZLO, 16, LANES), BF16),
             pltpu.VMEM((4, 4, ZLO, 16, LANES), BF16),
             pltpu.VMEM((16, ZLO, 16, LANES), BF16),
@@ -627,7 +663,7 @@
             pltpu.VMEM((ZLO, 16, LANES), F32),
             pltpu.VMEM((4, 16, LANES), F32),
             pltpu.VMEM((2, ZLO, 16, LANES), F32),
-            pltpu.VMEM((4, 32, 2 * C), BF16),
+            pltpu.VMEM((4, 64, LANES), BF16),
             pltpu.VMEM((16, 1, LANES), F32),
             pltpu.VMEM((4, 1, LANES), F32),
             dma((4,)), dma((4,)),
@@ -645,7 +681,7 @@
         ],
         compiler_params=pltpu.CompilerParams(collective_id=1, has_side_effects=True, vmem_limit_bytes=VMEM_LIMIT),
         name="sum_over_devices",
-    )(grads, bias, back)
+    )(*operands, jnp.asarray(spread, BF16))
 
 
 def output_kernel(
@@ -674,19 +710,28 @@
     lane = lax.broadcasted_iota(jnp.int32, (24, LANES), 1)
     sub = lax.broadcasted_iota(jnp.int32, (24, LANES), 0)
     small = jnp.zeros((24, LANES), F32)
+    wide = jnp.zeros((8, LANES), F32)
+    sub8 = lax.broadcasted_iota(jnp.int32, (8, LANES), 0)
+    line8 = jnp.broadcast_to(extra, (8, LANES))
     for row in range(3):
+        turned = jnp.where(odd, pltpu.roll(line8, LANES - 18 * (3 + row), 1), pltpu.roll(line8, (LANES - 18 * row) % LANES, 1))
+        wide = jnp.where(sub8 == row, turned, wide)
         start = jnp.where(odd, 18 * (3 + row), 18 * row)
         column = jnp.sum(jnp.where(lane == sub + start, extra, 0.0), axis=1, keepdims=True)
         small = small + jnp.where(lane == row, column, 0.0)
-    embed_ref[...] = small[0:KINDS, 0:3]
+    embed_ref[...] = wide[0:3, 0:KINDS]
     gain_ref[...] = small[KINDS : KINDS + 2, 0:3]
     for block in range(16):
         bias_s[12 * block : 12 * block + 12, :] = bias_ref[block // 8, block % 8, 0:12, :] * factor
     for row in range(HI):
         width = min(LANES, PAIRS - row * LANES)
-        table_ref[0, :, row * LANES : row * LANES + width] = bias_s[pl.ds(row, HEADS, stride=32), :][:, 0:width]
+        line = bias_s[pl.ds(row, HEADS, stride=32), :][:, 0:width]
+        for head in range(HEADS):
+            table_ref[head, :, row * LANES : row * LANES + width] = line[head : head + 1]
     for quarter in range(4):
-        back_s[quarter] = back_ref[quarter].astype(F32)
+        packed = back_ref[quarter].astype(F32)
+        for tile in range(3):
+            back_s[quarter, 0:CELLS, tile * LANES : (tile + 1) * LANES] = packed[CELLS * tile : CELLS * tile + CELLS]
         for i in range(3):
             row, half = 3 * (quarter // 2) + i, quarter % 2
             token_s[row, 6 * half : 6 * half + 6, :] = back_s[quarter, 6 * i : 6 * i + 6, :]
@@ -705,8 +750,8 @@
             jax.ShapeDtypeStruct((3, FF), F32),
             jax.ShapeDtypeStruct((12, C), F32),
             jax.ShapeDtypeStruct((2, 3), F32),
-            jax.ShapeDtypeStruct((KINDS, 3), F32),
-            jax.ShapeDtypeStruct((1, HEADS, PAIRS), F32),
+            jax.ShapeDtypeStruct((3, KINDS), F32),
+            jax.ShapeDtypeStruct((HEADS, 1, PAIRS), F32),
         ),
         in_specs=[vmem] * 4,
         out_specs=(vmem,) * 8,
@@ -726,12 +771,14 @@
     tokens, kinds, kind_embed, pair_index, bias_table, attn_gain, mlp_gain,
     mix_weight, out_weight, up_weight, down_weight, cotangent,
 ):
-    block = halo(tokens, kinds, kind_embed, cotangent)
-    grads, bias, back = window(
-        block, pair_index, bias_table, attn_gain.reshape(1, C), mlp_gain.reshape(1, C),
-        mix_weight, out_weight, up_weight, down_weight,
+    block, bias, high, low = halo(
+        tokens, kinds.transpose(0, 2, 1), kind_embed, cotangent, pair_index, bias_table.transpose(1, 0, 2)
     )
-    return outputs(*reduce(grads, bias, back))
+    parts = window(
+        block, bias, attn_gain.reshape(1, C), mlp_gain.reshape(1, C), mix_weight, out_weight, up_weight, down_weight.T
+    )
+    token, mix, out, up, down, gain, embed, table = outputs(*reduce(*parts, high, low))
+    return token, mix, out, up, down, gain, embed.T, table.transpose(1, 0, 2)
 
 
 def solution(mesh):

time: 117 us -> 96.6 us (0.83)
  Pallas kernels: 108 us -> 94.8 us
  local copies, waits for them, and re-layouts: 7.83 us -> 0 us
    pallas_call x2, Pallas kernels: 54.2 us -> 31.9 us  [the longest x1 25.3 us: halo(): pl.pallas_call(halo_kernel, out_shape=(jax.ShapeDtypeStruct((4, SENT, LAN...]
    pallas_call x1, Pallas kernels: 52.3 us -> 61.1 us  [reduce(): pl.pallas_call(reduce_kernel, out_shape=(jax.ShapeDtypeStruct((8, 16, LAN...]
    unnamed x3 -> x0, local copies, waits for them, and re-layouts: 4.87 us -> none
    pallas_call x2 -> x0, local copies, waits for them, and re-layouts: 2.96 us -> none  [outputs(): pl.pallas_call(output_kernel, out_shape=(jax.ShapeDtypeStruct((WIN_LAT, W...]
where the time goes in v2:
time: 96.6 us; the launch traced here: 95.4 us
  Pallas kernels  94.8 us (98%)
    pallas_call x1, Pallas kernels, reduce(): pl.pallas_call(reduce_kernel, out_shape=(jax.ShapeDtypeStruct((8, 16, LAN...  61.1 us
    pallas_call x1, Pallas kernels, halo(): pl.pallas_call(halo_kernel, out_shape=(jax.ShapeDtypeStruct((4, SENT, LAN...  25.3 us
    pallas_call x1, Pallas kernels, window(): pl.pallas_call(window_kernel, out_shape=(narrow, narrow, narrow, narrow,...  6.6 us

profile of v2, /device:TPU:1, one launch (start us, length us, event | category | flops | bytes accessed | tf_op | source)
XLA Modules:
  0.0 95.4 jit_solution(16633670912207017834)
XLA Ops:
  0.6 25.3 %halo_in.1 = (bf16[4,112,128]{2,1,0:T(8,128)(2,1)}, f32[864,144]{1,0:T(8,128)}, f32[176,128]{1,0:T(8,128)}, f32[176,128]{1,0:T(8,128)}) custom-call(bf16[6,12,384]{2,1,0:T(8,128)(2,1)} %tok_ref.1, s32[6,2,12]{2,1,0:T(2,128)} %bitcast.9, bf16[16,192]{1,0:T(8,128)(2,1)} %embed_ref.1, bf16[6,12,384]{2,1,0:T(8,128)(2,1)} %cot_ref.1, s32[144,144]{1,0:T(8,128)} %index_ref.1, ...), custom_call_target="tpu_custom_call" | custom-call | tf_op jit(solution)/shard_map/halo_in/pallas_call | solution.py:194
  25.9 6.6 %window.1 = (bf16[144,192]{1,0:T(8,128)(2,1)}, bf16[144,192]{1,0:T(8,128)(2,1)}, bf16[144,192]{1,0:T(8,128)(2,1)}, bf16[144,192]{1,0:T(8,128)(2,1)}, bf16[144,19...) custom-call(bf16[4,112,128]{2,1,0:T(8,128)(2,1)} %get-tuple-element., ...), custom_call_target="tpu_custom_call" | custom-call | tf_op jit(solution)/shard_map/window/pallas_call | solution.py:361
  32.5 61.1 %sum_over_devices.1 = (f32[8,16,128]{2,1,0:T(8,128)}, f32[2,8,16,128]{3,2,1,0:T(8,128)}, bf16[4,64,128]{2,1,0:T(8,128)(2,1)}, f32[1,128]{1,0:T(1,128)}) custom-call(bf16[144,192]{1,0:T(8,128)(2,1)} %get-tuple-element.39.first_in_ref, bf16[144,192]{1,0:T(8,128)(2,1)} %get-tuple-element.40.query_grad_ref, bf16[144,192]{1,0:T(8,128)(2,1)} %get-tuple-element.41.key_grad_ref, ...), custom_call_target="tpu_custom_call" | custom-call | tf_op jit(solution)/shard_map/sum_over_devices/pallas_call | solution.py:639
  93.6 1.8 %scaled_outputs.1 = (bf16[6,12,384]{2,1,0:T(8,128)(2,1)}, f32[3,576]{1,0:T(4,128)}, f32[3,192]{1,0:T(4,128)}, f32[3,768]{1,0:T(4,128)}, f32[12,192]{1,0:T(8,128)...) custom-call(f32[8,16,128]{2,1,0:T(8,128)} %get-tuple-element.54.dense_ref, ...), custom_call_target="tpu_custom_call" | custom-call | tf_op jit(solution)/shard_map/scaled_outputs/pallas_call | solution.py:744

commit v3 on v2

v3 whole, which is shorter than its diff:
```python
import jax
import jax.numpy as jnp
import numpy as np
from jax import lax
from jax.experimental import pallas as pl
from jax.experimental.pallas import tpu as pltpu
from jax.sharding import PartitionSpec as P

F32 = jnp.float32
BF16 = jnp.bfloat16
MESH = pl.DeviceIdType.MESH

C = 192
HEADS = 6
HEAD = 32
FF = 768
WIN_LAT = 6
WIN_LON = 12
KINDS = 16
PAIRS = 3312
TOK = 144
CELLS = 18
PART = 36
LANES = 128
HI = 26
COLS = 2304
TILES = 18
NORM_EPS = 1e-05
RMS_EPS = 1e-06
GELU_SQRT = 0.7978845608028654
GELU_CUBE = 0.044715
LON, LAT = 64, 8
ZLO = 8
VMEM_LIMIT = 56 * 1024 * 1024


def place():
    lon, lat = lax.axis_index("lon"), lax.axis_index("lat")
    return lat >> 1, lon >> 4, ((lat & 1) << 3) + ((lon >> 1) & 7), lon & 1


def at(x, y, z, core):
    return {"lon": (y << 4) + ((z & 7) << 1) + core, "lat": (x << 1) + (z >> 3)}


def beside(lat, lon, rows, columns):
    return {"lon": (lon + columns) & (LON - 1), "lat": (lat + rows) & (LAT - 1)}


def dot(a, b):
    return lax.dot_general(a, b, (((1,), (0,)), ((), ())), preferred_element_type=F32)


def dot_nt(a, b):
    return lax.dot_general(a, b, (((1,), (1,)), ((), ())), preferred_element_type=F32)


def dot_tn(a, b):
    return lax.dot_general(a, b, (((0,), (0,)), ((), ())), preferred_element_type=F32)


def two_terms(v):
    high = v.astype(BF16)
    return high, (v - high.astype(F32)).astype(BF16)


def dense_rows(ref, values, base):
    ref[base : base + TOK, :] = values[:, 0:LANES]
    tail = values[:, LANES:TOK]
    tail = jnp.concatenate([tail, jnp.zeros((TOK, LANES - 16), tail.dtype)], axis=1)
    row = tail[0:16]
    for group in range(1, 8):
        row = row + pltpu.roll(tail[16 * group : 16 * group + 16], 16 * group, 1)
    ref[base + TOK : base + TOK + 16, :] = row
    ref[base + TOK + 16 : base + TOK + 32, :] = tail[LANES:TOK]


DENSE = TOK + 32
FLAT = 3 * PART
SENT = FLAT + 4


def layer_norm(values, gain):
    centred = values - jnp.mean(values, axis=-1, keepdims=True)
    inverse = lax.rsqrt(jnp.mean(centred * centred, axis=-1, keepdims=True) + NORM_EPS)
    normed = centred * inverse
    return normed * gain, normed, inverse


def norm_backward(upstream, normed, inverse, gain):
    scaled = upstream * gain
    return inverse * (
        scaled
        - jnp.mean(scaled, axis=-1, keepdims=True)
        - normed * jnp.mean(scaled * normed, axis=-1, keepdims=True)
    )


def main_kernel(
    tok_ref, kind_ref, embed_ref, cot_ref, index_ref, table_ref, order_ref,
    gain1_ref, gain2_ref, mix_ref, outw_ref, up_ref, down_ref,
    dense_out, bias_out, back_out, total_out,
    tok_s, kind_s, flat_s, pack_s, send, recv, table_s, dense_s, high_s, low_s, bias_s, spread_s,
    grid_s, x_s, g_s, hot_s, ge_s, moved_s, unpack_s, score_s, extra_s, back_s,
    grad_s, rows_s, grads, acc_s, parts_s,
    core_r, plane_s, plane_r, line_s, line_r, share, bcore_r, bline_s, bline_r, brow_r, ball, back_r, squares_z, squares_y,
    halo_ss, halo_rs,
    core_ss, core_rs, plane_ss, plane_rs, line_ss, line_rs, share_ss, share_rs, bcore_ss, bcore_rs, bline_ss, bline_rs,
    brow_ss, brow_rs, ball_ss, ball_rs, bpair_ss, bpair_rs, back_ss, back_rs, sz_ss, sz_rs, sy_ss, sy_rs,
):
    lon, lat = lax.axis_index("lon"), lax.axis_index("lat")
    x, y, z, core = place()
    z_lo, z_hi = z & 7, z >> 3
    other = 1 - core

    def remote(src, dst, send_sem, recv_sem, target):
        return pltpu.make_async_remote_copy(
            src_ref=src, dst_ref=dst, send_sem=send_sem, recv_sem=recv_sem, device_id=target, device_id_type=MESH
        )

    barrier = pltpu.get_barrier_semaphore()
    peers = []
    for dr, dc in ((1, 0), (0, 1), (1, 1)):
        peers += [beside(lat, lon, -dr, -dc), beside(lat, lon, dr, dc)]
    peers += [at(x, y, (z + d) & 15, core) for d in range(1, 16)]
    peers += [at((x + d // 4) & 3, (y + d % 4) & 3, z, core) for d in range(1, 16)]
    peers += [at((x + d) & 3, y, z, other) for d in range(4)]
    for peer in peers:
        pl.semaphore_signal(barrier, inc=1, device_id=peer, device_id_type=MESH)

    embed = embed_ref[...].astype(F32)
    blank = jnp.zeros((KINDS, C), F32)
    wide = jnp.concatenate(
        [jnp.concatenate([embed, blank], axis=1), jnp.concatenate([blank, embed], axis=1)], axis=0
    ).astype(BF16)
    kind_s[...] = jnp.zeros((4, 8, LANES), F32)
    for row in range(WIN_LAT):
        tok = tok_ref[row].astype(F32)
        cot = cot_ref[row].astype(F32)
        kind = kind_ref[row].astype(F32)
        for half in range(2):
            quarter = 2 * (row // 3) + half
            start = 6 * (row % 3)
            cells = slice(6 * half, 6 * half + 6)
            tok_s[quarter, start : start + 6, :] = tok[cells]
            flat_s[quarter, CELLS + start : CELLS + start + 6, :] = cot[cells]
            kind_s[quarter, 0:2, start : start + 6] = kind[:, cells]
    sub = lax.broadcasted_iota(jnp.int32, (2 * KINDS, LANES), 0).astype(F32)
    for quarter in range(4):
        kinds = kind_s[quarter]
        hot = (sub == kinds[0:1]) | (sub - KINDS == kinds[1:2])
        hot = jnp.where(hot, 1.0, 0.0).astype(BF16)[:, 0:24]
        stored = tok_s[quarter] + dot_tn(hot, wide)
        flat_s[quarter, 0:CELLS, :] = stored[0:CELLS]
        for tile in range(3):
            pack_s[quarter, PART * tile : PART * tile + PART, :] = flat_s[
                quarter, 0:PART, tile * LANES : (tile + 1) * LANES
            ]
        pack_s[quarter, FLAT:SENT, :] = jnp.zeros((4, LANES), F32)
        pack_s[quarter, FLAT : FLAT + 1, :] = kinds[0:1] + pltpu.roll(kinds, CELLS, 1)[1:2]
        send[quarter] = pack_s[quarter].astype(BF16)
    order = order_ref[...]
    index = index_ref[...]
    high = (index // LANES).astype(F32).astype(BF16)
    low = (index % LANES).astype(F32).astype(BF16)
    dense_rows(high_s, dot_nt(dot(order, high).astype(BF16), order), 0)
    dense_rows(low_s, dot_nt(dot(order, low).astype(BF16), order), 0)
    table_s[...] = jnp.zeros((HEADS * 32, LANES), F32)
    for row in range(HI):
        width = min(LANES, PAIRS - row * LANES)
        for head in range(HEADS):
            table_s[32 * head + row : 32 * head + row + 1, 0:width] = table_ref[
                head, :, row * LANES : row * LANES + width
            ]

    column = lax.broadcasted_iota(jnp.int32, (1, FF), 1)
    part = jnp.where(column >= C, 1, 0) + jnp.where(column >= 2 * C, 1, 0) + jnp.where(column >= 3 * C, 1, 0)
    unit = (4 * (column - C * part) + part).astype(F32)
    for block in range(6):
        place_at = (lax.broadcasted_iota(jnp.int32, (LANES, FF), 0) + LANES * block).astype(F32)
        spread_s[LANES * block : LANES * (block + 1), :] = jnp.where(place_at == unit, 1.0, 0.0).astype(BF16)

    pl.semaphore_wait(barrier, len(peers))
    halo_copies = []
    for slot in (3, 2, 1):
        copy = remote(
            send.at[3 - slot], recv.at[slot], halo_ss.at[slot], halo_rs.at[slot], beside(lat, lon, -(slot // 2), -(slot % 2))
        )
        copy.start()
        halo_copies.append(copy)
    sends = list(halo_copies)

    def gather(step, carry):
        start = pl.multiple_of(step * 16, 16)
        lows = low_s[pl.ds(start, 16), :].astype(jnp.int32)
        highs = high_s[pl.ds(start, 16), :]
        totals = [jnp.zeros((16, LANES), F32) for _ in range(HEADS)]
        for row in range(HI):
            chosen = highs == float(row)
            for head in range(HEADS):
                line = jnp.broadcast_to(table_s[32 * head + row : 32 * head + row + 1, :], (16, LANES))
                found = jnp.take_along_axis(line, lows, axis=1, mode="promise_in_bounds")
                totals[head] = jnp.where(chosen, found, totals[head])
        for head in range(HEADS):
            dense_s[pl.ds(pl.multiple_of(head * DENSE + start, 16), 16), :] = totals[head]
        return carry

    lax.fori_loop(0, DENSE // 16, gather, 0)
    for head in range(HEADS):
        base = head * DENSE
        bias_s[head * TOK : head * TOK + TOK, 0:LANES] = dense_s[base : base + TOK, :]
        row = dense_s[base + TOK : base + TOK + 16, :]
        for group in range(8):
            turned = row if group == 0 else pltpu.roll(row, LANES - 16 * group, 1)
            bias_s[head * TOK + 16 * group : head * TOK + 16 * group + 16, LANES:TOK] = turned[:, 0:16]
        bias_s[head * TOK + LANES : head * TOK + TOK, LANES:TOK] = dense_s[base + TOK + 16 : base + TOK + 32, 0:16]

    for copy in halo_copies:
        copy.wait_recv()
    lane36 = lax.broadcasted_iota(jnp.int32, (PART, LANES), 1)
    sub36 = lax.broadcasted_iota(jnp.int32, (PART, LANES), 0)
    for slot in range(4):
        unpack_s[slot] = (send[3] if slot == 0 else recv[slot]).astype(F32)
        for tile in range(3):
            grid_s[slot, 0:PART, tile * LANES : (tile + 1) * LANES] = unpack_s[slot, PART * tile : PART * tile + PART, :]
        toks = grid_s[slot, 0:CELLS, :]
        cots = grid_s[slot, CELLS:PART, :]
        base = PART * slot
        x_s[base : base + CELLS, :] = toks[:, 0:C]
        x_s[base + CELLS : base + PART, :] = toks[:, C : 2 * C]
        g_s[base : base + CELLS, :] = cots[:, 0:C]
        g_s[base + CELLS : base + PART, :] = cots[:, C : 2 * C]
        kind_row = unpack_s[slot, FLAT : FLAT + 1, :]
        kind_col = jnp.sum(jnp.where(lane36 == sub36, kind_row, 0.0), axis=1, keepdims=True)
        hot_s[base : base + PART, :] = jnp.where(lane36.astype(F32) == kind_col, 1.0, 0.0)

    gain1, gain2 = gain1_ref[...], gain2_ref[...]
    mix_weight, out_weight = mix_ref[...], outw_ref[...]
    up_weight, down_weight = up_ref[...], down_ref[...]
    residual = x_s[...]
    upstream = g_s[...]
    upstream_low = upstream.astype(BF16)
    first, hat1, inv1 = layer_norm(residual, gain1)
    first_in = first.astype(BF16)
    mixed = dot(first_in, mix_weight)
    queries = mixed[:, 0:C].astype(BF16).astype(F32)
    keys = mixed[:, C : 2 * C].astype(BF16)
    values = mixed[:, 2 * C : 3 * C].astype(BF16)
    channel = lax.broadcasted_iota(jnp.int32, (TOK, C), 1)
    of_head = [(channel >= HEAD * n) & (channel < HEAD * n + HEAD) for n in range(HEADS)]
    q_stack = jnp.concatenate([jnp.where(m, queries, 0.0) for m in of_head], axis=0).astype(BF16)
    scores = dot_nt(q_stack, keys) * (HEAD**-0.5) + bias_s[...]
    last = lat == LAT - 1
    group_q = ((lax.broadcasted_iota(jnp.int32, (HEADS * TOK, TOK), 0) // 72) % 2).astype(F32)
    group_k = (lax.broadcasted_iota(jnp.int32, (HEADS * TOK, TOK), 1) >= 72).astype(F32)
    allowed = jnp.abs(group_q - group_k) * jnp.where(last, 1.0, 0.0) < 0.5
    expon = jnp.where(allowed, jnp.exp(scores), 0.0)
    attend = expon / jnp.sum(expon, axis=-1, keepdims=True)
    attend_low = attend.astype(BF16)
    context = jnp.zeros((TOK, C), F32)
    for n in range(HEADS):
        context += jnp.where(of_head[n], dot(attend_low[n * TOK : (n + 1) * TOK], values), 0.0)
    context = context.astype(BF16)
    mid = residual + dot(context, out_weight)
    second, hat2, inv2 = layer_norm(mid, gain2)
    second_in = second.astype(BF16)
    inner = dot(second_in, up_weight)
    tangent = jnp.tanh(GELU_SQRT * (inner + GELU_CUBE * inner * inner * inner))
    hidden_low = (0.5 * inner * (1.0 + tangent)).astype(BF16)
    slope = 0.5 * (1.0 + tangent) + 0.5 * inner * (1.0 - tangent * tangent) * GELU_SQRT * (
        1.0 + 3.0 * GELU_CUBE * inner * inner
    )
    hidden_grad = (dot(upstream_low, down_weight) * slope).astype(BF16)
    second_grad = dot_nt(hidden_grad, up_weight)
    mid_grad = upstream + norm_backward(second_grad, hat2, inv2, gain2)
    mid_low = mid_grad.astype(BF16)
    context_grad = dot_nt(mid_low, out_weight).astype(BF16).astype(F32)
    c_stack = jnp.concatenate([jnp.where(m, context_grad, 0.0) for m in of_head], axis=0).astype(BF16)
    attend_grad = dot_nt(c_stack, values)
    value_grad = dot_tn(attend_low, c_stack).astype(BF16)
    score_grad = attend * (attend_grad - jnp.sum(attend * attend_grad, axis=-1, keepdims=True))
    score_s[...] = score_grad
    score_low = score_grad.astype(BF16)
    query_grad = jnp.zeros((TOK, C), F32)
    for n in range(HEADS):
        query_grad += jnp.where(of_head[n], dot(score_low[n * TOK : (n + 1) * TOK], keys), 0.0)
    query_grad = (query_grad * (HEAD**-0.5)).astype(BF16)
    key_grad = (dot_tn(score_low, q_stack) * (HEAD**-0.5)).astype(BF16)
    first_grad = (
        dot_nt(query_grad, mix_weight[:, 0:C])
        + dot_nt(key_grad, mix_weight[:, C : 2 * C])
        + dot_nt(value_grad, mix_weight[:, 2 * C : 3 * C])
    )
    moved = mid_grad + norm_backward(first_grad, hat1, inv1, gain1)

    moved_s[...] = moved
    for slot in range(4):
        base = PART * slot
        grid_s[slot, 0:CELLS, 0:C] = moved_s[base : base + CELLS, :]
        grid_s[slot, 0:CELLS, C : 2 * C] = moved_s[base + CELLS : base + PART, :]
        for tile in range(3):
            unpack_s[slot, CELLS * tile : CELLS * tile + CELLS, :] = grid_s[
                slot, 0:CELLS, tile * LANES : (tile + 1) * LANES
            ]
        back_s[slot] = unpack_s[slot, 0:64, :].astype(BF16)

    back_copies = []
    for slot in (3, 2, 1):
        copy = remote(
            back_s.at[slot], back_r.at[3 - slot], back_ss.at[slot], back_rs.at[slot], beside(lat, lon, slot // 2, slot % 2)
        )
        copy.start()
        back_copies.append((slot, copy))
    sends += [copy for _, copy in back_copies]

    lane = lax.broadcasted_iota(jnp.int32, (TOK, LANES), 1)
    small = jnp.zeros((C, LANES), F32)
    for left, right in (
        (moved, hot_s[...]),
        (first_grad * hat1, jnp.where(lane == KINDS, 1.0, 0.0)),
        (second_grad * hat2, jnp.where(lane == KINDS + 1, 1.0, 0.0)),
    ):
        for term in two_terms(left):
            small += dot_tn(term, right.astype(BF16))
    ge_s[...] = small
    extra = jnp.zeros((32, LANES), F32)
    for k in range(6):
        line = ge_s[pl.ds(k, 32, stride=6), :]
        extra += pltpu.roll(line, 18 * k, 1) if k else line
    extra_s[...] = extra

    grad_s[:, 0:C] = dot_tn(first_in, query_grad)
    grad_s[:, C : 2 * C] = dot_tn(first_in, key_grad)
    grad_s[:, 2 * C : 3 * C] = dot_tn(first_in, value_grad)
    grad_s[:, 3 * C : 4 * C] = dot_tn(context, mid_low)
    grad_s[:, 4 * C : 8 * C] = dot_tn(second_in, hidden_grad)
    spread = dot(hidden_low, spread_s[...]).astype(BF16)
    for part in range(4):
        grad_s[:, (8 + part) * C : (9 + part) * C] = dot_tn(spread[:, part * C : (part + 1) * C], upstream_low)
    for tile in range(TILES):
        for part in range(4):
            rows_s[tile // 9, part, pl.ds(tile % 9, 48, stride=9), :] = grad_s[
                48 * part : 48 * part + 48, tile * LANES : (tile + 1) * LANES
            ]
    sub64 = lax.broadcasted_iota(jnp.int32, (64, LANES), 0)

    def blocks(half, part):
        for block in range(ZLO):
            got = rows_s[half, part, 54 * block : 54 * block + 64, :]
            line = extra_s[pl.ds(part * ZLO + block, 1), :] * jnp.where(half == 0, 1.0, 0.0)
            got = jnp.where(sub64 < 54, got, jnp.where(sub64 == 54, line, 0.0)).astype(BF16)
            for quarter in range(4):
                grads[half, part, quarter, block] = got[16 * quarter : 16 * quarter + 16]

    core_copies = []
    for j in range(4):
        to = (y + 1 + j) & 3
        blocks(other, to)
        copy = remote(grads.at[other, to], core_r.at[to], core_ss.at[j], core_rs.at[j], at(x, y, z, other))
        copy.start()
        core_copies.append(copy)
    sends += core_copies
    plane_copies = {}
    for j in range(4):
        to_y = (y + 1 + j) & 3
        blocks(core, to_y)
        core_copies[j].wait_recv()
        for part in range(4):
            plane_s[to_y, part] = (grads[core, to_y, part].astype(F32) + core_r[to_y, part].astype(F32)).astype(BF16)
        for i in range(4):
            dx, dy = (i + 1) % 4, (j + 1) % 4
            d = dx * 4 + dy
            to_x = (x + dx) & 3
            if d == 0:
                plane_r[x * 4 + y] = plane_s[y, x]
                continue
            copy = remote(
                plane_s.at[to_y, to_x], plane_r.at[x * 4 + y], plane_ss.at[d], plane_rs.at[d], at(to_x, to_y, z, core)
            )
            copy.start()
            plane_copies[d] = copy
    sends += list(plane_copies.values())

    acc_s[...] = jnp.zeros((208, LANES), F32)
    for n in range(HEADS):
        dense_rows(dense_s, score_s[n * TOK : (n + 1) * TOK, :], n * DENSE)
    row32 = lax.broadcasted_iota(jnp.int32, (32, LANES), 0).astype(F32)
    row128 = lax.broadcasted_iota(jnp.int32, (LANES, LANES), 0).astype(F32)

    def scatter(step, carry):
        left, right = [], []
        start = pl.multiple_of(step * 16, 16)
        highs, lows = high_s[pl.ds(start, 16), :], low_s[pl.ds(start, 16), :]
        scores = [dense_s[pl.ds(pl.multiple_of(n * DENSE + start, 16), 16), :] for n in range(HEADS)]
        for row in range(16):
            chosen = row32 == highs[row : row + 1]
            right.append(jnp.where(row128 == lows[row : row + 1], 1.0, 0.0).astype(BF16))
            taken = [jnp.where(chosen, scores[n][row : row + 1], 0.0).astype(BF16) for n in range(HEADS)]
            left.append(jnp.concatenate(taken, axis=0))
        acc_s[0 : 32 * HEADS, :] += dot_nt(jnp.concatenate(left, axis=1), jnp.concatenate(right, axis=1))
        return carry

    lax.fori_loop(0, DENSE // 16, scatter, 0)
    sub16 = lax.broadcasted_iota(jnp.int32, (16, LANES), 0)
    for block in range(16):
        parts_s[block // 8, block % 8] = jnp.where(sub16 < 12, acc_s[12 * block : 12 * block + 16, :], 0.0)

    bcore = remote(parts_s.at[other], bcore_r, bcore_ss, bcore_rs, at(x, y, z, other))
    bcore.start()
    sends.append(bcore)
    bcore.wait_recv()
    for part in range(ZLO):
        bline_s[part] = parts_s[core, part] + bcore_r[part]
    bline_r[z_lo] = bline_s[z_lo]
    bline_copies = []
    for d in range(1, ZLO):
        to = (z_lo + d) & 7
        copy = remote(
            bline_s.at[to], bline_r.at[z_lo], bline_ss.at[d], bline_rs.at[d], at(x, y, z_hi * ZLO + to, core)
        )
        copy.start()
        bline_copies.append(copy)
    sends += bline_copies

    for copy in plane_copies.values():
        copy.wait_recv()
    for part in range(ZLO):
        block = plane_r[0, part].astype(F32)
        for source in range(1, 16):
            block = block + plane_r[source, part].astype(F32)
        line_s[part] = block.astype(BF16)
    line_r[z] = line_s[z_lo]
    line_copies = []
    for d in range(1, 16):
        to = (z + d) & 15
        copy = remote(line_s.at[to & 7], line_r.at[z], line_ss.at[d], line_rs.at[d], at(x, y, to, core))
        copy.start()
        line_copies.append(copy)
    sends += line_copies

    for copy in bline_copies:
        copy.wait_recv()
    part_sum = bline_r[0]
    for part in range(1, ZLO):
        part_sum = part_sum + bline_r[part]
    brow_r[y] = part_sum
    brow_copies = []
    for d in range(1, 4):
        to = (y + d) & 3
        copy = remote(brow_r.at[y], brow_r.at[y], brow_ss.at[d], brow_rs.at[d], at(x, to, z, core))
        copy.start()
        brow_copies.append(copy)
    sends += brow_copies

    for copy in brow_copies:
        copy.wait_recv()
    bias_part = (brow_r[0] + brow_r[1]) + (brow_r[2] + brow_r[3])
    ball[core, z_lo] = bias_part
    ball_copies = []
    for d in range(1, ZLO):
        to = (z_lo + d) & 7
        copy = remote(
            ball.at[core, z_lo], ball.at[core, z_lo], ball_ss.at[d], ball_rs.at[d], at(x, y, z_hi * ZLO + to, core)
        )
        copy.start()
        ball_copies.append(copy)
    sends += ball_copies

    for copy in line_copies:
        copy.wait_recv()
    piece = line_r[0].astype(F32)
    for source in range(1, 16):
        piece = piece + line_r[source].astype(F32)
    square = 0.5 * jnp.sum(piece * piece) + 0.25 * jnp.sum(bias_part * bias_part)
    mine = core * 4 + x
    share[mine, 0:16, :] = piece
    share[mine, 16:24, :] = jnp.full((8, LANES), square, F32)
    share_copies = []
    for dx, dcore in ((1, 0), (2, 0), (3, 0), (0, 1), (1, 1), (2, 1), (3, 1)):
        d = dcore * 4 + dx
        copy = remote(
            share.at[mine],
            share.at[mine],
            share_ss.at[d],
            share_rs.at[d],
            at((x + dx) & 3, y, z, core + dcore * (1 - 2 * core)),
        )
        copy.start()
        share_copies.append(copy)
    sends += share_copies

    for copy in share_copies:
        copy.wait_recv()
    square = share[0, 16:17, :]
    for source in range(1, 8):
        square = square + share[source, 16:17, :]
    squares_z[z] = square
    sz_copies = []
    for d in range(1, 16):
        to = (z + d) & 15
        copy = remote(squares_z.at[z], squares_z.at[z], sz_ss.at[d], sz_rs.at[d], at(x, y, to, core))
        copy.start()
        sz_copies.append(copy)
    sends += sz_copies
    for copy in ball_copies:
        copy.wait_recv()
    bpair = remote(ball.at[core], ball.at[core], bpair_ss, bpair_rs, at(x, y, z, other))
    bpair.start()
    sends.append(bpair)
    for source in range(8):
        dense_out[source] = share[source, 0:16, :]
    back_out[3] = back_s[0]
    for slot, copy in back_copies:
        copy.wait_recv()
        back_out[3 - slot] = back_r[3 - slot]
    for copy in sz_copies:
        copy.wait_recv()
    square = squares_z[0]
    for source in range(1, 16):
        square = square + squares_z[source]
    squares_y[y] = square
    sy_copies = []
    for d in range(1, 4):
        copy = remote(squares_y.at[y], squares_y.at[y], sy_ss.at[d], sy_rs.at[d], at(x, (y + d) & 3, z, core))
        copy.start()
        sy_copies.append(copy)
    sends += sy_copies
    bpair.wait_recv()
    bias_out[...] = ball[...]
    for copy in sy_copies:
        copy.wait_recv()
    total_out[...] = (squares_y[0] + squares_y[1]) + (squares_y[2] + squares_y[3])
    for copy in sends:
        copy.wait_send()


def main(*operands):
    token = np.arange(TOK)
    slot, level, cell = token // PART, (token % PART) // CELLS, token % CELLS
    row, col = 3 * (slot // 2) + cell // 6, 6 * (slot % 2) + cell % 6
    order = np.zeros((TOK, TOK), np.float32)
    order[token, (row * WIN_LON + col) * 2 + level] = 1.0
    operands = operands[:6] + (jnp.asarray(order, BF16),) + operands[6:]
    vmem = pl.BlockSpec(memory_space=pltpu.VMEM)
    dma = pltpu.SemaphoreType.DMA
    return pl.pallas_call(
        main_kernel,
        out_shape=(
            jax.ShapeDtypeStruct((8, 16, LANES), F32),
            jax.ShapeDtypeStruct((2, ZLO, 16, LANES), F32),
            jax.ShapeDtypeStruct((4, 64, LANES), BF16),
            jax.ShapeDtypeStruct((1, LANES), F32),
        ),
        in_specs=[vmem] * 13,
        out_specs=(vmem,) * 4,
        scratch_shapes=[
            pltpu.VMEM((4, 24, 2 * C), F32),
            pltpu.VMEM((4, 8, LANES), F32),
            pltpu.VMEM((4, 40, 2 * C), F32),
            pltpu.VMEM((4, SENT, LANES), F32),
            pltpu.VMEM((4, SENT, LANES), BF16),
            pltpu.VMEM((4, SENT, LANES), BF16),
            pltpu.VMEM((HEADS * 32, LANES), F32),
            pltpu.VMEM((HEADS * DENSE, LANES), F32),
            pltpu.VMEM((DENSE, LANES), F32),
            pltpu.VMEM((DENSE, LANES), F32),
            pltpu.VMEM((HEADS * TOK, TOK), F32),
            pltpu.VMEM((FF, FF), BF16),
            pltpu.VMEM((4, 40, 2 * C), F32),
            pltpu.VMEM((TOK, C), F32),
            pltpu.VMEM((TOK, C), F32),
            pltpu.VMEM((TOK, LANES), F32),
            pltpu.VMEM((C, LANES), F32),
            pltpu.VMEM((TOK, C), F32),
            pltpu.VMEM((4, SENT, LANES), F32),
            pltpu.VMEM((HEADS * TOK, TOK), F32),
            pltpu.VMEM((32, LANES), F32),
            pltpu.VMEM((4, 64, LANES), BF16),
            pltpu.VMEM((C, COLS), F32),
            pltpu.VMEM((2, 4, 448, LANES), F32),
            pltpu.VMEM((2, 4, 4, ZLO, 16, LANES), BF16),
            pltpu.VMEM((208, LANES), F32),
            pltpu.VMEM((2, ZLO, 16, LANES), F32),
            pltpu.VMEM((4, 4, ZLO, 16, LANES), BF16),
            pltpu.VMEM((4, 4, ZLO, 16, LANES), BF16),
            pltpu.VMEM((16, ZLO, 16, LANES), BF16),
            pltpu.VMEM((ZLO, 16, LANES), BF16),
            pltpu.VMEM((16, 16, LANES), BF16),
            pltpu.VMEM((8, 24, LANES), F32),
            pltpu.VMEM((ZLO, 16, LANES), F32),
            pltpu.VMEM((ZLO, 16, LANES), F32),
            pltpu.VMEM((ZLO, 16, LANES), F32),
            pltpu.VMEM((4, 16, LANES), F32),
            pltpu.VMEM((2, ZLO, 16, LANES), F32),
            pltpu.VMEM((4, 64, LANES), BF16),
            pltpu.VMEM((16, 1, LANES), F32),
            pltpu.VMEM((4, 1, LANES), F32),
            dma((4,)), dma((4,)),
            dma((4,)), dma((4,)),
            dma((16,)), dma((16,)),
            dma((16,)), dma((16,)),
            dma((8,)), dma((8,)),
            dma, dma,
            dma((8,)), dma((8,)),
            dma((4,)), dma((4,)),
            dma((8,)), dma((8,)),
            dma, dma,
            dma((4,)), dma((4,)),
            dma((16,)), dma((16,)),
            dma((4,)), dma((4,)),
        ],
        compiler_params=pltpu.CompilerParams(collective_id=0, has_side_effects=True, vmem_limit_bytes=VMEM_LIMIT),
        name="window_and_sums",
    )(*operands)


def output_kernel(
    dense_ref, bias_ref, back_ref, total_ref,
    token_ref, mix_ref, out_ref, up_ref, down_ref, gain_ref, embed_ref, table_ref,
    dense_s, flat_s, bias_s, back_s, token_s,
):
    count = C * COLS + (KINDS + 2) * C + LAT * HEADS * PAIRS
    factor = lax.rsqrt(total_ref[...] / count + RMS_EPS)
    odd = lax.axis_index("lon") % 2 == 1
    for part in range(8):
        dense_s[part // 4, 16 * (part % 4) : 16 * (part % 4) + 16, :] = dense_ref[part] * factor
    for tile in range(TILES):
        half, t = tile // 9, tile % 9
        even_rows = dense_s[half, pl.ds(t, 3, stride=9), :]
        odd_rows = dense_s[half, pl.ds(27 + t, 3, stride=9), :]
        flat_s[0:3, tile * LANES : (tile + 1) * LANES] = jnp.where(odd, odd_rows, even_rows)
    flat = flat_s[0:3, :]
    mix_ref[...] = flat[:, 0 : 3 * C]
    out_ref[...] = flat[:, 3 * C : 4 * C]
    up_ref[...] = flat[:, 4 * C : 8 * C]
    for row in range(3):
        for part in range(4):
            down_ref[4 * row + part : 4 * row + part + 1, :] = flat[row : row + 1, (8 + part) * C : (9 + part) * C]
    extra = dense_s[0, 54:55, :]
    lane = lax.broadcasted_iota(jnp.int32, (24, LANES), 1)
    sub = lax.broadcasted_iota(jnp.int32, (24, LANES), 0)
    small = jnp.zeros((24, LANES), F32)
    wide = jnp.zeros((8, LANES), F32)
    sub8 = lax.broadcasted_iota(jnp.int32, (8, LANES), 0)
    line8 = jnp.broadcast_to(extra, (8, LANES))
    for row in range(3):
        turned = jnp.where(odd, pltpu.roll(line8, LANES - 18 * (3 + row), 1), pltpu.roll(line8, (LANES - 18 * row) % LANES, 1))
        wide = jnp.where(sub8 == row, turned, wide)
        start = jnp.where(odd, 18 * (3 + row), 18 * row)
        column = jnp.sum(jnp.where(lane == sub + start, extra, 0.0), axis=1, keepdims=True)
        small = small + jnp.where(lane == row, column, 0.0)
    embed_ref[...] = wide[0:3, 0:KINDS]
    gain_ref[...] = small[KINDS : KINDS + 2, 0:3]
    for block in range(16):
        bias_s[12 * block : 12 * block + 12, :] = bias_ref[block // 8, block % 8, 0:12, :] * factor
    for row in range(HI):
        width = min(LANES, PAIRS - row * LANES)
        line = bias_s[pl.ds(row, HEADS, stride=32), :][:, 0:width]
        for head in range(HEADS):
            table_ref[head, :, row * LANES : row * LANES + width] = line[head : head + 1]
    for quarter in range(4):
        packed = back_ref[quarter].astype(F32)
        for tile in range(3):
            back_s[quarter, 0:CELLS, tile * LANES : (tile + 1) * LANES] = packed[CELLS * tile : CELLS * tile + CELLS]
        for i in range(3):
            row, half = 3 * (quarter // 2) + i, quarter % 2
            token_s[row, 6 * half : 6 * half + 6, :] = back_s[quarter, 6 * i : 6 * i + 6, :]
    for row in range(WIN_LAT):
        token_ref[row] = token_s[row, 0:WIN_LON, :].astype(BF16)


def outputs(dense, bias, back, total):
    vmem = pl.BlockSpec(memory_space=pltpu.VMEM)
    return pl.pallas_call(
        output_kernel,
        out_shape=(
            jax.ShapeDtypeStruct((WIN_LAT, WIN_LON, 2 * C), BF16),
            jax.ShapeDtypeStruct((3, 3 * C), F32),
            jax.ShapeDtypeStruct((3, C), F32),
            jax.ShapeDtypeStruct((3, FF), F32),
            jax.ShapeDtypeStruct((12, C), F32),
            jax.ShapeDtypeStruct((2, 3), F32),
            jax.ShapeDtypeStruct((3, KINDS), F32),
            jax.ShapeDtypeStruct((HEADS, 1, PAIRS), F32),
        ),
        in_specs=[vmem] * 4,
        out_specs=(vmem,) * 8,
        scratch_shapes=[
            pltpu.VMEM((2, 64, LANES), F32),
            pltpu.VMEM((8, COLS), F32),
            pltpu.VMEM((HEADS * 32, LANES), F32),
            pltpu.VMEM((4, 32, 2 * C), F32),
            pltpu.VMEM((WIN_LAT, 16, 2 * C), F32),
        ],
        compiler_params=pltpu.CompilerParams(vmem_limit_bytes=VMEM_LIMIT),
        name="scaled_outputs",
    )(dense, bias, back, total)


def shards(
    tokens, kinds, kind_embed, pair_index, bias_table, attn_gain, mlp_gain,
    mix_weight, out_weight, up_weight, down_weight, cotangent,
):
    sums = main(
        tokens, kinds.transpose(0, 2, 1), kind_embed, cotangent, pair_index, bias_table.transpose(1, 0, 2),
        attn_gain.reshape(1, C), mlp_gain.reshape(1, C), mix_weight, out_weight, up_weight, down_weight.T,
    )
    token, mix, out, up, down, gain, embed, table = outputs(*sums)
    return token, mix, out, up, down, gain, embed.T, table.transpose(1, 0, 2)


def solution(mesh):
    return jax.shard_map(
        shards,
        mesh=mesh,
        in_specs=(
            P("lat", "lon", None),
            P("lat", "lon", None),
            P(),
            P(),
            P("lat", None, None),
            P(),
            P(),
            P(),
            P(),
            P(),
            P(),
            P("lat", "lon", None),
        ),
        out_specs=(
            P("lat", "lon", None),
            P("lon", None),
            P("lon", None),
            P("lon", None),
            P("lon", None),
            P(None, "lon"),
            P(None, "lon"),
            P("lat", None, None),
        ),
        check_vma=False,
    )
```

time: 96.6 us -> 69 us (0.71); the launches traced: 95.4 us -> 68.8 us
  Pallas kernels: 94.8 us -> 68.2 us
    pallas_call x3 -> x1, Pallas kernels: 93 us -> 66.4 us  [main(): pl.pallas_call(main_kernel, out_shape=(jax.ShapeDtypeStruct((8, 16, LANES...]
where the time goes in v3:
time: 69 us; the launch traced here: 68.8 us
  Pallas kernels  68.2 us (99%)
    pallas_call x1, Pallas kernels, main(): pl.pallas_call(main_kernel, out_shape=(jax.ShapeDtypeStruct((8, 16, LANES...  66.4 us
    pallas_call x1, Pallas kernels, outputs(): pl.pallas_call(output_kernel, out_shape=(jax.ShapeDtypeStruct((WIN_LAT, W...  1.76 us

profile of v3, /device:TPU:1, one launch (start us, length us, event | category | flops | bytes accessed | tf_op | source)
XLA Modules:
  0.0 68.8 jit_solution(14040323707726411862)
XLA Ops:
  0.6 66.4 %window_and_sums.1 = (f32[8,16,128]{2,1,0:T(8,128)}, f32[2,8,16,128]{3,2,1,0:T(8,128)}, bf16[4,64,128]{2,1,0:T(8,128)(2,1)}, f32[1,128]{1,0:T(1,128)}) custom-call(bf16[6,12,384]{2,1,0:T(8,128)(2,1)} %tok_ref.1, s32[6,2,12]{2,1,0:T(2,128)} %bitcast.9, bf16[16,192]{1,0:T(8,128)(2,1)} %embed_ref.1, bf16[6,12,384]{2,1,0:T(8,128)(2,1)} %cot_ref.1, ...), custom_call_target="tpu_custom_call" | custom-call | tf_op jit(solution)/shard_map/window_and_sums/pallas_call | solution.py:546
  67.1 1.8 %scaled_outputs.1 = (bf16[6,12,384]{2,1,0:T(8,128)(2,1)}, f32[3,576]{1,0:T(4,128)}, f32[3,192]{1,0:T(4,128)}, f32[3,768]{1,0:T(4,128)}, f32[12,192]{1,0:T(8,128)...) custom-call(f32[8,16,128]{2,1,0:T(8,128)} %get-tuple-element.20.dense_ref, ...), custom_call_target="tpu_custom_call" | custom-call | tf_op jit(solution)/shard_map/scaled_outputs/pallas_call | solution.py:674

commit v4 on v3

--- a/solution.py
+++ b/solution.py
@@ -34,8 +34,7 @@
 VMEM_LIMIT = 56 * 1024 * 1024
 
 
-def place():
-    lon, lat = lax.axis_index("lon"), lax.axis_index("lat")
+def coords(lat, lon):
     return lat >> 1, lon >> 4, ((lat & 1) << 3) + ((lon >> 1) & 7), lon & 1
 
 
@@ -97,19 +96,21 @@
 
 
 def main_kernel(
+    tok_in, kind_in, embed_in, cot_in, index_in, table_in, order_in,
+    gain1_in, gain2_in, mix_in, outw_in, up_in, down_in,
+    dense_out, bias_out, back_out, total_out,
     tok_ref, kind_ref, embed_ref, cot_ref, index_ref, table_ref, order_ref,
     gain1_ref, gain2_ref, mix_ref, outw_ref, up_ref, down_ref,
-    dense_out, bias_out, back_out, total_out,
     tok_s, kind_s, flat_s, pack_s, send, recv, table_s, dense_s, high_s, low_s, bias_s, spread_s,
     grid_s, x_s, g_s, hot_s, ge_s, moved_s, unpack_s, score_s, extra_s, back_s,
     grad_s, rows_s, grads, acc_s, parts_s,
     core_r, plane_s, plane_r, line_s, line_r, share, bcore_r, bline_s, bline_r, brow_r, ball, back_r, squares_z, squares_y,
-    halo_ss, halo_rs,
+    relay, in_sems, relay_ss, relay_rs, halo_ss, halo_rs,
     core_ss, core_rs, plane_ss, plane_rs, line_ss, line_rs, share_ss, share_rs, bcore_ss, bcore_rs, bline_ss, bline_rs,
     brow_ss, brow_rs, ball_ss, ball_rs, bpair_ss, bpair_rs, back_ss, back_rs, sz_ss, sz_rs, sy_ss, sy_rs,
 ):
     lon, lat = lax.axis_index("lon"), lax.axis_index("lat")
-    x, y, z, core = place()
+    x, y, z, core = coords(lat, lon)
     z_lo, z_hi = z & 7, z >> 3
     other = 1 - core
 
@@ -118,8 +119,31 @@
             src_ref=src, dst_ref=dst, send_sem=send_sem, recv_sem=recv_sem, device_id=target, device_id_type=MESH
         )
 
+    sources = (
+        tok_in, kind_in, embed_in, cot_in, index_in, table_in, order_in,
+        gain1_in, gain2_in, mix_in, outw_in, up_in, down_in,
+    )
+    targets = (
+        tok_ref, kind_ref, embed_ref, cot_ref, index_ref, table_ref, order_ref,
+        gain1_ref, gain2_ref, mix_ref, outw_ref, up_ref, down_ref,
+    )
+    fetches = [pltpu.make_async_copy(s, t, in_sems.at[i]) for i, (s, t) in enumerate(zip(sources, targets))]
+    for fetch in fetches[:4]:
+        fetch.start()
+
+    below, above = at(x, y, z - 4 & 15, core), at(x, y, z + 4 & 15, core)
+    relay_to = {2: below, 3: above}
+    relayed_to = {
+        2: beside(above["lat"], above["lon"], -1, 0),
+        3: beside(below["lat"], below["lon"], -1, -1),
+    }
+    south = beside(lat, lon, 1, 0)
+    south_x, south_y, south_z, south_c = coords(south["lat"], south["lon"])
+    corner = beside(lat, lon, 1, 1)
+    corner_x, corner_y, corner_z, corner_c = coords(corner["lat"], corner["lon"])
     barrier = pltpu.get_barrier_semaphore()
-    peers = []
+    peers = [relayed_to[2], relayed_to[3]]
+    peers += [at(south_x, south_y, south_z - 4 & 15, south_c), at(corner_x, corner_y, corner_z + 4 & 15, corner_c)]
     for dr, dc in ((1, 0), (0, 1), (1, 1)):
         peers += [beside(lat, lon, -dr, -dc), beside(lat, lon, dr, dc)]
     peers += [at(x, y, (z + d) & 15, core) for d in range(1, 16)]
@@ -128,6 +152,10 @@
     for peer in peers:
         pl.semaphore_signal(barrier, inc=1, device_id=peer, device_id_type=MESH)
 
+    for fetch in fetches[4:]:
+        fetch.start()
+    for fetch in fetches[:4]:
+        fetch.wait()
     embed = embed_ref[...].astype(F32)
     blank = jnp.zeros((KINDS, C), F32)
     wide = jnp.concatenate(
@@ -159,6 +187,8 @@
         pack_s[quarter, FLAT:SENT, :] = jnp.zeros((4, LANES), F32)
         pack_s[quarter, FLAT : FLAT + 1, :] = kinds[0:1] + pltpu.roll(kinds, CELLS, 1)[1:2]
         send[quarter] = pack_s[quarter].astype(BF16)
+    for fetch in fetches[4:7]:
+        fetch.wait()
     order = order_ref[...]
     index = index_ref[...]
     high = (index // LANES).astype(F32).astype(BF16)
@@ -181,14 +211,13 @@
         spread_s[LANES * block : LANES * (block + 1), :] = jnp.where(place_at == unit, 1.0, 0.0).astype(BF16)
 
     pl.semaphore_wait(barrier, len(peers))
-    halo_copies = []
-    for slot in (3, 2, 1):
-        copy = remote(
-            send.at[3 - slot], recv.at[slot], halo_ss.at[slot], halo_rs.at[slot], beside(lat, lon, -(slot // 2), -(slot % 2))
-        )
-        copy.start()
-        halo_copies.append(copy)
-    sends = list(halo_copies)
+    relay_copies = []
+    for slot in (2, 3):
+        copy = remote(send.at[3 - slot], relay.at[slot - 2], relay_ss.at[slot - 2], relay_rs.at[slot - 2], relay_to[slot])
+        copy.start()
+        relay_copies.append(copy)
+    direct = remote(send.at[2], recv.at[1], halo_ss.at[1], halo_rs.at[1], beside(lat, lon, 0, -1))
+    direct.start()
 
     def gather(step, carry):
         start = pl.multiple_of(step * 16, 16)
@@ -205,7 +234,16 @@
             dense_s[pl.ds(pl.multiple_of(head * DENSE + start, 16), 16), :] = totals[head]
         return carry
 
-    lax.fori_loop(0, DENSE // 16, gather, 0)
+    lax.fori_loop(0, 5, gather, 0)
+    halo_copies = []
+    for slot, arrived in zip((2, 3), relay_copies):
+        arrived.wait_recv()
+        copy = remote(relay.at[slot - 2], recv.at[slot], halo_ss.at[slot], halo_rs.at[slot], relayed_to[slot])
+        copy.start()
+        halo_copies.append(copy)
+    halo_copies.append(direct)
+    sends = relay_copies + halo_copies
+    lax.fori_loop(5, DENSE // 16, gather, 0)
     for head in range(HEADS):
         base = head * DENSE
         bias_s[head * TOK : head * TOK + TOK, 0:LANES] = dense_s[base : base + TOK, :]
@@ -234,6 +272,8 @@
         kind_col = jnp.sum(jnp.where(lane36 == sub36, kind_row, 0.0), axis=1, keepdims=True)
         hot_s[base : base + PART, :] = jnp.where(lane36.astype(F32) == kind_col, 1.0, 0.0)
 
+    for fetch in fetches[7:]:
+        fetch.wait()
     gain1, gain2 = gain1_ref[...], gain2_ref[...]
     mix_weight, out_weight = mix_ref[...], outw_ref[...]
     up_weight, down_weight = up_ref[...], down_ref[...]
@@ -255,7 +295,7 @@
     group_k = (lax.broadcasted_iota(jnp.int32, (HEADS * TOK, TOK), 1) >= 72).astype(F32)
     allowed = jnp.abs(group_q - group_k) * jnp.where(last, 1.0, 0.0) < 0.5
     expon = jnp.where(allowed, jnp.exp(scores), 0.0)
-    attend = expon / jnp.sum(expon, axis=-1, keepdims=True)
+    attend = expon * (1.0 / jnp.sum(expon, axis=-1, keepdims=True))
     attend_low = attend.astype(BF16)
     context = jnp.zeros((TOK, C), F32)
     for n in range(HEADS):
@@ -410,7 +450,7 @@
     sends.append(bcore)
     bcore.wait_recv()
     for part in range(ZLO):
-        bline_s[part] = parts_s[core, part] + bcore_r[part]
+        bline_s[part] = (parts_s[core, part] + bcore_r[part]).astype(BF16)
     bline_r[z_lo] = bline_s[z_lo]
     bline_copies = []
     for d in range(1, ZLO):
@@ -440,9 +480,9 @@
 
     for copy in bline_copies:
         copy.wait_recv()
-    part_sum = bline_r[0]
+    part_sum = bline_r[0].astype(F32)
     for part in range(1, ZLO):
-        part_sum = part_sum + bline_r[part]
+        part_sum = part_sum + bline_r[part].astype(F32)
     brow_r[y] = part_sum
     brow_copies = []
     for d in range(1, 4):
@@ -551,9 +591,9 @@
             jax.ShapeDtypeStruct((4, 64, LANES), BF16),
             jax.ShapeDtypeStruct((1, LANES), F32),
         ),
-        in_specs=[vmem] * 13,
+        in_specs=[pl.BlockSpec(memory_space=pl.ANY)] * 13,
         out_specs=(vmem,) * 4,
-        scratch_shapes=[
+        scratch_shapes=[pltpu.VMEM(v.shape, v.dtype) for v in operands] + [
             pltpu.VMEM((4, 24, 2 * C), F32),
             pltpu.VMEM((4, 8, LANES), F32),
             pltpu.VMEM((4, 40, 2 * C), F32),
@@ -588,13 +628,15 @@
             pltpu.VMEM((16, 16, LANES), BF16),
             pltpu.VMEM((8, 24, LANES), F32),
             pltpu.VMEM((ZLO, 16, LANES), F32),
-            pltpu.VMEM((ZLO, 16, LANES), F32),
-            pltpu.VMEM((ZLO, 16, LANES), F32),
+            pltpu.VMEM((ZLO, 16, LANES), BF16),
+            pltpu.VMEM((ZLO, 16, LANES), BF16),
             pltpu.VMEM((4, 16, LANES), F32),
             pltpu.VMEM((2, ZLO, 16, LANES), F32),
             pltpu.VMEM((4, 64, LANES), BF16),
             pltpu.VMEM((16, 1, LANES), F32),
             pltpu.VMEM((4, 1, LANES), F32),
+            pltpu.VMEM((2, SENT, LANES), BF16),
+            dma((13,)), dma((2,)), dma((2,)),
             dma((4,)), dma((4,)),
             dma((4,)), dma((4,)),
             dma((16,)), dma((16,)),

time: 69 us -> 69.4 us (level)
  no operation moved by 1% of the time
where the time goes in v4:
time: 69.4 us; the launch traced here: 69.3 us
  Pallas kernels  68.6 us (99%)
    pallas_call x1, Pallas kernels, main(): pl.pallas_call(main_kernel, out_shape=(jax.ShapeDtypeStruct((8, 16, LANES...  66.8 us
    pallas_call x1, Pallas kernels, outputs(): pl.pallas_call(output_kernel, out_shape=(jax.ShapeDtypeStruct((WIN_LAT, W...  1.76 us

profile of v4, /device:TPU:1, one launch (start us, length us, event | category | flops | bytes accessed | tf_op | source)
XLA Modules:
  0.0 69.3 jit_solution(2296118615091026626)
XLA Ops:
  0.6 66.8 %window_and_sums.1 = (f32[8,16,128]{2,1,0:T(8,128)}, f32[2,8,16,128]{3,2,1,0:T(8,128)}, bf16[4,64,128]{2,1,0:T(8,128)(2,1)}, f32[1,128]{1,0:T(1,128)}) custom-call(bf16[6,12,384]{2,1,0:T(8,128)(2,1)} %tok_in.1, s32[6,2,12]{2,1,0:T(2,128)} %bitcast.9, bf16[16,192]{1,0:T(8,128)(2,1)} %embed_in.1, bf16[6,12,384]{2,1,0:T(8,128)(2,1)} %cot_in.1, ...), custom_call_target="tpu_custom_call" | custom-call | tf_op jit(solution)/shard_map/window_and_sums/pallas_call | solution.py:586
  67.5 1.8 %scaled_outputs.1 = (bf16[6,12,384]{2,1,0:T(8,128)(2,1)}, f32[3,576]{1,0:T(4,128)}, f32[3,192]{1,0:T(4,128)}, f32[3,768]{1,0:T(4,128)}, f32[12,192]{1,0:T(8,128)...) custom-call(f32[8,16,128]{2,1,0:T(8,128)} %get-tuple-element.20.dense_ref, ...), custom_call_target="tpu_custom_call" | custom-call | tf_op jit(solution)/shard_map/scaled_outputs/pallas_call | solution.py:716

commit v5 on v4

--- a/solution.py
+++ b/solution.py
@@ -105,7 +105,7 @@
     grid_s, x_s, g_s, hot_s, ge_s, moved_s, unpack_s, score_s, extra_s, back_s,
     grad_s, rows_s, grads, acc_s, parts_s,
     core_r, plane_s, plane_r, line_s, line_r, share, bcore_r, bline_s, bline_r, brow_r, ball, back_r, squares_z, squares_y,
-    relay, in_sems, relay_ss, relay_rs, halo_ss, halo_rs,
+    in_sems, halo_ss, halo_rs,
     core_ss, core_rs, plane_ss, plane_rs, line_ss, line_rs, share_ss, share_rs, bcore_ss, bcore_rs, bline_ss, bline_rs,
     brow_ss, brow_rs, ball_ss, ball_rs, bpair_ss, bpair_rs, back_ss, back_rs, sz_ss, sz_rs, sy_ss, sy_rs,
 ):
@@ -131,24 +131,13 @@
     for fetch in fetches[:4]:
         fetch.start()
 
-    below, above = at(x, y, z - 4 & 15, core), at(x, y, z + 4 & 15, core)
-    relay_to = {2: below, 3: above}
-    relayed_to = {
-        2: beside(above["lat"], above["lon"], -1, 0),
-        3: beside(below["lat"], below["lon"], -1, -1),
-    }
-    south = beside(lat, lon, 1, 0)
-    south_x, south_y, south_z, south_c = coords(south["lat"], south["lon"])
-    corner = beside(lat, lon, 1, 1)
-    corner_x, corner_y, corner_z, corner_c = coords(corner["lat"], corner["lon"])
     barrier = pltpu.get_barrier_semaphore()
-    peers = [relayed_to[2], relayed_to[3]]
-    peers += [at(south_x, south_y, south_z - 4 & 15, south_c), at(corner_x, corner_y, corner_z + 4 & 15, corner_c)]
+    peers = []
     for dr, dc in ((1, 0), (0, 1), (1, 1)):
         peers += [beside(lat, lon, -dr, -dc), beside(lat, lon, dr, dc)]
     peers += [at(x, y, (z + d) & 15, core) for d in range(1, 16)]
     peers += [at((x + d // 4) & 3, (y + d % 4) & 3, z, core) for d in range(1, 16)]
-    peers += [at((x + d) & 3, y, z, other) for d in range(4)]
+    peers += [at((x + d // 4) & 3, (y + d % 4) & 3, z, other) for d in range(16)]
     for peer in peers:
         pl.semaphore_signal(barrier, inc=1, device_id=peer, device_id_type=MESH)
 
@@ -187,6 +176,16 @@
         pack_s[quarter, FLAT:SENT, :] = jnp.zeros((4, LANES), F32)
         pack_s[quarter, FLAT : FLAT + 1, :] = kinds[0:1] + pltpu.roll(kinds, CELLS, 1)[1:2]
         send[quarter] = pack_s[quarter].astype(BF16)
+    pl.semaphore_wait(barrier, len(peers))
+    halo_copies = []
+    for slot in (3, 2, 1):
+        copy = remote(
+            send.at[3 - slot], recv.at[slot], halo_ss.at[slot], halo_rs.at[slot], beside(lat, lon, -(slot // 2), -(slot % 2))
+        )
+        copy.start()
+        halo_copies.append(copy)
+    sends = list(halo_copies)
+
     for fetch in fetches[4:7]:
         fetch.wait()
     order = order_ref[...]
@@ -210,15 +209,6 @@
         place_at = (lax.broadcasted_iota(jnp.int32, (LANES, FF), 0) + LANES * block).astype(F32)
         spread_s[LANES * block : LANES * (block + 1), :] = jnp.where(place_at == unit, 1.0, 0.0).astype(BF16)
 
-    pl.semaphore_wait(barrier, len(peers))
-    relay_copies = []
-    for slot in (2, 3):
-        copy = remote(send.at[3 - slot], relay.at[slot - 2], relay_ss.at[slot - 2], relay_rs.at[slot - 2], relay_to[slot])
-        copy.start()
-        relay_copies.append(copy)
-    direct = remote(send.at[2], recv.at[1], halo_ss.at[1], halo_rs.at[1], beside(lat, lon, 0, -1))
-    direct.start()
-
     def gather(step, carry):
         start = pl.multiple_of(step * 16, 16)
         lows = low_s[pl.ds(start, 16), :].astype(jnp.int32)
@@ -234,16 +224,7 @@
             dense_s[pl.ds(pl.multiple_of(head * DENSE + start, 16), 16), :] = totals[head]
         return carry
 
-    lax.fori_loop(0, 5, gather, 0)
-    halo_copies = []
-    for slot, arrived in zip((2, 3), relay_copies):
-        arrived.wait_recv()
-        copy = remote(relay.at[slot - 2], recv.at[slot], halo_ss.at[slot], halo_rs.at[slot], relayed_to[slot])
-        copy.start()
-        halo_copies.append(copy)
-    halo_copies.append(direct)
-    sends = relay_copies + halo_copies
-    lax.fori_loop(5, DENSE // 16, gather, 0)
+    lax.fori_loop(0, DENSE // 16, gather, 0)
     for head in range(HEADS):
         base = head * DENSE
         bias_s[head * TOK : head * TOK + TOK, 0:LANES] = dense_s[base : base + TOK, :]
@@ -333,26 +314,6 @@
     )
     moved = mid_grad + norm_backward(first_grad, hat1, inv1, gain1)
 
-    moved_s[...] = moved
-    for slot in range(4):
-        base = PART * slot
-        grid_s[slot, 0:CELLS, 0:C] = moved_s[base : base + CELLS, :]
-        grid_s[slot, 0:CELLS, C : 2 * C] = moved_s[base + CELLS : base + PART, :]
-        for tile in range(3):
-            unpack_s[slot, CELLS * tile : CELLS * tile + CELLS, :] = grid_s[
-                slot, 0:CELLS, tile * LANES : (tile + 1) * LANES
-            ]
-        back_s[slot] = unpack_s[slot, 0:64, :].astype(BF16)
-
-    back_copies = []
-    for slot in (3, 2, 1):
-        copy = remote(
-            back_s.at[slot], back_r.at[3 - slot], back_ss.at[slot], back_rs.at[slot], beside(lat, lon, slot // 2, slot % 2)
-        )
-        copy.start()
-        back_copies.append((slot, copy))
-    sends += [copy for _, copy in back_copies]
-
     lane = lax.broadcasted_iota(jnp.int32, (TOK, LANES), 1)
     small = jnp.zeros((C, LANES), F32)
     for left, right in (
@@ -400,6 +361,26 @@
         copy.start()
         core_copies.append(copy)
     sends += core_copies
+    moved_s[...] = moved
+    for slot in range(4):
+        base = PART * slot
+        grid_s[slot, 0:CELLS, 0:C] = moved_s[base : base + CELLS, :]
+        grid_s[slot, 0:CELLS, C : 2 * C] = moved_s[base + CELLS : base + PART, :]
+        for tile in range(3):
+            unpack_s[slot, CELLS * tile : CELLS * tile + CELLS, :] = grid_s[
+                slot, 0:CELLS, tile * LANES : (tile + 1) * LANES
+            ]
+        back_s[slot] = unpack_s[slot, 0:64, :].astype(BF16)
+
+    back_copies = []
+    for slot in (3, 2, 1):
+        copy = remote(
+            back_s.at[slot], back_r.at[3 - slot], back_ss.at[slot], back_rs.at[slot], beside(lat, lon, slot // 2, slot % 2)
+        )
+        copy.start()
+        back_copies.append((slot, copy))
+    sends += [copy for _, copy in back_copies]
+
     plane_copies = {}
     for j in range(4):
         to_y = (y + 1 + j) & 3
@@ -424,8 +405,12 @@
     acc_s[...] = jnp.zeros((208, LANES), F32)
     for n in range(HEADS):
         dense_rows(dense_s, score_s[n * TOK : (n + 1) * TOK, :], n * DENSE)
-    row32 = lax.broadcasted_iota(jnp.int32, (32, LANES), 0).astype(F32)
-    row128 = lax.broadcasted_iota(jnp.int32, (LANES, LANES), 0).astype(F32)
+    row32 = lax.broadcasted_iota(jnp.int32, (32, LANES), 0).astype(F32).astype(BF16)
+    row128 = lax.broadcasted_iota(jnp.int32, (LANES, LANES), 0).astype(F32).astype(BF16)
+    zero, one = jnp.zeros((), BF16), jnp.ones((), BF16)
+
+    def low_rows(line, count):
+        return jnp.concatenate([jnp.broadcast_to(line, (16, LANES)).astype(BF16)] * (count // 16), axis=0)
 
     def scatter(step, carry):
         left, right = [], []
@@ -433,10 +418,11 @@
         highs, lows = high_s[pl.ds(start, 16), :], low_s[pl.ds(start, 16), :]
         scores = [dense_s[pl.ds(pl.multiple_of(n * DENSE + start, 16), 16), :] for n in range(HEADS)]
         for row in range(16):
-            chosen = row32 == highs[row : row + 1]
-            right.append(jnp.where(row128 == lows[row : row + 1], 1.0, 0.0).astype(BF16))
-            taken = [jnp.where(chosen, scores[n][row : row + 1], 0.0).astype(BF16) for n in range(HEADS)]
-            left.append(jnp.concatenate(taken, axis=0))
+            chosen = row32 == low_rows(highs[row : row + 1], 32)
+            right.append(jnp.where(row128 == low_rows(lows[row : row + 1], LANES), one, zero))
+            left.append(
+                jnp.concatenate([jnp.where(chosen, low_rows(scores[n][row : row + 1], 32), zero) for n in range(HEADS)], axis=0)
+            )
         acc_s[0 : 32 * HEADS, :] += dot_nt(jnp.concatenate(left, axis=1), jnp.concatenate(right, axis=1))
         return carry
 
@@ -495,26 +481,22 @@
     for copy in brow_copies:
         copy.wait_recv()
     bias_part = (brow_r[0] + brow_r[1]) + (brow_r[2] + brow_r[3])
-    ball[core, z_lo] = bias_part
-    ball_copies = []
-    for d in range(1, ZLO):
-        to = (z_lo + d) & 7
-        copy = remote(
-            ball.at[core, z_lo], ball.at[core, z_lo], ball_ss.at[d], ball_rs.at[d], at(x, y, z_hi * ZLO + to, core)
-        )
-        copy.start()
-        ball_copies.append(copy)
-    sends += ball_copies
-
     for copy in line_copies:
         copy.wait_recv()
     piece = line_r[0].astype(F32)
     for source in range(1, 16):
         piece = piece + line_r[source].astype(F32)
     square = 0.5 * jnp.sum(piece * piece) + 0.25 * jnp.sum(bias_part * bias_part)
+    squares_z[z] = jnp.full((1, LANES), square, F32)
+    sz_copies = []
+    for d in range(1, 16):
+        to = (z + d) & 15
+        copy = remote(squares_z.at[z], squares_z.at[z], sz_ss.at[d], sz_rs.at[d], at(x, y, to, core))
+        copy.start()
+        sz_copies.append(copy)
+    sends += sz_copies
     mine = core * 4 + x
-    share[mine, 0:16, :] = piece
-    share[mine, 16:24, :] = jnp.full((8, LANES), square, F32)
+    share[mine] = piece
     share_copies = []
     for dx, dcore in ((1, 0), (2, 0), (3, 0), (0, 1), (1, 1), (2, 1), (3, 1)):
         d = dcore * 4 + dx
@@ -528,48 +510,51 @@
         copy.start()
         share_copies.append(copy)
     sends += share_copies
-
-    for copy in share_copies:
-        copy.wait_recv()
-    square = share[0, 16:17, :]
-    for source in range(1, 8):
-        square = square + share[source, 16:17, :]
-    squares_z[z] = square
-    sz_copies = []
-    for d in range(1, 16):
-        to = (z + d) & 15
-        copy = remote(squares_z.at[z], squares_z.at[z], sz_ss.at[d], sz_rs.at[d], at(x, y, to, core))
-        copy.start()
-        sz_copies.append(copy)
-    sends += sz_copies
+    ball[core, z_lo] = bias_part
+    ball_copies = []
+    for d in range(1, ZLO):
+        to = (z_lo + d) & 7
+        copy = remote(
+            ball.at[core, z_lo], ball.at[core, z_lo], ball_ss.at[d], ball_rs.at[d], at(x, y, z_hi * ZLO + to, core)
+        )
+        copy.start()
+        ball_copies.append(copy)
+    sends += ball_copies
+
+    for copy in sz_copies:
+        copy.wait_recv()
+    square = squares_z[0]
+    for source in range(1, 16):
+        square = square + squares_z[source]
+    spot = core * 16 + x * 4 + y
+    squares_y[spot] = square
+    sy_copies = []
+    for d in range(1, 32):
+        target = at((x + (d >> 2 & 3)) & 3, (y + (d & 3)) & 3, z, core + (d >> 4) * (1 - 2 * core))
+        copy = remote(squares_y.at[spot], squares_y.at[spot], sy_ss.at[d], sy_rs.at[d], target)
+        copy.start()
+        sy_copies.append(copy)
+    sends += sy_copies
     for copy in ball_copies:
         copy.wait_recv()
     bpair = remote(ball.at[core], ball.at[core], bpair_ss, bpair_rs, at(x, y, z, other))
     bpair.start()
     sends.append(bpair)
-    for source in range(8):
-        dense_out[source] = share[source, 0:16, :]
+    for copy in share_copies:
+        copy.wait_recv()
+    dense_out[...] = share[...]
     back_out[3] = back_s[0]
     for slot, copy in back_copies:
         copy.wait_recv()
         back_out[3 - slot] = back_r[3 - slot]
-    for copy in sz_copies:
-        copy.wait_recv()
-    square = squares_z[0]
-    for source in range(1, 16):
-        square = square + squares_z[source]
-    squares_y[y] = square
-    sy_copies = []
-    for d in range(1, 4):
-        copy = remote(squares_y.at[y], squares_y.at[y], sy_ss.at[d], sy_rs.at[d], at(x, (y + d) & 3, z, core))
-        copy.start()
-        sy_copies.append(copy)
-    sends += sy_copies
+    for copy in sy_copies:
+        copy.wait_recv()
+    square = squares_y[0]
+    for source in range(1, 32):
+        square = square + squares_y[source]
+    total_out[...] = square
     bpair.wait_recv()
     bias_out[...] = ball[...]
-    for copy in sy_copies:
-        copy.wait_recv()
-    total_out[...] = (squares_y[0] + squares_y[1]) + (squares_y[2] + squares_y[3])
     for copy in sends:
         copy.wait_send()
 
@@ -626,7 +611,7 @@
             pltpu.VMEM((16, ZLO, 16, LANES), BF16),
             pltpu.VMEM((ZLO, 16, LANES), BF16),
             pltpu.VMEM((16, 16, LANES), BF16),
-            pltpu.VMEM((8, 24, LANES), F32),
+            pltpu.VMEM((8, 16, LANES), F32),
             pltpu.VMEM((ZLO, 16, LANES), F32),
             pltpu.VMEM((ZLO, 16, LANES), BF16),
             pltpu.VMEM((ZLO, 16, LANES), BF16),
@@ -634,9 +619,8 @@
             pltpu.VMEM((2, ZLO, 16, LANES), F32),
             pltpu.VMEM((4, 64, LANES), BF16),
             pltpu.VMEM((16, 1, LANES), F32),
-            pltpu.VMEM((4, 1, LANES), F32),
-            pltpu.VMEM((2, SENT, LANES), BF16),
-            dma((13,)), dma((2,)), dma((2,)),
+            pltpu.VMEM((32, 1, LANES), F32),
+            dma((13,)),
             dma((4,)), dma((4,)),
             dma((4,)), dma((4,)),
             dma((16,)), dma((16,)),
@@ -649,7 +633,7 @@
             dma, dma,
             dma((4,)), dma((4,)),
             dma((16,)), dma((16,)),
-            dma((4,)), dma((4,)),
+            dma((32,)), dma((32,)),
         ],
         compiler_params=pltpu.CompilerParams(collective_id=0, has_side_effects=True, vmem_limit_bytes=VMEM_LIMIT),
         name="window_and_sums",

time: 69.4 us -> 67.4 us (0.971)
  Pallas kernels: 68.6 us -> 66.6 us
    pallas_call x1, Pallas kernels: 66.8 us -> 64.8 us  [main(): pl.pallas_call(main_kernel, out_shape=(jax.ShapeDtypeStruct((8, 16, LANES...]
where the time goes in v5:
time: 67.4 us; the launch traced here: 67.2 us
  Pallas kernels  66.6 us (99%)
    pallas_call x1, Pallas kernels, main(): pl.pallas_call(main_kernel, out_shape=(jax.ShapeDtypeStruct((8, 16, LANES...  64.8 us
    pallas_call x1, Pallas kernels, outputs(): pl.pallas_call(output_kernel, out_shape=(jax.ShapeDtypeStruct((WIN_LAT, W...  1.76 us

profile of v5, /device:TPU:1, one launch (start us, length us, event | category | flops | bytes accessed | tf_op | source)
XLA Modules:
  0.0 67.2 jit_solution(3887161757470654929)
XLA Ops:
  0.6 64.8 %window_and_sums.1 = (f32[8,16,128]{2,1,0:T(8,128)}, f32[2,8,16,128]{3,2,1,0:T(8,128)}, bf16[4,64,128]{2,1,0:T(8,128)(2,1)}, f32[1,128]{1,0:T(1,128)}) custom-call(bf16[6,12,384]{2,1,0:T(8,128)(2,1)} %tok_in.1, s32[6,2,12]{2,1,0:T(2,128)} %bitcast.9, bf16[16,192]{1,0:T(8,128)(2,1)} %embed_in.1, bf16[6,12,384]{2,1,0:T(8,128)(2,1)} %cot_in.1, ...), custom_call_target="tpu_custom_call" | custom-call | tf_op jit(solution)/shard_map/window_and_sums/pallas_call | solution.py:571
  65.5 1.8 %scaled_outputs.1 = (bf16[6,12,384]{2,1,0:T(8,128)(2,1)}, f32[3,576]{1,0:T(4,128)}, f32[3,192]{1,0:T(4,128)}, f32[3,768]{1,0:T(4,128)}, f32[12,192]{1,0:T(8,128)...) custom-call(f32[8,16,128]{2,1,0:T(8,128)} %get-tuple-element.20.dense_ref, ...), custom_call_target="tpu_custom_call" | custom-call | tf_op jit(solution)/shard_map/scaled_outputs/pallas_call | solution.py:700

commit v6 on v5

--- a/solution.py
+++ b/solution.py
@@ -75,8 +75,8 @@
 
 
 DENSE = TOK + 32
-FLAT = 3 * PART
-SENT = FLAT + 4
+FLAT = 3 * CELLS
+SENT = 64
 
 
 def layer_norm(values, gain):
@@ -101,9 +101,9 @@
     dense_out, bias_out, back_out, total_out,
     tok_ref, kind_ref, embed_ref, cot_ref, index_ref, table_ref, order_ref,
     gain1_ref, gain2_ref, mix_ref, outw_ref, up_ref, down_ref,
-    tok_s, kind_s, flat_s, pack_s, send, recv, table_s, dense_s, high_s, low_s, bias_s, spread_s,
+    tok_s, kind_s, flat_s, pack_s, cots_s, send, recv, send_g, recv_g, table_s, dense_s, high_s, low_s, bias_s, spread_s,
     grid_s, x_s, g_s, hot_s, ge_s, moved_s, unpack_s, score_s, extra_s, back_s,
-    grad_s, rows_s, grads, acc_s, parts_s,
+    grad_s, wide_s, rows_s, grads, acc_s, parts_s,
     core_r, plane_s, plane_r, line_s, line_r, share, bcore_r, bline_s, bline_r, brow_r, ball, back_r, squares_z, squares_y,
     in_sems, halo_ss, halo_rs,
     core_ss, core_rs, plane_ss, plane_rs, line_ss, line_rs, share_ss, share_rs, bcore_ss, bcore_rs, bline_ss, bline_rs,
@@ -160,7 +160,7 @@
             start = 6 * (row % 3)
             cells = slice(6 * half, 6 * half + 6)
             tok_s[quarter, start : start + 6, :] = tok[cells]
-            flat_s[quarter, CELLS + start : CELLS + start + 6, :] = cot[cells]
+            flat_s[quarter, start : start + 6, :] = cot[cells]
             kind_s[quarter, 0:2, start : start + 6] = kind[:, cells]
     sub = lax.broadcasted_iota(jnp.int32, (2 * KINDS, LANES), 0).astype(F32)
     for quarter in range(4):
@@ -168,23 +168,30 @@
         hot = (sub == kinds[0:1]) | (sub - KINDS == kinds[1:2])
         hot = jnp.where(hot, 1.0, 0.0).astype(BF16)[:, 0:24]
         stored = tok_s[quarter] + dot_tn(hot, wide)
-        flat_s[quarter, 0:CELLS, :] = stored[0:CELLS]
+        tok_s[quarter, 0:CELLS, :] = stored[0:CELLS]
+        pack_s[quarter, FLAT:SENT, :] = jnp.zeros((SENT - FLAT, LANES), F32)
+        cots_s[quarter, FLAT:SENT, :] = jnp.zeros((SENT - FLAT, LANES), F32)
         for tile in range(3):
-            pack_s[quarter, PART * tile : PART * tile + PART, :] = flat_s[
-                quarter, 0:PART, tile * LANES : (tile + 1) * LANES
-            ]
-        pack_s[quarter, FLAT:SENT, :] = jnp.zeros((4, LANES), F32)
+            rows, lanes = slice(CELLS * tile, CELLS * tile + CELLS), slice(tile * LANES, (tile + 1) * LANES)
+            pack_s[quarter, rows, :] = tok_s[quarter, 0:CELLS, lanes]
+            cots_s[quarter, rows, :] = flat_s[quarter, 0:CELLS, lanes]
         pack_s[quarter, FLAT : FLAT + 1, :] = kinds[0:1] + pltpu.roll(kinds, CELLS, 1)[1:2]
         send[quarter] = pack_s[quarter].astype(BF16)
+        send_g[quarter] = cots_s[quarter].astype(BF16)
     pl.semaphore_wait(barrier, len(peers))
-    halo_copies = []
-    for slot in (3, 2, 1):
-        copy = remote(
-            send.at[3 - slot], recv.at[slot], halo_ss.at[slot], halo_rs.at[slot], beside(lat, lon, -(slot // 2), -(slot % 2))
-        )
-        copy.start()
-        halo_copies.append(copy)
-    sends = list(halo_copies)
+    halo_copies, cot_copies = [], []
+    for copies, src, dst, base in ((halo_copies, send, recv, 0), (cot_copies, send_g, recv_g, 4)):
+        for slot in (3, 2, 1):
+            copy = remote(
+                src.at[3 - slot],
+                dst.at[slot],
+                halo_ss.at[base + slot],
+                halo_rs.at[base + slot],
+                beside(lat, lon, -(slot // 2), -(slot % 2)),
+            )
+            copy.start()
+            copies.append(copy)
+    sends = halo_copies + cot_copies
 
     for fetch in fetches[4:7]:
         fetch.wait()
@@ -241,14 +248,13 @@
     for slot in range(4):
         unpack_s[slot] = (send[3] if slot == 0 else recv[slot]).astype(F32)
         for tile in range(3):
-            grid_s[slot, 0:PART, tile * LANES : (tile + 1) * LANES] = unpack_s[slot, PART * tile : PART * tile + PART, :]
+            grid_s[slot, 0:CELLS, tile * LANES : (tile + 1) * LANES] = unpack_s[
+                slot, CELLS * tile : CELLS * tile + CELLS, :
+            ]
         toks = grid_s[slot, 0:CELLS, :]
-        cots = grid_s[slot, CELLS:PART, :]
         base = PART * slot
         x_s[base : base + CELLS, :] = toks[:, 0:C]
         x_s[base + CELLS : base + PART, :] = toks[:, C : 2 * C]
-        g_s[base : base + CELLS, :] = cots[:, 0:C]
-        g_s[base + CELLS : base + PART, :] = cots[:, C : 2 * C]
         kind_row = unpack_s[slot, FLAT : FLAT + 1, :]
         kind_col = jnp.sum(jnp.where(lane36 == sub36, kind_row, 0.0), axis=1, keepdims=True)
         hot_s[base : base + PART, :] = jnp.where(lane36.astype(F32) == kind_col, 1.0, 0.0)
@@ -259,8 +265,6 @@
     mix_weight, out_weight = mix_ref[...], outw_ref[...]
     up_weight, down_weight = up_ref[...], down_ref[...]
     residual = x_s[...]
-    upstream = g_s[...]
-    upstream_low = upstream.astype(BF16)
     first, hat1, inv1 = layer_norm(residual, gain1)
     first_in = first.astype(BF16)
     mixed = dot(first_in, mix_weight)
@@ -291,7 +295,44 @@
     slope = 0.5 * (1.0 + tangent) + 0.5 * inner * (1.0 - tangent * tangent) * GELU_SQRT * (
         1.0 + 3.0 * GELU_CUBE * inner * inner
     )
+    for copy in cot_copies:
+        copy.wait_recv()
+    for slot in range(4):
+        cots_s[slot] = (send_g[3] if slot == 0 else recv_g[slot]).astype(F32)
+        for tile in range(3):
+            flat_s[slot, 0:CELLS, tile * LANES : (tile + 1) * LANES] = cots_s[
+                slot, CELLS * tile : CELLS * tile + CELLS, :
+            ]
+        cots = flat_s[slot, 0:CELLS, :]
+        base = PART * slot
+        g_s[base : base + CELLS, :] = cots[:, 0:C]
+        g_s[base + CELLS : base + PART, :] = cots[:, C : 2 * C]
+    upstream = g_s[...]
+    upstream_low = upstream.astype(BF16)
     hidden_grad = (dot(upstream_low, down_weight) * slope).astype(BF16)
+
+    grad_s[:, 4 * C : 8 * C] = dot_tn(second_in, hidden_grad)
+    spread = dot(hidden_low, spread_s[...]).astype(BF16)
+    for part in range(4):
+        grad_s[:, (8 + part) * C : (9 + part) * C] = dot_tn(spread[:, part * C : (part + 1) * C], upstream_low)
+    for tile in range(12):
+        for part in range(4):
+            wide_s[tile // 6, part, pl.ds(tile % 6, 48, stride=6), :] = grad_s[
+                48 * part : 48 * part + 48, (6 + tile) * LANES : (7 + tile) * LANES
+            ]
+
+    def first_blocks(half):
+        for part in range(4):
+            for block in range(ZLO):
+                got = wide_s[half, part, 36 * block : 36 * block + 32, :].astype(BF16)
+                grads[half, 0, part, 0, block] = got[0:16]
+                grads[half, 0, part, 1, block] = got[16:32]
+
+    first_blocks(other)
+    core_copies = [remote(grads.at[other, 0], core_r.at[0], core_ss.at[0], core_rs.at[0], at(x, y, z, other))]
+    core_copies[0].start()
+    first_blocks(core)
+
     second_grad = dot_nt(hidden_grad, up_weight)
     mid_grad = upstream + norm_backward(second_grad, hat2, inv2, gain2)
     mid_low = mid_grad.astype(BF16)
@@ -314,6 +355,30 @@
     )
     moved = mid_grad + norm_backward(first_grad, hat1, inv1, gain1)
 
+    here = x * 4 + y
+
+    def plane(batch):
+        core_copies[batch].wait_recv()
+        for part in range(4):
+            for i in range(2):
+                plane_s[batch, part, i] = (
+                    grads[core, batch, part, i].astype(F32) + core_r[batch, part, i].astype(F32)
+                ).astype(BF16)
+        for dy in (1, 2, 3, 0):
+            for i in (1, 0) if dy else (1,):
+                to_y, to_i = (y + dy) & 3, (x + i) & 1
+                copy = remote(
+                    plane_s.at[batch, to_y, to_i],
+                    plane_r.at[here],
+                    plane_ss.at[batch * 8 + dy * 2 + i],
+                    plane_rs.at[here],
+                    at(batch * 2 + to_i, to_y, z, core),
+                )
+                copy.start()
+                sends.append(copy)
+
+    plane(0)
+
     lane = lax.broadcasted_iota(jnp.int32, (TOK, LANES), 1)
     small = jnp.zeros((C, LANES), F32)
     for left, right in (
@@ -334,33 +399,29 @@
     grad_s[:, C : 2 * C] = dot_tn(first_in, key_grad)
     grad_s[:, 2 * C : 3 * C] = dot_tn(first_in, value_grad)
     grad_s[:, 3 * C : 4 * C] = dot_tn(context, mid_low)
-    grad_s[:, 4 * C : 8 * C] = dot_tn(second_in, hidden_grad)
-    spread = dot(hidden_low, spread_s[...]).astype(BF16)
-    for part in range(4):
-        grad_s[:, (8 + part) * C : (9 + part) * C] = dot_tn(spread[:, part * C : (part + 1) * C], upstream_low)
-    for tile in range(TILES):
+    for tile in range(6):
         for part in range(4):
-            rows_s[tile // 9, part, pl.ds(tile % 9, 48, stride=9), :] = grad_s[
+            rows_s[tile // 3, part, pl.ds(8 + tile % 3, 48, stride=3), :] = grad_s[
                 48 * part : 48 * part + 48, tile * LANES : (tile + 1) * LANES
             ]
-    sub64 = lax.broadcasted_iota(jnp.int32, (64, LANES), 0)
-
-    def blocks(half, part):
-        for block in range(ZLO):
-            got = rows_s[half, part, 54 * block : 54 * block + 64, :]
-            line = extra_s[pl.ds(part * ZLO + block, 1), :] * jnp.where(half == 0, 1.0, 0.0)
-            got = jnp.where(sub64 < 54, got, jnp.where(sub64 == 54, line, 0.0)).astype(BF16)
-            for quarter in range(4):
-                grads[half, part, quarter, block] = got[16 * quarter : 16 * quarter + 16]
-
-    core_copies = []
-    for j in range(4):
-        to = (y + 1 + j) & 3
-        blocks(other, to)
-        copy = remote(grads.at[other, to], core_r.at[to], core_ss.at[j], core_rs.at[j], at(x, y, z, other))
-        copy.start()
-        core_copies.append(copy)
+    sub16 = lax.broadcasted_iota(jnp.int32, (16, LANES), 0)
+
+    def last_blocks(half):
+        for part in range(4):
+            for block in range(ZLO):
+                wide_rows = wide_s[half, part, 36 * block + 32 : 36 * block + 48, :]
+                upper = rows_s[half, part, 18 * block + 4 : 18 * block + 20, :]
+                lower = rows_s[half, part, 18 * block + 20 : 18 * block + 36, :]
+                line = extra_s[part * ZLO + block : part * ZLO + block + 1, :] * jnp.where(half == 0, 1.0, 0.0)
+                grads[half, 1, part, 0, block] = jnp.where(sub16 < 4, wide_rows, upper).astype(BF16)
+                lower = jnp.where(sub16 < 6, lower, jnp.where(sub16 == 6, line, 0.0))
+                grads[half, 1, part, 1, block] = lower.astype(BF16)
+
+    last_blocks(other)
+    core_copies.append(remote(grads.at[other, 1], core_r.at[1], core_ss.at[1], core_rs.at[1], at(x, y, z, other)))
+    core_copies[1].start()
     sends += core_copies
+    last_blocks(core)
     moved_s[...] = moved
     for slot in range(4):
         base = PART * slot
@@ -381,26 +442,13 @@
         back_copies.append((slot, copy))
     sends += [copy for _, copy in back_copies]
 
-    plane_copies = {}
-    for j in range(4):
-        to_y = (y + 1 + j) & 3
-        blocks(core, to_y)
-        core_copies[j].wait_recv()
-        for part in range(4):
-            plane_s[to_y, part] = (grads[core, to_y, part].astype(F32) + core_r[to_y, part].astype(F32)).astype(BF16)
-        for i in range(4):
-            dx, dy = (i + 1) % 4, (j + 1) % 4
-            d = dx * 4 + dy
-            to_x = (x + dx) & 3
-            if d == 0:
-                plane_r[x * 4 + y] = plane_s[y, x]
-                continue
-            copy = remote(
-                plane_s.at[to_y, to_x], plane_r.at[x * 4 + y], plane_ss.at[d], plane_rs.at[d], at(to_x, to_y, z, core)
-            )
-            copy.start()
-            plane_copies[d] = copy
-    sends += list(plane_copies.values())
+    plane(1)
+    copy = remote(
+        plane_s.at[1 - (x >> 1), y, x & 1], plane_r.at[here], plane_ss.at[0], plane_rs.at[here], at(x ^ 2, y, z, core)
+    )
+    copy.start()
+    sends.append(copy)
+    plane_r[here] = plane_s[x >> 1, y, x & 1]
 
     acc_s[...] = jnp.zeros((208, LANES), F32)
     for n in range(HEADS):
@@ -427,7 +475,6 @@
         return carry
 
     lax.fori_loop(0, DENSE // 16, scatter, 0)
-    sub16 = lax.broadcasted_iota(jnp.int32, (16, LANES), 0)
     for block in range(16):
         parts_s[block // 8, block % 8] = jnp.where(sub16 < 12, acc_s[12 * block : 12 * block + 16, :], 0.0)
 
@@ -448,8 +495,11 @@
         bline_copies.append(copy)
     sends += bline_copies
 
-    for copy in plane_copies.values():
-        copy.wait_recv()
+    for d in range(1, 16):
+        source = ((x + (d >> 2)) & 3) * 4 + ((y + d) & 3)
+        remote(
+            plane_s.at[0, 0, 0], plane_r.at[source], plane_ss.at[0], plane_rs.at[source], at(x, y, z, other)
+        ).wait_recv()
     for part in range(ZLO):
         block = plane_r[0, part].astype(F32)
         for source in range(1, 16):
@@ -583,6 +633,9 @@
             pltpu.VMEM((4, 8, LANES), F32),
             pltpu.VMEM((4, 40, 2 * C), F32),
             pltpu.VMEM((4, SENT, LANES), F32),
+            pltpu.VMEM((4, SENT, LANES), F32),
+            pltpu.VMEM((4, SENT, LANES), BF16),
+            pltpu.VMEM((4, SENT, LANES), BF16),
             pltpu.VMEM((4, SENT, LANES), BF16),
             pltpu.VMEM((4, SENT, LANES), BF16),
             pltpu.VMEM((HEADS * 32, LANES), F32),
@@ -602,12 +655,13 @@
             pltpu.VMEM((32, LANES), F32),
             pltpu.VMEM((4, 64, LANES), BF16),
             pltpu.VMEM((C, COLS), F32),
-            pltpu.VMEM((2, 4, 448, LANES), F32),
-            pltpu.VMEM((2, 4, 4, ZLO, 16, LANES), BF16),
+            pltpu.VMEM((2, 4, 304, LANES), F32),
+            pltpu.VMEM((2, 4, 168, LANES), F32),
+            pltpu.VMEM((2, 2, 4, 2, ZLO, 16, LANES), BF16),
             pltpu.VMEM((208, LANES), F32),
             pltpu.VMEM((2, ZLO, 16, LANES), F32),
-            pltpu.VMEM((4, 4, ZLO, 16, LANES), BF16),
-            pltpu.VMEM((4, 4, ZLO, 16, LANES), BF16),
+            pltpu.VMEM((2, 4, 2, ZLO, 16, LANES), BF16),
+            pltpu.VMEM((2, 4, 2, ZLO, 16, LANES), BF16),
             pltpu.VMEM((16, ZLO, 16, LANES), BF16),
             pltpu.VMEM((ZLO, 16, LANES), BF16),
             pltpu.VMEM((16, 16, LANES), BF16),
@@ -621,7 +675,7 @@
             pltpu.VMEM((16, 1, LANES), F32),
             pltpu.VMEM((32, 1, LANES), F32),
             dma((13,)),
-            dma((4,)), dma((4,)),
+            dma((8,)), dma((8,)),
             dma((4,)), dma((4,)),
             dma((16,)), dma((16,)),
             dma((16,)), dma((16,)),
@@ -651,9 +705,12 @@
     for part in range(8):
         dense_s[part // 4, 16 * (part % 4) : 16 * (part % 4) + 16, :] = dense_ref[part] * factor
     for tile in range(TILES):
-        half, t = tile // 9, tile % 9
-        even_rows = dense_s[half, pl.ds(t, 3, stride=9), :]
-        odd_rows = dense_s[half, pl.ds(27 + t, 3, stride=9), :]
+        if tile < 6:
+            half, start, step = tile // 3, 36 + tile % 3, 3
+        else:
+            half, start, step = (tile - 6) // 6, tile % 6, 6
+        even_rows = dense_s[half, pl.ds(start, 3, stride=step), :]
+        odd_rows = dense_s[half, pl.ds(start + 3 * step, 3, stride=step), :]
         flat_s[0:3, tile * LANES : (tile + 1) * LANES] = jnp.where(odd, odd_rows, even_rows)
     flat = flat_s[0:3, :]
     mix_ref[...] = flat[:, 0 : 3 * C]

time: 67.4 us -> 68.5 us (1.016)
  Pallas kernels: 66.6 us -> 67.6 us
    pallas_call x1, Pallas kernels: 64.8 us -> 65.9 us  [main(): pl.pallas_call(main_kernel, out_shape=(jax.ShapeDtypeStruct((8, 16, LANES...]
where the time goes in v6:
time: 68.5 us; the launch traced here: 68.3 us
  Pallas kernels  67.6 us (99%)
    pallas_call x1, Pallas kernels, main(): pl.pallas_call(main_kernel, out_shape=(jax.ShapeDtypeStruct((8, 16, LANES...  65.9 us
    pallas_call x1, Pallas kernels, outputs(): pl.pallas_call(output_kernel, out_shape=(jax.ShapeDtypeStruct((WIN_LAT, W...  1.76 us

profile of v6, /device:TPU:1, one launch (start us, length us, event | category | flops | bytes accessed | tf_op | source)
XLA Modules:
  0.0 68.3 jit_solution(11552536913609795312)
XLA Ops:
  0.6 65.9 %window_and_sums.1 = (f32[8,16,128]{2,1,0:T(8,128)}, f32[2,8,16,128]{3,2,1,0:T(8,128)}, bf16[4,64,128]{2,1,0:T(8,128)(2,1)}, f32[1,128]{1,0:T(1,128)}) custom-call(bf16[6,12,384]{2,1,0:T(8,128)(2,1)} %tok_in.1, s32[6,2,12]{2,1,0:T(2,128)} %bitcast.9, bf16[16,192]{1,0:T(8,128)(2,1)} %embed_in.1, bf16[6,12,384]{2,1,0:T(8,128)(2,1)} %cot_in.1, ...), custom_call_target="tpu_custom_call" | custom-call | tf_op jit(solution)/shard_map/window_and_sums/pallas_call | solution.py:621
  66.5 1.8 %scaled_outputs.1 = (bf16[6,12,384]{2,1,0:T(8,128)(2,1)}, f32[3,576]{1,0:T(4,128)}, f32[3,192]{1,0:T(4,128)}, f32[3,768]{1,0:T(4,128)}, f32[12,192]{1,0:T(8,128)...) custom-call(f32[8,16,128]{2,1,0:T(8,128)} %get-tuple-element.20.dense_ref, ...), custom_call_target="tpu_custom_call" | custom-call | tf_op jit(solution)/shard_map/scaled_outputs/pallas_call | solution.py:757

commit v7 on v5

--- a/solution.py
+++ b/solution.py
@@ -30,6 +30,7 @@
 GELU_SQRT = 0.7978845608028654
 GELU_CUBE = 0.044715
 LON, LAT = 64, 8
+FIXED = 8191.0
 ZLO = 8
 VMEM_LIMIT = 56 * 1024 * 1024
 
@@ -101,7 +102,7 @@
     dense_out, bias_out, back_out, total_out,
     tok_ref, kind_ref, embed_ref, cot_ref, index_ref, table_ref, order_ref,
     gain1_ref, gain2_ref, mix_ref, outw_ref, up_ref, down_ref,
-    tok_s, kind_s, flat_s, pack_s, send, recv, table_s, dense_s, high_s, low_s, bias_s, spread_s,
+    tok_s, kind_s, flat_s, pack_s, send, recv, table_s, pairs_s, dense_s, high_s, low_s, bias_s, spread_s,
     grid_s, x_s, g_s, hot_s, ge_s, moved_s, unpack_s, score_s, extra_s, back_s,
     grad_s, rows_s, grads, acc_s, parts_s,
     core_r, plane_s, plane_r, line_s, line_r, share, bcore_r, bline_s, bline_r, brow_r, ball, back_r, squares_z, squares_y,
@@ -190,8 +191,8 @@
         fetch.wait()
     order = order_ref[...]
     index = index_ref[...]
-    high = (index // LANES).astype(F32).astype(BF16)
-    low = (index % LANES).astype(F32).astype(BF16)
+    high = (index >> 7).astype(F32).astype(BF16)
+    low = (index & (LANES - 1)).astype(F32).astype(BF16)
     dense_rows(high_s, dot_nt(dot(order, high).astype(BF16), order), 0)
     dense_rows(low_s, dot_nt(dot(order, low).astype(BF16), order), 0)
     table_s[...] = jnp.zeros((HEADS * 32, LANES), F32)
@@ -209,19 +210,27 @@
         place_at = (lax.broadcasted_iota(jnp.int32, (LANES, FF), 0) + LANES * block).astype(F32)
         spread_s[LANES * block : LANES * (block + 1), :] = jnp.where(place_at == unit, 1.0, 0.0).astype(BF16)
 
+    for pair in range(3):
+        fixed = [
+            ((table_s[64 * pair + 32 * k : 64 * pair + 32 * k + 32, :] + 4.0) * FIXED + 0.5).astype(jnp.int32) for k in range(2)
+        ]
+        pairs_s[32 * pair : 32 * pair + 32, :] = (fixed[0] << 16) | fixed[1]
+
     def gather(step, carry):
         start = pl.multiple_of(step * 16, 16)
         lows = low_s[pl.ds(start, 16), :].astype(jnp.int32)
         highs = high_s[pl.ds(start, 16), :]
-        totals = [jnp.zeros((16, LANES), F32) for _ in range(HEADS)]
+        totals = [jnp.zeros((16, LANES), jnp.int32) for _ in range(3)]
         for row in range(HI):
             chosen = highs == float(row)
-            for head in range(HEADS):
-                line = jnp.broadcast_to(table_s[32 * head + row : 32 * head + row + 1, :], (16, LANES))
+            for pair in range(3):
+                line = jnp.broadcast_to(pairs_s[32 * pair + row : 32 * pair + row + 1, :], (16, LANES))
                 found = jnp.take_along_axis(line, lows, axis=1, mode="promise_in_bounds")
-                totals[head] = jnp.where(chosen, found, totals[head])
+                totals[pair] = jnp.where(chosen, found, totals[pair])
         for head in range(HEADS):
-            dense_s[pl.ds(pl.multiple_of(head * DENSE + start, 16), 16), :] = totals[head]
+            fixed = totals[head // 2]
+            fixed = (fixed if head % 2 else fixed >> 16) & 0xFFFF
+            dense_s[pl.ds(pl.multiple_of(head * DENSE + start, 16), 16), :] = fixed.astype(F32) * (1.0 / FIXED) - 4.0
         return carry
 
     lax.fori_loop(0, DENSE // 16, gather, 0)
@@ -272,9 +281,10 @@
     q_stack = jnp.concatenate([jnp.where(m, queries, 0.0) for m in of_head], axis=0).astype(BF16)
     scores = dot_nt(q_stack, keys) * (HEAD**-0.5) + bias_s[...]
     last = lat == LAT - 1
-    group_q = ((lax.broadcasted_iota(jnp.int32, (HEADS * TOK, TOK), 0) // 72) % 2).astype(F32)
-    group_k = (lax.broadcasted_iota(jnp.int32, (HEADS * TOK, TOK), 1) >= 72).astype(F32)
-    allowed = jnp.abs(group_q - group_k) * jnp.where(last, 1.0, 0.0) < 0.5
+    group_q = jnp.where(lax.broadcasted_iota(jnp.int32, (TOK, TOK), 0) >= 72, 1.0, 0.0)
+    group_k = jnp.where(lax.broadcasted_iota(jnp.int32, (TOK, TOK), 1) >= 72, 1.0, 0.0)
+    apart = jnp.abs(group_q - group_k) * jnp.where(last, 1.0, 0.0)
+    allowed = jnp.concatenate([apart] * HEADS, axis=0) < 0.5
     expon = jnp.where(allowed, jnp.exp(scores), 0.0)
     attend = expon * (1.0 / jnp.sum(expon, axis=-1, keepdims=True))
     attend_low = attend.astype(BF16)
@@ -586,6 +596,7 @@
             pltpu.VMEM((4, SENT, LANES), BF16),
             pltpu.VMEM((4, SENT, LANES), BF16),
             pltpu.VMEM((HEADS * 32, LANES), F32),
+            pltpu.VMEM((3 * 32, LANES), jnp.int32),
             pltpu.VMEM((HEADS * DENSE, LANES), F32),
             pltpu.VMEM((DENSE, LANES), F32),
             pltpu.VMEM((DENSE, LANES), F32),

time: 67.4 us -> 66.9 us (level)
  no operation moved by 1% of the time
where the time goes in v7:
time: 66.9 us; the launch traced here: 66.8 us
  Pallas kernels  66.1 us (99%)
    pallas_call x1, Pallas kernels, main(): pl.pallas_call(main_kernel, out_shape=(jax.ShapeDtypeStruct((8, 16, LANES...  64.4 us
    pallas_call x1, Pallas kernels, outputs(): pl.pallas_call(output_kernel, out_shape=(jax.ShapeDtypeStruct((WIN_LAT, W...  1.76 us

profile of v7, /device:TPU:1, one launch (start us, length us, event | category | flops | bytes accessed | tf_op | source)
XLA Modules:
  0.0 66.8 jit_solution(4485385719319755823)
XLA Ops:
  0.6 64.4 %window_and_sums.1 = (f32[8,16,128]{2,1,0:T(8,128)}, f32[2,8,16,128]{3,2,1,0:T(8,128)}, bf16[4,64,128]{2,1,0:T(8,128)(2,1)}, f32[1,128]{1,0:T(1,128)}) custom-call(bf16[6,12,384]{2,1,0:T(8,128)(2,1)} %tok_in.1, s32[6,2,12]{2,1,0:T(2,128)} %bitcast.9, bf16[16,192]{1,0:T(8,128)(2,1)} %embed_in.1, bf16[6,12,384]{2,1,0:T(8,128)(2,1)} %cot_in.1, ...), custom_call_target="tpu_custom_call" | custom-call | tf_op jit(solution)/shard_map/window_and_sums/pallas_call | solution.py:581
  65.0 1.8 %scaled_outputs.1 = (bf16[6,12,384]{2,1,0:T(8,128)(2,1)}, f32[3,576]{1,0:T(4,128)}, f32[3,192]{1,0:T(4,128)}, f32[3,768]{1,0:T(4,128)}, f32[12,192]{1,0:T(8,128)...) custom-call(f32[8,16,128]{2,1,0:T(8,128)} %get-tuple-element.20.dense_ref, ...), custom_call_target="tpu_custom_call" | custom-call | tf_op jit(solution)/shard_map/scaled_outputs/pallas_call | solution.py:711

commit v8 on v7

--- a/solution.py
+++ b/solution.py
@@ -105,9 +105,9 @@
     tok_s, kind_s, flat_s, pack_s, send, recv, table_s, pairs_s, dense_s, high_s, low_s, bias_s, spread_s,
     grid_s, x_s, g_s, hot_s, ge_s, moved_s, unpack_s, score_s, extra_s, back_s,
     grad_s, rows_s, grads, acc_s, parts_s,
-    core_r, plane_s, plane_r, line_s, line_r, share, bcore_r, bline_s, bline_r, brow_r, ball, back_r, squares_z, squares_y,
+    core_r, plane_s, plane_r, line_s, line_r, share, bline_s, bline_r, brow_r, ball, back_r, squares_z, squares_y,
     in_sems, halo_ss, halo_rs,
-    core_ss, core_rs, plane_ss, plane_rs, line_ss, line_rs, share_ss, share_rs, bcore_ss, bcore_rs, bline_ss, bline_rs,
+    core_ss, core_rs, plane_ss, plane_rs, line_ss, line_rs, share_ss, share_rs, bline_ss, bline_rs,
     brow_ss, brow_rs, ball_ss, ball_rs, bpair_ss, bpair_rs, back_ss, back_rs, sz_ss, sz_rs, sy_ss, sy_rs,
 ):
     lon, lat = lax.axis_index("lon"), lax.axis_index("lat")
@@ -139,6 +139,7 @@
     peers += [at(x, y, (z + d) & 15, core) for d in range(1, 16)]
     peers += [at((x + d // 4) & 3, (y + d % 4) & 3, z, core) for d in range(1, 16)]
     peers += [at((x + d // 4) & 3, (y + d % 4) & 3, z, other) for d in range(16)]
+    peers += [at(x, y, z_hi * ZLO + ((z_lo + d) & 7), other) for d in range(1, ZLO)]
     for peer in peers:
         pl.semaphore_signal(barrier, inc=1, device_id=peer, device_id_type=MESH)
 
@@ -391,6 +392,32 @@
         back_copies.append((slot, copy))
     sends += [copy for _, copy in back_copies]
 
+    acc_s[...] = jnp.zeros((208, LANES), F32)
+    for n in range(HEADS):
+        dense_rows(dense_s, score_s[n * TOK : (n + 1) * TOK, :], n * DENSE)
+    row32 = lax.broadcasted_iota(jnp.int32, (32, LANES), 0).astype(F32).astype(BF16)
+    row128 = lax.broadcasted_iota(jnp.int32, (LANES, LANES), 0).astype(F32).astype(BF16)
+    zero, one = jnp.zeros((), BF16), jnp.ones((), BF16)
+
+    def low_rows(line, count):
+        return jnp.concatenate([jnp.broadcast_to(line, (16, LANES)).astype(BF16)] * (count // 16), axis=0)
+
+    def scatter(step, carry):
+        left, right = [], []
+        start = pl.multiple_of(step * 16, 16)
+        highs, lows = high_s[pl.ds(start, 16), :], low_s[pl.ds(start, 16), :]
+        scores = [dense_s[pl.ds(pl.multiple_of(n * DENSE + start, 16), 16), :] for n in range(HEADS)]
+        for row in range(16):
+            chosen = row32 == low_rows(highs[row : row + 1], 32)
+            right.append(jnp.where(row128 == low_rows(lows[row : row + 1], LANES), one, zero))
+            left.append(
+                jnp.concatenate([jnp.where(chosen, low_rows(scores[n][row : row + 1], 32), zero) for n in range(HEADS)], axis=0)
+            )
+        acc_s[0 : 32 * HEADS, :] += dot_nt(jnp.concatenate(left, axis=1), jnp.concatenate(right, axis=1))
+        return carry
+
+    lax.fori_loop(0, 4, scatter, 0)
+
     plane_copies = {}
     for j in range(4):
         to_y = (y + 1 + j) & 3
@@ -412,47 +439,22 @@
             plane_copies[d] = copy
     sends += list(plane_copies.values())
 
-    acc_s[...] = jnp.zeros((208, LANES), F32)
-    for n in range(HEADS):
-        dense_rows(dense_s, score_s[n * TOK : (n + 1) * TOK, :], n * DENSE)
-    row32 = lax.broadcasted_iota(jnp.int32, (32, LANES), 0).astype(F32).astype(BF16)
-    row128 = lax.broadcasted_iota(jnp.int32, (LANES, LANES), 0).astype(F32).astype(BF16)
-    zero, one = jnp.zeros((), BF16), jnp.ones((), BF16)
-
-    def low_rows(line, count):
-        return jnp.concatenate([jnp.broadcast_to(line, (16, LANES)).astype(BF16)] * (count // 16), axis=0)
-
-    def scatter(step, carry):
-        left, right = [], []
-        start = pl.multiple_of(step * 16, 16)
-        highs, lows = high_s[pl.ds(start, 16), :], low_s[pl.ds(start, 16), :]
-        scores = [dense_s[pl.ds(pl.multiple_of(n * DENSE + start, 16), 16), :] for n in range(HEADS)]
-        for row in range(16):
-            chosen = row32 == low_rows(highs[row : row + 1], 32)
-            right.append(jnp.where(row128 == low_rows(lows[row : row + 1], LANES), one, zero))
-            left.append(
-                jnp.concatenate([jnp.where(chosen, low_rows(scores[n][row : row + 1], 32), zero) for n in range(HEADS)], axis=0)
-            )
-        acc_s[0 : 32 * HEADS, :] += dot_nt(jnp.concatenate(left, axis=1), jnp.concatenate(right, axis=1))
-        return carry
-
-    lax.fori_loop(0, DENSE // 16, scatter, 0)
+    lax.fori_loop(4, DENSE // 16, scatter, 0)
     sub16 = lax.broadcasted_iota(jnp.int32, (16, LANES), 0)
     for block in range(16):
         parts_s[block // 8, block % 8] = jnp.where(sub16 < 12, acc_s[12 * block : 12 * block + 16, :], 0.0)
 
-    bcore = remote(parts_s.at[other], bcore_r, bcore_ss, bcore_rs, at(x, y, z, other))
-    bcore.start()
-    sends.append(bcore)
-    bcore.wait_recv()
-    for part in range(ZLO):
-        bline_s[part] = (parts_s[core, part] + bcore_r[part]).astype(BF16)
-    bline_r[z_lo] = bline_s[z_lo]
+    bline_s[...] = parts_s[...].astype(BF16)
+    bline_r[core, z_lo] = bline_s[core, z_lo]
     bline_copies = []
-    for d in range(1, ZLO):
-        to = (z_lo + d) & 7
+    for d in range(1, 16):
+        to_core, to = core + (d >> 3) * (1 - 2 * core), (z_lo + d) & 7
         copy = remote(
-            bline_s.at[to], bline_r.at[z_lo], bline_ss.at[d], bline_rs.at[d], at(x, y, z_hi * ZLO + to, core)
+            bline_s.at[to_core, to],
+            bline_r.at[core, z_lo],
+            bline_ss.at[d],
+            bline_rs.at[d],
+            at(x, y, z_hi * ZLO + to, to_core),
         )
         copy.start()
         bline_copies.append(copy)
@@ -476,9 +478,9 @@
 
     for copy in bline_copies:
         copy.wait_recv()
-    part_sum = bline_r[0].astype(F32)
-    for part in range(1, ZLO):
-        part_sum = part_sum + bline_r[part].astype(F32)
+    part_sum = bline_r[0, 0].astype(F32)
+    for part in range(1, 16):
+        part_sum = part_sum + bline_r[part // ZLO, part % ZLO].astype(F32)
     brow_r[y] = part_sum
     brow_copies = []
     for d in range(1, 4):
@@ -623,9 +625,8 @@
             pltpu.VMEM((ZLO, 16, LANES), BF16),
             pltpu.VMEM((16, 16, LANES), BF16),
             pltpu.VMEM((8, 16, LANES), F32),
-            pltpu.VMEM((ZLO, 16, LANES), F32),
-            pltpu.VMEM((ZLO, 16, LANES), BF16),
-            pltpu.VMEM((ZLO, 16, LANES), BF16),
+            pltpu.VMEM((2, ZLO, 16, LANES), BF16),
+            pltpu.VMEM((2, ZLO, 16, LANES), BF16),
             pltpu.VMEM((4, 16, LANES), F32),
             pltpu.VMEM((2, ZLO, 16, LANES), F32),
             pltpu.VMEM((4, 64, LANES), BF16),
@@ -637,8 +638,7 @@
             dma((16,)), dma((16,)),
             dma((16,)), dma((16,)),
             dma((8,)), dma((8,)),
-            dma, dma,
-            dma((8,)), dma((8,)),
+            dma((16,)), dma((16,)),
             dma((4,)), dma((4,)),
             dma((8,)), dma((8,)),
             dma, dma,

time: 66.9 us -> 67.6 us (1.010)
  Pallas kernels: 66.1 us -> 66.8 us
    pallas_call x1, Pallas kernels: 64.4 us -> 65.1 us  [main(): pl.pallas_call(main_kernel, out_shape=(jax.ShapeDtypeStruct((8, 16, LANES...]
where the time goes in v8:
time: 67.6 us; the launch traced here: 67.5 us
  Pallas kernels  66.8 us (99%)
    pallas_call x1, Pallas kernels, main(): pl.pallas_call(main_kernel, out_shape=(jax.ShapeDtypeStruct((8, 16, LANES...  65.1 us
    pallas_call x1, Pallas kernels, outputs(): pl.pallas_call(output_kernel, out_shape=(jax.ShapeDtypeStruct((WIN_LAT, W...  1.76 us

profile of v8, /device:TPU:1, one launch (start us, length us, event | category | flops | bytes accessed | tf_op | source)
XLA Modules:
  0.0 67.5 jit_solution(7283405272169087682)
XLA Ops:
  0.6 65.1 %window_and_sums.1 = (f32[8,16,128]{2,1,0:T(8,128)}, f32[2,8,16,128]{3,2,1,0:T(8,128)}, bf16[4,64,128]{2,1,0:T(8,128)(2,1)}, f32[1,128]{1,0:T(1,128)}) custom-call(bf16[6,12,384]{2,1,0:T(8,128)(2,1)} %tok_in.1, s32[6,2,12]{2,1,0:T(2,128)} %bitcast.9, bf16[16,192]{1,0:T(8,128)(2,1)} %embed_in.1, bf16[6,12,384]{2,1,0:T(8,128)(2,1)} %cot_in.1, ...), custom_call_target="tpu_custom_call" | custom-call | tf_op jit(solution)/shard_map/window_and_sums/pallas_call | solution.py:583
  65.7 1.8 %scaled_outputs.1 = (bf16[6,12,384]{2,1,0:T(8,128)(2,1)}, f32[3,576]{1,0:T(4,128)}, f32[3,192]{1,0:T(4,128)}, f32[3,768]{1,0:T(4,128)}, f32[12,192]{1,0:T(8,128)...) custom-call(f32[8,16,128]{2,1,0:T(8,128)} %get-tuple-element.20.dense_ref, ...), custom_call_target="tpu_custom_call" | custom-call | tf_op jit(solution)/shard_map/scaled_outputs/pallas_call | solution.py:711
